TPU v7x, 32 devices: a whole 2x2x4 slice. The times are simulated.
32 devices in a mesh: wide: 8 (over z, core), narrow: 4 (over y, x).
Axes of the slice: x: 2, y: 2, z: 4, core: 2. Of those that a mesh axis runs over, the one named last changes fastest.
Arguments:
- image_tokens: bfloat16 [32, 1024, 1024], P(('wide', 'narrow')), may hold values from -6 to 6
- text_states: bfloat16 [8, 128, 1024], P('wide', 'narrow'), may hold values from -6 to 6
- text_segments: int32 [8, 128], P('wide'), may hold values from 0 to 3, never falling along the last dimension, each value on 1 to 64 neighbouring positions
- image_segment: int32 [8, 4], P('wide', 'narrow'), may hold values from 0 to 3, each once within a row
- out_grad: bfloat16 [32, 1024, 1024], P(('wide', 'narrow')), may hold values from -6 to 6
- norm1_gain: bfloat16 [1024], P(('wide', 'narrow')), may hold values from 0.5 to 1.5
- norm1_bias: bfloat16 [1024], P(('wide', 'narrow')), may hold values from -1.75 to 1.75
- self_query: bfloat16 [1024, 1024], P(('wide', 'narrow')), may hold values from -0.1875 to 0.1875
- self_key: bfloat16 [1024, 1024], P(('wide', 'narrow')), may hold values from -0.1875 to 0.1875
- self_value: bfloat16 [1024, 1024], P(('wide', 'narrow')), may hold values from -0.1875 to 0.1875
- self_output: bfloat16 [1024, 1024], P(('wide', 'narrow')), may hold values from -0.5 to 0.5
- norm2_gain: bfloat16 [1024], P(('wide', 'narrow')), may hold values from 0.5 to 1.5
- norm2_bias: bfloat16 [1024], P(('wide', 'narrow')), may hold values from -1.75 to 1.75
- cross_query: bfloat16 [1024, 1024], P(('wide', 'narrow')), may hold values from -0.1875 to 0.1875
- cross_key: bfloat16 [1024, 1024], P(('wide', 'narrow')), may hold values from -0.1875 to 0.1875
- cross_value: bfloat16 [1024, 1024], P(('wide', 'narrow')), may hold values from -0.1875 to 0.1875
- cross_output: bfloat16 [1024, 1024], P(('wide', 'narrow')), may hold values from -0.375 to 0.375
- norm3_gain: bfloat16 [1024], P(('wide', 'narrow')), may hold values from 0.5 to 1.5
- norm3_bias: bfloat16 [1024], P(('wide', 'narrow')), may hold values from -1.75 to 1.75
- mlp_in: bfloat16 [1024, 4096], P(('wide', 'narrow')), may hold values from -0.1875 to 0.1875
- mlp_in_bias: bfloat16 [4096], P(('wide', 'narrow')), may hold values from -1.75 to 1.75
- mlp_out: bfloat16 [4096, 1024], P(('wide', 'narrow')), may hold values from -0.09375 to 0.09375
- mlp_out_bias: bfloat16 [1024], P(('wide', 'narrow')), may hold values from -1.75 to 1.75
Outputs:
- block_out: bfloat16 [32, 1024, 1024], P(('wide', 'narrow'))
- image_grad: float32 [32, 1024, 1024], P(('wide', 'narrow'))
- text_grad: float32 [8, 128, 1024], P('wide', 'narrow')
- grad_norm1_gain: float32 [1024], P(('wide', 'narrow'))
- grad_norm1_bias: float32 [1024], P(('wide', 'narrow'))
- grad_self_query: float32 [1024, 1024], P(('wide', 'narrow'))
- grad_self_key: float32 [1024, 1024], P(('wide', 'narrow'))
- grad_self_value: float32 [1024, 1024], P(('wide', 'narrow'))
- grad_self_output: float32 [1024, 1024], P(('wide', 'narrow'))
- grad_norm2_gain: float32 [1024], P(('wide', 'narrow'))
- grad_norm2_bias: float32 [1024], P(('wide', 'narrow'))
- grad_cross_query: float32 [1024, 1024], P(('wide', 'narrow'))
- grad_cross_key: float32 [1024, 1024], P(('wide', 'narrow'))
- grad_cross_value: float32 [1024, 1024], P(('wide', 'narrow'))
- grad_cross_output: float32 [1024, 1024], P(('wide', 'narrow'))
- grad_norm3_gain: float32 [1024], P(('wide', 'narrow'))
- grad_norm3_bias: float32 [1024], P(('wide', 'narrow'))
- grad_mlp_in: float32 [1024, 4096], P(('wide', 'narrow'))
- grad_mlp_in_bias: float32 [4096], P(('wide', 'narrow'))
- grad_mlp_out: float32 [4096, 1024], P(('wide', 'narrow'))
- grad_mlp_out_bias: float32 [1024], P(('wide', 'narrow'))
Inputs may be any that keep to these rules, and one draw needn't show every extreme that they name: `text_segments`: within a text row slot caption numbers never fall; each of the 4 captions fills 1 to 64 slots, and one fills exactly 64. `image_segment`: the 4 images of a text row name its captions, each caption once.
All inputs are finite; a program needn't handle non-finite values.
Results may differ from a plain program's by a relative error of at most 0.015.
Values may be sent and summed in bfloat16 or wider, within the bound.
A program may use at most 320 MiB of HBM per device.

v0:
```python
import jax
import jax.numpy as jnp
from jax import lax
from jax.sharding import PartitionSpec as P

HEAD_DIM = 64


EPSILON = 1e-05
NEGATIVE = -1e30


def matmul(leading, trailing):
    return jnp.dot(leading, trailing, preferred_element_type=jnp.float32)


def matmul_nt(leading, trailing):
    return lax.dot_general(
        leading, trailing, (((1,), (1,)), ((), ())), preferred_element_type=jnp.float32
    )


def matmul_tn(leading, trailing):
    return lax.dot_general(
        leading, trailing, (((0,), (0,)), ((), ())), preferred_element_type=jnp.float32
    )


def layer_norm(values, norm_gain, norm_bias):
    center = jnp.mean(values, axis=-1, keepdims=True)
    offset = values - center
    spread = jnp.mean(offset * offset, axis=-1, keepdims=True)
    return offset * lax.rsqrt(spread + EPSILON) * norm_gain + norm_bias


def exact_gelu(values):
    return jax.nn.gelu(values, approximate=False)


def fetch_self(norm1_gain, norm1_bias, self_query, self_key, self_value, self_output):
    return (
        lax.all_gather(norm1_gain, ("wide", "narrow"), axis=0, tiled=True),
        lax.all_gather(norm1_bias, ("wide", "narrow"), axis=0, tiled=True),
        lax.all_gather(self_query, ("wide", "narrow"), axis=0, tiled=True),
        lax.all_gather(self_key, ("wide", "narrow"), axis=0, tiled=True),
        lax.all_gather(self_value, ("wide", "narrow"), axis=0, tiled=True),
        lax.all_gather(self_output, ("wide", "narrow"), axis=0, tiled=True),
    )


def fetch_cross(norm2_gain, norm2_bias, cross_query, cross_key, cross_value, cross_output):
    return (
        lax.all_gather(norm2_gain, ("wide", "narrow"), axis=0, tiled=True),
        lax.all_gather(norm2_bias, ("wide", "narrow"), axis=0, tiled=True),
        lax.all_gather(cross_query, ("wide", "narrow"), axis=0, tiled=True),
        lax.all_gather(cross_key, ("wide", "narrow"), axis=0, tiled=True),
        lax.all_gather(cross_value, ("wide", "narrow"), axis=0, tiled=True),
        lax.all_gather(cross_output, ("wide", "narrow"), axis=0, tiled=True),
    )


def fetch_mlp(norm3_gain, norm3_bias, mlp_in, mlp_in_bias, mlp_out, mlp_out_bias):
    return (
        lax.all_gather(norm3_gain, ("wide", "narrow"), axis=0, tiled=True),
        lax.all_gather(norm3_bias, ("wide", "narrow"), axis=0, tiled=True),
        lax.all_gather(mlp_in, ("wide", "narrow"), axis=0, tiled=True),
        lax.all_gather(mlp_in_bias, ("wide", "narrow"), axis=0, tiled=True),
        lax.all_gather(mlp_out, ("wide", "narrow"), axis=0, tiled=True),
        lax.all_gather(mlp_out_bias, ("wide", "narrow"), axis=0, tiled=True),
    )


def head_slices(source, column, pair_width):
    return lax.dynamic_slice_in_dim(source, column, pair_width, 1).reshape(
        source.shape[0], 2, HEAD_DIM
    )


def attend_forward(queries, key_rows, value_rows, allowed):
    row_count = queries.shape[0]
    pair_width = 2 * HEAD_DIM
    groups = queries.shape[1] // pair_width
    scaling = HEAD_DIM ** (-0.5)

    def per_group(group_index, running):
        result, log_sums = running
        column = group_index * pair_width
        query_pair = head_slices(queries, column, pair_width)
        key_pair = head_slices(key_rows, column, pair_width)
        value_pair = head_slices(value_rows, column, pair_width)
        scores = (
            jnp.einsum("qhe,khe->hqk", query_pair, key_pair, preferred_element_type=jnp.float32)
            * scaling
        )
        scores = jnp.where(allowed, scores, NEGATIVE)
        row_max = jnp.max(scores, axis=2, keepdims=True)
        exp_scores = jnp.exp(scores - row_max)
        row_total = jnp.sum(exp_scores, axis=2, keepdims=True)
        weights = (exp_scores / row_total).astype(jnp.bfloat16)
        mixture = jnp.einsum(
            "hqk,khe->qhe", weights, value_pair, preferred_element_type=jnp.float32
        )
        result = lax.dynamic_update_slice_in_dim(
            result, mixture.reshape(row_count, pair_width).astype(jnp.bfloat16), column, 1
        )
        log_sums = lax.dynamic_update_slice_in_dim(
            log_sums, (row_max + jnp.log(row_total))[:, :, 0], 2 * group_index, 0
        )
        return (result, log_sums)

    initial = (
        jnp.zeros((row_count, queries.shape[1]), jnp.bfloat16),
        jnp.zeros((2 * groups, row_count), jnp.float32),
    )
    return lax.fori_loop(0, groups, per_group, initial)


def attend_backward(queries, key_rows, value_rows, allowed, log_sums, grad_mix):
    row_count = queries.shape[0]
    pair_width = 2 * HEAD_DIM
    groups = queries.shape[1] // pair_width
    scaling = HEAD_DIM ** (-0.5)

    def per_group(group_index, running):
        grad_queries, grad_keys, grad_values = running
        column = group_index * pair_width
        query_pair = head_slices(queries, column, pair_width)
        key_pair = head_slices(key_rows, column, pair_width)
        value_pair = head_slices(value_rows, column, pair_width)
        grad_pair = head_slices(grad_mix, column, pair_width)
        pair_sums = lax.dynamic_slice_in_dim(log_sums, 2 * group_index, 2, 0)
        scores = (
            jnp.einsum("qhe,khe->hqk", query_pair, key_pair, preferred_element_type=jnp.float32)
            * scaling
        )
        scores = jnp.where(allowed, scores, NEGATIVE)
        softmax_out = jnp.exp(scores - pair_sums[:, :, None])
        grad_value_pair = jnp.einsum(
            "hqk,qhe->khe",
            softmax_out.astype(jnp.bfloat16),
            grad_pair,
            preferred_element_type=jnp.float32,
        )
        grad_probs = jnp.einsum(
            "qhe,khe->hqk", grad_pair, value_pair, preferred_element_type=jnp.float32
        )
        inner_sum = jnp.sum(softmax_out * grad_probs, axis=2, keepdims=True)
        grad_scores = (softmax_out * (grad_probs - inner_sum)).astype(jnp.bfloat16)
        grad_query_pair = (
            jnp.einsum("hqk,khe->qhe", grad_scores, key_pair, preferred_element_type=jnp.float32)
            * scaling
        )
        grad_key_pair = (
            jnp.einsum("hqk,qhe->khe", grad_scores, query_pair, preferred_element_type=jnp.float32)
            * scaling
        )
        grad_queries = lax.dynamic_update_slice_in_dim(
            grad_queries,
            grad_query_pair.reshape(row_count, pair_width).astype(jnp.bfloat16),
            column,
            1,
        )
        grad_keys = lax.dynamic_update_slice_in_dim(
            grad_keys,
            grad_key_pair.reshape(key_rows.shape[0], pair_width).astype(jnp.bfloat16),
            column,
            1,
        )
        grad_values = lax.dynamic_update_slice_in_dim(
            grad_values,
            grad_value_pair.reshape(key_rows.shape[0], pair_width).astype(jnp.bfloat16),
            column,
            1,
        )
        return (grad_queries, grad_keys, grad_values)

    initial = (
        jnp.zeros(queries.shape, jnp.bfloat16),
        jnp.zeros(key_rows.shape, jnp.bfloat16),
        jnp.zeros(value_rows.shape, jnp.bfloat16),
    )
    return lax.fori_loop(0, groups, per_group, initial)


def on_device(
    image_tokens,
    text_states,
    text_segments,
    image_segment,
    out_grad,
    norm1_gain,
    norm1_bias,
    self_query,
    self_key,
    self_value,
    self_output,
    norm2_gain,
    norm2_bias,
    cross_query,
    cross_key,
    cross_value,
    cross_output,
    norm3_gain,
    norm3_bias,
    mlp_in,
    mlp_in_bias,
    mlp_out,
    mlp_out_bias,
):
    tokens = image_tokens[0].astype(jnp.float32)
    row_count = tokens.shape[0]
    self_full = fetch_self(norm1_gain, norm1_bias, self_query, self_key, self_value, self_output)
    gain_one = self_full[0].astype(jnp.float32)
    bias_one = self_full[1].astype(jnp.float32)
    normed_one = layer_norm(tokens, gain_one, bias_one).astype(jnp.bfloat16)
    queries = matmul(normed_one, self_full[2]).astype(jnp.bfloat16)
    key_rows = matmul(normed_one, self_full[3]).astype(jnp.bfloat16)
    value_rows = matmul(normed_one, self_full[4]).astype(jnp.bfloat16)
    row_pos = lax.broadcasted_iota(jnp.int32, (row_count, row_count), 0)
    column_pos = lax.broadcasted_iota(jnp.int32, (row_count, row_count), 1)
    causal = (row_pos >= column_pos)[None]
    mixed_self, sums_self = attend_forward(queries, key_rows, value_rows, causal)
    after_self = tokens + matmul(mixed_self, self_full[5])
    cross_full = fetch_cross(
        norm2_gain, norm2_bias, cross_query, cross_key, cross_value, cross_output
    )
    gain_two = cross_full[0].astype(jnp.float32)
    bias_two = cross_full[1].astype(jnp.float32)
    normed_two = layer_norm(after_self, gain_two, bias_two).astype(jnp.bfloat16)
    cross_queries = matmul(normed_two, cross_full[2]).astype(jnp.bfloat16)
    own_text = text_states[0]
    text_full = lax.all_gather(own_text, "narrow", axis=0, tiled=True)
    cross_keys = matmul(text_full, cross_full[3]).astype(jnp.bfloat16)
    cross_values = matmul(text_full, cross_full[4]).astype(jnp.bfloat16)
    matches = (text_segments[0] == image_segment[0, 0])[None, None, :]
    mixed_cross, sums_cross = attend_forward(cross_queries, cross_keys, cross_values, matches)
    after_cross = after_self + matmul(mixed_cross, cross_full[5])
    mlp_full = fetch_mlp(norm3_gain, norm3_bias, mlp_in, mlp_in_bias, mlp_out, mlp_out_bias)
    gain_three = mlp_full[0].astype(jnp.float32)
    bias_three = mlp_full[1].astype(jnp.float32)
    normed_three = layer_norm(after_cross, gain_three, bias_three).astype(jnp.bfloat16)
    hidden_pre = matmul(normed_three, mlp_full[2]) + mlp_full[3].astype(jnp.float32)
    hidden_act, gelu_pull = jax.vjp(exact_gelu, hidden_pre)
    hidden = hidden_act.astype(jnp.bfloat16)
    block_out = after_cross + matmul(hidden, mlp_full[4]) + mlp_full[5].astype(jnp.float32)
    grad_out = out_grad[0]
    grad_tail = grad_out.astype(jnp.float32)
    mlp_full = fetch_mlp(norm3_gain, norm3_bias, mlp_in, mlp_in_bias, mlp_out, mlp_out_bias)
    grad_down = matmul_tn(hidden, grad_out)
    grad_down_bias = jnp.sum(grad_tail, axis=0)
    grad_hidden = matmul_nt(grad_out, mlp_full[4])
    grad_pre = gelu_pull(grad_hidden)[0].astype(jnp.bfloat16)
    grad_up = matmul_tn(normed_three, grad_pre)
    grad_up_bias = jnp.sum(grad_pre.astype(jnp.float32), axis=0)
    grad_normed = matmul_nt(grad_pre, mlp_full[2])
    unused_three, norm_pull = jax.vjp(layer_norm, after_cross, gain_three, bias_three)
    grad_middle, grad_gain_three, grad_bias_three = norm_pull(grad_normed)
    grad_after_cross = grad_tail + grad_middle
    mlp_terms = (grad_gain_three, grad_bias_three, grad_up, grad_up_bias, grad_down, grad_down_bias)
    mlp_grads = (
        lax.psum_scatter(mlp_terms[0], ("wide", "narrow"), scatter_dimension=0, tiled=True),
        lax.psum_scatter(mlp_terms[1], ("wide", "narrow"), scatter_dimension=0, tiled=True),
        lax.psum_scatter(mlp_terms[2], ("wide", "narrow"), scatter_dimension=0, tiled=True),
        lax.psum_scatter(mlp_terms[3], ("wide", "narrow"), scatter_dimension=0, tiled=True),
        lax.psum_scatter(mlp_terms[4], ("wide", "narrow"), scatter_dimension=0, tiled=True),
        lax.psum_scatter(mlp_terms[5], ("wide", "narrow"), scatter_dimension=0, tiled=True),
    )
    cross_full = fetch_cross(
        norm2_gain, norm2_bias, cross_query, cross_key, cross_value, cross_output
    )
    grad_mix_out = grad_after_cross.astype(jnp.bfloat16)
    grad_cross_out = matmul_tn(mixed_cross, grad_mix_out)
    grad_mixed = matmul_nt(grad_mix_out, cross_full[5]).astype(jnp.bfloat16)
    query_grad_two, key_grad_two, value_grad_two = attend_backward(
        cross_queries, cross_keys, cross_values, matches, sums_cross, grad_mixed
    )
    grad_cross_query = matmul_tn(normed_two, query_grad_two)
    grad_normed = matmul_nt(query_grad_two, cross_full[2])
    grad_cross_key = matmul_tn(text_full, key_grad_two)
    grad_cross_value = matmul_tn(text_full, value_grad_two)
    text_term = matmul_nt(key_grad_two, cross_full[3]) + matmul_nt(value_grad_two, cross_full[4])
    text_grad = lax.psum_scatter(text_term, "narrow", scatter_dimension=0, tiled=True)
    unused_two, norm_pull = jax.vjp(layer_norm, after_self, gain_two, bias_two)
    grad_middle, grad_gain_two, grad_bias_two = norm_pull(grad_normed)
    grad_after_self = grad_after_cross + grad_middle
    cross_terms = (
        grad_gain_two,
        grad_bias_two,
        grad_cross_query,
        grad_cross_key,
        grad_cross_value,
        grad_cross_out,
    )
    cross_grads = (
        lax.psum_scatter(cross_terms[0], ("wide", "narrow"), scatter_dimension=0, tiled=True),
        lax.psum_scatter(cross_terms[1], ("wide", "narrow"), scatter_dimension=0, tiled=True),
        lax.psum_scatter(cross_terms[2], ("wide", "narrow"), scatter_dimension=0, tiled=True),
        lax.psum_scatter(cross_terms[3], ("wide", "narrow"), scatter_dimension=0, tiled=True),
        lax.psum_scatter(cross_terms[4], ("wide", "narrow"), scatter_dimension=0, tiled=True),
        lax.psum_scatter(cross_terms[5], ("wide", "narrow"), scatter_dimension=0, tiled=True),
    )
    self_full = fetch_self(norm1_gain, norm1_bias, self_query, self_key, self_value, self_output)
    grad_self_mix = grad_after_self.astype(jnp.bfloat16)
    grad_self_out = matmul_tn(mixed_self, grad_self_mix)
    grad_mixed = matmul_nt(grad_self_mix, self_full[5]).astype(jnp.bfloat16)
    query_grad_one, key_grad_one, value_grad_one = attend_backward(
        queries, key_rows, value_rows, causal, sums_self, grad_mixed
    )
    grad_self_query = matmul_tn(normed_one, query_grad_one)
    grad_self_key = matmul_tn(normed_one, key_grad_one)
    grad_self_value = matmul_tn(normed_one, value_grad_one)
    grad_normed = (
        matmul_nt(query_grad_one, self_full[2])
        + matmul_nt(key_grad_one, self_full[3])
        + matmul_nt(value_grad_one, self_full[4])
    )
    unused_one, norm_pull = jax.vjp(layer_norm, tokens, gain_one, bias_one)
    grad_middle, grad_gain_one, grad_bias_one = norm_pull(grad_normed)
    image_grad = grad_after_self + grad_middle
    self_terms = (
        grad_gain_one,
        grad_bias_one,
        grad_self_query,
        grad_self_key,
        grad_self_value,
        grad_self_out,
    )
    self_grads = (
        lax.psum_scatter(self_terms[0], ("wide", "narrow"), scatter_dimension=0, tiled=True),
        lax.psum_scatter(self_terms[1], ("wide", "narrow"), scatter_dimension=0, tiled=True),
        lax.psum_scatter(self_terms[2], ("wide", "narrow"), scatter_dimension=0, tiled=True),
        lax.psum_scatter(self_terms[3], ("wide", "narrow"), scatter_dimension=0, tiled=True),
        lax.psum_scatter(self_terms[4], ("wide", "narrow"), scatter_dimension=0, tiled=True),
        lax.psum_scatter(self_terms[5], ("wide", "narrow"), scatter_dimension=0, tiled=True),
    )
    return (
        block_out.astype(jnp.bfloat16)[None],
        image_grad[None],
        text_grad[None],
        self_grads[0],
        self_grads[1],
        self_grads[2],
        self_grads[3],
        self_grads[4],
        self_grads[5],
        cross_grads[0],
        cross_grads[1],
        cross_grads[2],
        cross_grads[3],
        cross_grads[4],
        cross_grads[5],
        mlp_grads[0],
        mlp_grads[1],
        mlp_grads[2],
        mlp_grads[3],
        mlp_grads[4],
        mlp_grads[5],
    )


def solution(mesh):
    placed = (
        P(("wide", "narrow"), None, None),
        P("wide", "narrow", None),
        P("wide", None),
        P("wide", "narrow"),
        P(("wide", "narrow"), None, None),
        P(("wide", "narrow")),
        P(("wide", "narrow")),
        P(("wide", "narrow"), None),
        P(("wide", "narrow"), None),
        P(("wide", "narrow"), None),
        P(("wide", "narrow"), None),
        P(("wide", "narrow")),
        P(("wide", "narrow")),
        P(("wide", "narrow"), None),
        P(("wide", "narrow"), None),
        P(("wide", "narrow"), None),
        P(("wide", "narrow"), None),
        P(("wide", "narrow")),
        P(("wide", "narrow")),
        P(("wide", "narrow"), None),
        P(("wide", "narrow")),
        P(("wide", "narrow"), None),
        P(("wide", "narrow")),
    )
    return jax.shard_map(
        on_device,
        mesh=mesh,
        in_specs=placed,
        out_specs=(
            P(("wide", "narrow"), None, None),
            P(("wide", "narrow"), None, None),
            P("wide", "narrow", None),
            P(("wide", "narrow")),
            P(("wide", "narrow")),
            P(("wide", "narrow"), None),
            P(("wide", "narrow"), None),
            P(("wide", "narrow"), None),
            P(("wide", "narrow"), None),
            P(("wide", "narrow")),
            P(("wide", "narrow")),
            P(("wide", "narrow"), None),
            P(("wide", "narrow"), None),
            P(("wide", "narrow"), None),
            P(("wide", "narrow"), None),
            P(("wide", "narrow")),
            P(("wide", "narrow")),
            P(("wide", "narrow"), None),
            P(("wide", "narrow")),
            P(("wide", "narrow"), None),
            P(("wide", "narrow")),
        ),
        check_vma=False,
    )
```

profile of v0, /device:TPU:0, one launch (start us, length us, event | category | flops | bytes accessed | tf_op | source)
XLA Modules:
  0.0 2730.4 jit_solution(10465723237157293187)
XLA Ops:
  19.9 42.4 %all-reduce.16 = (bf16[1024]{0:T(1024)(128)(2,1)S(1)}, bf16[1024]{0:T(1024)(128)(2,1)S(1)}, bf16[1024]{0:T(1024)(128)(2,1)S(1)}, bf16[1024]{0:T(1024)(128)(2,1)S...) all-reduce(bf16[1024]{0:T(1024)(128)(2,1)S(1)} %dynamic-update-slic, ...), channel_id=1, replica_groups=mesh['wide'=8,'narrow'=4] {'wide','narrow'}, use_global_device_ids=true, to_apply=%add.1 | all-reduce | flops 7168 | bytes 28672
  66.9 10.6 all-gather
  78.1 64.1 %all-gather.1 = bf16[32,1,128]{2,1,0:T(2,128)(2,1)S(1)} all-gather(bf16[1,1,128]{2,1,0:T(2,128)(2,1)S(1)} %bitcast.326), channel_id=1, replica_groups=mesh['wide'=8,'narrow'=4] {'wide','narrow'}, dimensions={0}, use_global_device_ids=true | all-gather | bytes 8448 | tf_op jit(solution)/shard_map/all_gather | solution.py:67
  146.3 5.6 convolution_convert_fusion.5
  155.9 5.6 convolution_convert_fusion.6
  165.4 21.6 all-gather.13.cloned.1.call-done
  187.0 5.6 convolution_convert_fusion.7
  198.1 123.0 %while.68 = (s32[]{:T(128)}, bf16[1024,1024]{0,1:T(8,128)(2,1)}, f32[16,1024]{1,0:T(8,128)S(1)}, bf16[1024,1024]{0,1:T(8,128)(2,1)}, bf16[1024,1024]{0,1:T(8,128...) while((s32[]{:T(128)}, bf16[1024,1024]{0,1:T(8,128)(2,1)}, ...), condition=%wide.region_5.6_spmd.clone, body=%wide.region_2.5_spmd.clone.sunk | while | flops 563214336 | bytes 66126076 | solution.py:115
  207.9 5.0 fusion.228
  223.2 5.0 fusion.228
  238.6 5.1 fusion.228
  253.9 5.1 fusion.228
  269.3 5.0 fusion.228
  284.6 5.0 fusion.228
  300.0 5.1 fusion.228
  328.6 6.9 convolution_convert_fusion.4
  338.5 22.6 all-gather.21.cloned.1.call-done
  363.3 55.9 %all-gather.25.cloned.1.call-done = bf16[1024,1024]{1,0:T(8,128)(2,1)} async-done(((bf16[32,1024]{1,0:T(8,128)(2,1)}), bf16[1024,1024]{1,0:T(8,128)(2,1)}) %all-gather.25.cloned.1.call-update) | async-done | bytes 2097168 | tf_op jit(solution)/shard_map/all_gather | solution.py:56
  423.0 13.7 while.66
  436.8 40.6 %all-gather.27.cloned.1.call-done = bf16[1024,1024]{1,0:T(8,128)(2,1)} async-done(((bf16[32,1024]{1,0:T(8,128)(2,1)}), bf16[1024,1024]{1,0:T(8,128)(2,1)}) %all-gather.27.cloned.1.call-update) | async-done | bytes 2097168 | tf_op jit(solution)/shard_map/all_gather | solution.py:58
  477.4 5.9 fusion.87
  485.9 70.7 %all-gather.29.cloned.1.call-done = bf16[1024,4096]{1,0:T(8,128)(2,1)} async-done(((bf16[32,4096]{1,0:T(8,128)(2,1)}), bf16[1024,4096]{1,0:T(8,128)(2,1)}) %all-gather.29.cloned.1.call-update) | async-done | bytes 8388624 | tf_op jit(solution)/shard_map/all_gather | solution.py:66
  556.7 47.8 %multiply_convert_fusion.2 = (bf16[1024,4096]{1,0:T(8,128)(2,1)}, f32[1024,4096]{1,0:T(8,128)}, f32[1024,4096]{1,0:T(8,128)}) fusion(f32[4096]{0:T(1024)S(1)} %bitcast.324, bf16[1024,4096]{1,0:T(8,128)(2,1)} %all-gather.29.cloned.1.call-done, bf16[1024,1024]{0,1:T(8,128)(2,1)S(1)} %add_convert_fusion.5.clone.4), kind=kOutput, calls=%fused_computation.76 | convolution fusion | flops 8866758656 | bytes 52445184 | tf_op jit(solution)/shard_map/dot_general | solution.py:14
  604.5 31.1 %all-gather.31.cloned.1.call-done = bf16[4096,1024]{1,0:T(8,128)(2,1)} async-done(((bf16[128,1024]{1,0:T(8,128)(2,1)}), bf16[4096,1024]{1,0:T(8,128)(2,1)}) %all-gather.31.cloned.1.call-update) | async-done | bytes 8388624 | tf_op jit(solution)/shard_map/all_gather | solution.py:68
  635.6 24.9 convert_reduce_fusion
  660.5 15.7 fusion.89
  676.2 5.5 copy.97
  681.8 5.4 multiply_reduce_fusion.2
  697.4 56.7 %while.67 = (s32[]{:T(128)}, bf16[1024,1024]{0,1:T(8,128)(2,1)}, bf16[128,1024]{0,1:T(8,128)(2,1)S(1)}, bf16[128,1024]{0,1:T(8,128)(2,1)S(1)}, bf16[128,1024]{0,...) while((s32[]{:T(128)}, bf16[1024,1024]{0,1:T(8,128)(2,1)}, ...), condition=%wide.region_18.19_spmd, body=%wide.region_16.18_spmd.sunk | while | flops 170440704 | bytes 11739533 | solution.py:182
  754.1 7.4 fusion.72
  761.6 6.6 fusion.88
  768.2 5.5 copy.102
  785.0 7.6 convert_reduce_fusion.1
  794.2 6.0 convolution_convert_fusion.2
  805.0 196.7 %while.69 = (s32[]{:T(128)}, bf16[1024,1024]{0,1:T(8,128)(2,1)}, bf16[1024,1024]{0,1:T(8,128)(2,1)}, bf16[1024,1024]{0,1:T(8,128)(2,1)}, bf16[1024,1024]{0,1:T(8...) while((s32[]{:T(128)}, bf16[1024,1024]{0,1:T(8,128)(2,1)}, ...), condition=%wide.region_23.24_spmd.clone, body=%wide.region_21.23_spmd.clone.sunk | while | flops 1375336448 | bytes 99148080 | solution.py:182
  815.4 5.5 multiply_reduce_fusion.11
  840.0 5.4 multiply_reduce_fusion.11
  864.6 5.4 multiply_reduce_fusion.11
  889.1 5.4 multiply_reduce_fusion.11
  913.6 5.4 multiply_reduce_fusion.11
  938.1 5.4 multiply_reduce_fusion.11
  962.5 5.4 multiply_reduce_fusion.11
  987.0 5.4 multiply_reduce_fusion.11
  1001.7 6.0 fusion.77
  1007.9 6.0 fusion.75
  1014.0 6.1 fusion.73
  1020.1 7.2 fusion.58
  1027.4 6.6 fusion.93
  1037.7 5.5 copy.128
  1046.9 5.5 copy.130
  1053.0 16.8 fusion.70
  1070.1 16.3 fusion.52
  1103.4 41.2 %all-reduce.15 = (f32[1024]{0:T(1024)S(1)}, f32[1024]{0:T(1024)S(1)}, f32[1024]{0:T(1024)S(1)}, f32[1024]{0:T(1024)S(1)}, f32[1024]{0:T(1024)S(1)}, /*index=5*/f...) all-reduce(f32[1024]{0:T(1024)S(1)} %get-tuple-element.767, ...), channel_id=4, replica_groups=mesh['wide'=8,'narrow'=4] {'wide','narrow'}, use_global_device_ids=true, to_apply=%region_28.29.clone | all-reduce | flops 11264 | bytes 90112
  1148.7 6.8 add_bitcast_fusion
  1155.4 5.3 copy.113
  1160.8 14.5 fusion.51
  1178.4 111.8 %reduce-scatter.20.cloned.1.call-done = f32[32,1024]{1,0:T(8,128)} async-done(((f32[1024,1024]{1,0:T(8,128)}), f32[32,1024]{1,0:T(8,128)}) %reduce-scatter.20.cloned.1.call-update) | async-done | bytes 131088 | tf_op jit(solution)/shard_map/reduce_scatter | solution.py:332
  1290.2 142.6 %reduce-scatter.22.cloned.1.call-done = f32[32,1024]{1,0:T(8,128)} async-done(((f32[1024,1024]{1,0:T(8,128)}), f32[32,1024]{1,0:T(8,128)}) %reduce-scatter.22.cloned.1.call-update) | async-done | bytes 131088 | tf_op jit(solution)/shard_map/reduce_scatter | solution.py:333
  1432.8 142.0 %reduce-scatter.24.cloned.1.call-done = f32[32,1024]{1,0:T(8,128)} async-done(((f32[1024,1024]{1,0:T(8,128)}), f32[32,1024]{1,0:T(8,128)}) %reduce-scatter.24.cloned.1.call-update) | async-done | bytes 131088 | tf_op jit(solution)/shard_map/reduce_scatter | solution.py:334
  1574.8 142.1 %reduce-scatter.28.cloned.1.call-done = f32[32,1024]{1,0:T(8,128)} async-done(((f32[1024,1024]{1,0:T(8,128)}), f32[32,1024]{1,0:T(8,128)}) %reduce-scatter.28.cloned.1.call-update) | async-done | bytes 131088 | tf_op jit(solution)/shard_map/reduce_scatter | solution.py:300
  1716.9 142.2 %reduce-scatter.34.cloned.1.call-done = f32[32,1024]{1,0:T(8,128)} async-done(((f32[1024,1024]{1,0:T(8,128)}), f32[32,1024]{1,0:T(8,128)}) %reduce-scatter.34.cloned.1.call-update) | async-done | bytes 131088
  1859.1 143.1 %reduce-scatter.36.cloned.1.call-done = f32[32,1024]{1,0:T(8,128)} async-done(((f32[1024,1024]{1,0:T(8,128)}), f32[32,1024]{1,0:T(8,128)}) %reduce-scatter.36.cloned.1.call-update) | async-done | bytes 131088
  2002.2 358.9 %reduce-scatter.30.cloned.1.call-done = f32[32,4096]{1,0:T(8,128)} async-done(((f32[1024,4096]{1,0:T(8,128)}), f32[32,4096]{1,0:T(8,128)}) %reduce-scatter.30.cloned.1.call-update) | async-done | bytes 524304 | tf_op jit(solution)/shard_map/reduce_scatter | solution.py:263
  2361.1 362.0 %reduce-scatter.32.cloned.1.call-done = f32[128,1024]{1,0:T(8,128)} async-done(((f32[4096,1024]{1,0:T(8,128)}), f32[128,1024]{1,0:T(8,128)}) %reduce-scatter.32.cloned.1.call-update) | async-done | bytes 524304 | tf_op jit(solution)/shard_map/reduce_scatter | solution.py:265
  (679 shorter events, 422.7 us)
Async XLA Ops:
  7.2 139.1 %all-gather.17.cloned.1.call-start = ((), (), s32[]{:S(2)}) async-start(), calls=%async_computation.13 | async-start | bytes 2162688 | tf_op jit(solution)/shard_map/all_gather | solution.py:45
  7.9 147.9 %all-gather.15.cloned.1.call-start = ((), (), s32[]{:S(2)}) async-start(), calls=%async_computation.12 | async-start | bytes 2162688 | tf_op jit(solution)/shard_map/all_gather | solution.py:44
  8.7 178.3 %all-gather.13.cloned.1.call-start = ((), (), s32[]{:S(2)}) async-start(), calls=%async_computation.11 | async-start | bytes 2162688 | tf_op jit(solution)/shard_map/all_gather | solution.py:46
  9.4 311.7 %all-gather.19.cloned.1.call-start = ((), (), s32[]{:S(2)}) async-start(), calls=%async_computation.14 | async-start | bytes 2162688 | tf_op jit(solution)/shard_map/all_gather | solution.py:47
  10.0 318.6 %all-gather.23.cloned.1.call-start = ((), (), s32[]{:S(2)}) async-start(), calls=%async_computation.16 | async-start | bytes 2162688 | tf_op jit(solution)/shard_map/all_gather | solution.py:55
  10.6 350.5 %all-gather.21.cloned.1.call-start = ((), (), s32[]{:S(2)}) async-start(), calls=%async_computation.15 | async-start | bytes 2162688 | tf_op jit(solution)/shard_map/all_gather | solution.py:57
  11.1 408.1 %all-gather.25.cloned.1.call-start = ((), (), s32[]{:S(2)}) async-start(), calls=%async_computation.17 | async-start | bytes 2162688 | tf_op jit(solution)/shard_map/all_gather | solution.py:56
  11.9 465.5 %all-gather.27.cloned.1.call-start = ((), (), s32[]{:S(2)}) async-start(), calls=%async_computation.18 | async-start | bytes 2162688 | tf_op jit(solution)/shard_map/all_gather | solution.py:58
  12.6 544.0 %all-gather.29.cloned.1.call-start = ((), (), s32[]{:S(2)}) async-start(), calls=%async_computation.19 | async-start | bytes 8650752 | tf_op jit(solution)/shard_map/all_gather | solution.py:66
  13.4 622.2 %all-gather.31.cloned.1.call-start = ((), (), s32[]{:S(2)}) async-start(), calls=%async_computation.20 | async-start | bytes 8650752 | tf_op jit(solution)/shard_map/all_gather | solution.py:68
  14.0 1164.4 %reduce-scatter.16.cloned.1.call-start = ((), (), s32[]{:S(2)}) async-start(), calls=%async_computation.21 | async-start | bytes 655360 | tf_op jit(solution)/shard_map/reduce_scatter | solution.py:282
  62.3 124.7 %copy-start.46 = (f32[1024]{0:T(1024)}, f32[1024]{0:T(1024)S(1)}, u32[]{:S(2)}) copy-start(f32[1024]{0:T(1024)S(1)} %convert_element_type.232) | copy-start | bytes 12292
  62.3 124.6 %copy-start.64 = (f32[1024]{0:T(1024)}, f32[1024]{0:T(1024)S(1)}, u32[]{:S(2)}) copy-start(f32[1024]{0:T(1024)S(1)} %convert_element_type.233) | copy-start | bytes 12292
  62.3 15.8 copy-start.71
  65.2 255.9 %copy-start.6 = (bf16[1,1024,1024]{1,2,0:T(8,128)(2,1)}, bf16[1,1024,1024]{1,2,0:T(8,128)(2,1)S(1)}, u32[]{:S(2)}) copy-start(bf16[1,1024,1024]{1,2,0:T(8,128)(2,1)S(1)} %copy.88) | copy-start | bytes 6291460
  65.2 81.0 %copy-start.77 = (s32[1,128]{1,0:T(1,128)S(1)}, s32[1,128]{1,0:T(1,128)}, u32[]{:S(2)}) copy-start(s32[1,128]{1,0:T(1,128)} %param.33) | copy-start | bytes 1540
  65.6 121.3 %copy-start.33 = (f32[1024]{0:T(1024)}, f32[1024]{0:T(1024)S(1)}, u32[]{:S(2)}) copy-start(f32[1024]{0:T(1024)S(1)} %broadcast_multiply_fusion.2) | copy-start | bytes 12292
  66.3 120.7 %copy-start.48 = (f32[1024]{0:T(1024)}, f32[1024]{0:T(1024)S(1)}, u32[]{:S(2)}) copy-start(f32[1024]{0:T(1024)S(1)} %fusion.66) | copy-start | bytes 12292
  66.3 262.3 %copy-start.42 = (f32[1024]{0:T(1024)}, f32[1024]{0:T(1024)S(1)}, u32[]{:S(2)}) copy-start(f32[1024]{0:T(1024)S(1)} %convert_element_type.239) | copy-start | bytes 12292
  66.9 261.8 %copy-start.66 = (f32[1024]{0:T(1024)}, f32[1024]{0:T(1024)S(1)}, u32[]{:S(2)}) copy-start(f32[1024]{0:T(1024)S(1)} %convert_element_type.240) | copy-start | bytes 12292
  77.4 341.8 %copy-start.16 = (bf16[1,128,1024]{2,1,0:T(8,128)(2,1)}, bf16[1,128,1024]{2,1,0:T(8,128)(2,1)S(1)}, u32[]{:S(2)}) copy-start(bf16[1,128,1024]{2,1,0:T(8,128)(2,1)S(1)} %all-gather) | copy-start | bytes 786436
  78.1 405.7 %copy-start.35 = (f32[1024]{0:T(1024)}, f32[1024]{0:T(1024)S(1)}, u32[]{:S(2)}) copy-start(f32[1024]{0:T(1024)S(1)} %convert_element_type.244) | copy-start | bytes 12292
  78.1 405.7 %copy-start.59 = (f32[1024]{0:T(1024)}, f32[1024]{0:T(1024)S(1)}, u32[]{:S(2)}) copy-start(f32[1024]{0:T(1024)S(1)} %convert_element_type.245) | copy-start | bytes 12292
  328.6 7.0 copy-start.52
  328.6 7.0 copy-start.56
  436.7 46.5 %copy-start.13 = (bf16[1024,1024]{0,1:T(8,128)(2,1)}, bf16[1024,1024]{0,1:T(8,128)(2,1)S(1)}, u32[]{:S(2)}) copy-start(bf16[1024,1024]{0,1:T(8,128)(2,1)S(1)} %get-tuple-element.1310) | copy-start | bytes 6291460
  436.7 46.5 %copy-start.24 = (bf16[128,1024]{0,1:T(8,128)(2,1)}, bf16[128,1024]{0,1:T(8,128)(2,1)S(1)}, u32[]{:S(2)}) copy-start(bf16[128,1024]{0,1:T(8,128)(2,1)S(1)} %get-tuple-element.1329) | copy-start | bytes 786436
  436.7 46.5 %copy-start.25 = (bf16[128,1024]{0,1:T(8,128)(2,1)}, bf16[128,1024]{0,1:T(8,128)(2,1)S(1)}, u32[]{:S(2)}) copy-start(bf16[128,1024]{0,1:T(8,128)(2,1)S(1)} %get-tuple-element.1330) | copy-start | bytes 786436
  436.8 46.5 %copy-start.26 = (f32[16,1024]{1,0:T(8,128)}, f32[16,1024]{1,0:T(8,128)S(1)}, u32[]{:S(2)}) copy-start(f32[16,1024]{1,0:T(8,128)S(1)} %get-tuple-element.1194) | copy-start | bytes 196612
  436.8 46.5 %copy-start.44 = (pred[1,1,128]{2,1,0:T(4,128)(4,1)}, pred[1,1,128]{2,1,0:T(4,128)(4,1)S(1)}, u32[]{:S(2)}) copy-start(pred[1,1,128]{2,1,0:T(4,128)(4,1)S(1)} %get-tuple-element.1351) | copy-start | bytes 388
  483.8 120.7 %copy-start.54 = (f32[1024]{0:T(1024)}, f32[1024]{0:T(1024)S(1)}, u32[]{:S(2)}) copy-start(f32[1024]{0:T(1024)S(1)} %multiply_reduce_fusion.6) | copy-start | bytes 12292
  485.3 119.2 %copy-start.38 = (f32[1024]{0:T(1024)}, f32[1024]{0:T(1024)S(1)}, u32[]{:S(2)}) copy-start(f32[1024]{0:T(1024)S(1)} %fusion.68) | copy-start | bytes 12292
  681.8 5.9 copy-start.8
  697.4 56.7 %copy-start.32 = (f32[1024]{0:T(1024)S(1)}, f32[1024]{0:T(1024)}, u32[]{:S(2)}) copy-start(f32[1024]{0:T(1024)} %copy-done.31) | copy-start | bytes 12292
  697.4 56.7 %copy-start.43 = (f32[1024]{0:T(1024)S(1)}, f32[1024]{0:T(1024)}, u32[]{:S(2)}) copy-start(f32[1024]{0:T(1024)} %copy-done.42) | copy-start | bytes 12292
  697.4 56.7 %copy-start.57 = (f32[1024]{0:T(1024)S(1)}, f32[1024]{0:T(1024)}, u32[]{:S(2)}) copy-start(f32[1024]{0:T(1024)} %copy-done.56) | copy-start | bytes 12292
  697.4 56.7 %copy-start.67 = (f32[1024]{0:T(1024)S(1)}, f32[1024]{0:T(1024)}, u32[]{:S(2)}) copy-start(f32[1024]{0:T(1024)} %copy-done.66) | copy-start | bytes 12292
  754.1 28.3 %copy-start.18 = (bf16[128,1024]{0,1:T(8,128)(2,1)}, bf16[128,1024]{0,1:T(8,128)(2,1)S(1)}, u32[]{:S(2)}) copy-start(bf16[128,1024]{0,1:T(8,128)(2,1)S(1)} %get-tuple-element.621) | copy-start | bytes 786436
  754.1 29.1 %copy-start.20 = (bf16[128,1024]{0,1:T(8,128)(2,1)}, bf16[128,1024]{0,1:T(8,128)(2,1)S(1)}, u32[]{:S(2)}) copy-start(bf16[128,1024]{0,1:T(8,128)(2,1)S(1)} %get-tuple-element.622) | copy-start | bytes 786436
  754.1 7.5 copy-start.75
  773.7 5.9 copy-start.5
  784.9 393.5 %reduce-scatter.26.cloned.1.call-start = ((), (), s32[]{:S(2)}) async-start(), calls=%async_computation.26 | async-start | bytes 4325376 | tf_op jit(solution)/shard_map/reduce_scatter | solution.py:297
  792.6 385.8 %reduce-scatter.18.cloned.1.call-start = ((), (), s32[]{:S(2)}) async-start(), calls=%async_computation.22 | async-start | bytes 4325376 | tf_op jit(solution)/shard_map/reduce_scatter | solution.py:331
  805.0 196.7 %copy-start.7 = (bf16[1,1024,1024]{1,2,0:T(8,128)(2,1)S(1)}, bf16[1,1024,1024]{1,2,0:T(8,128)(2,1)}, u32[]{:S(2)}) copy-start(bf16[1,1024,1024]{1,2,0:T(8,128)(2,1)} %copy-done.6) | copy-start | bytes 6291460
  805.0 196.7 %copy-start.34 = (f32[1024]{0:T(1024)S(1)}, f32[1024]{0:T(1024)}, u32[]{:S(2)}) copy-start(f32[1024]{0:T(1024)} %copy-done.33) | copy-start | bytes 12292
  805.0 196.7 %copy-start.47 = (f32[1024]{0:T(1024)S(1)}, f32[1024]{0:T(1024)}, u32[]{:S(2)}) copy-start(f32[1024]{0:T(1024)} %copy-done.46) | copy-start | bytes 12292
  805.0 196.7 %copy-start.49 = (f32[1024]{0:T(1024)S(1)}, f32[1024]{0:T(1024)}, u32[]{:S(2)}) copy-start(f32[1024]{0:T(1024)} %copy-done.48) | copy-start | bytes 12292
  805.0 196.7 %copy-start.65 = (f32[1024]{0:T(1024)S(1)}, f32[1024]{0:T(1024)}, u32[]{:S(2)}) copy-start(f32[1024]{0:T(1024)} %copy-done.64) | copy-start | bytes 12292
  815.1 5.8 slice-start
  815.4 5.8 slice-start.1
  839.7 5.8 slice-start
  840.0 5.8 slice-start.1
  864.5 5.8 slice-start.1
  888.8 5.7 slice-start
  889.1 5.7 slice-start.1
  937.8 5.8 slice-start
  1007.7 282.5 %reduce-scatter.20.cloned.1.call-start = ((), (), s32[]{:S(2)}) async-start(), calls=%async_computation.23 | async-start | bytes 4325376 | tf_op jit(solution)/shard_map/reduce_scatter | solution.py:332
  1013.9 418.9 %reduce-scatter.22.cloned.1.call-start = ((), (), s32[]{:S(2)}) async-start(), calls=%async_computation.24 | async-start | bytes 4325376 | tf_op jit(solution)/shard_map/reduce_scatter | solution.py:333
  1020.1 554.7 %reduce-scatter.24.cloned.1.call-start = ((), (), s32[]{:S(2)}) async-start(), calls=%async_computation.25 | async-start | bytes 4325376 | tf_op jit(solution)/shard_map/reduce_scatter | solution.py:334
  1027.3 689.6 %reduce-scatter.28.cloned.1.call-start = ((), (), s32[]{:S(2)}) async-start(), calls=%async_computation.27 | async-start | bytes 4325376 | tf_op jit(solution)/shard_map/reduce_scatter | solution.py:300
  1034.1 825.1 %reduce-scatter.34.cloned.1.call-start = ((), (), s32[]{:S(2)}) async-start(), calls=%async_computation.30 | async-start | bytes 4325376
  1043.2 959.0 %reduce-scatter.36.cloned.1.call-start = ((), (), s32[]{:S(2)}) async-start(), calls=%async_computation.31 | async-start | bytes 4325376
  1052.3 1308.7 %reduce-scatter.30.cloned.1.call-start = ((), (), s32[]{:S(2)}) async-start(), calls=%async_computation.28 | async-start | bytes 17301504 | tf_op jit(solution)/shard_map/reduce_scatter | solution.py:263
  1069.8 1653.3 %reduce-scatter.32.cloned.1.call-start = ((), (), s32[]{:S(2)}) async-start(), calls=%async_computation.29 | async-start | bytes 17301504 | tf_op jit(solution)/shard_map/reduce_scatter | solution.py:265
  (58 other events, 203.5 us)
Sparse Core Ops, SparseCore 0:
  10.9 59.6 all-gather.16
  73.5 55.2 all-gather.14
  131.7 55.2 all-gather.12
  189.7 55.2 all-gather.18
  247.7 55.2 all-gather.22
  305.7 55.2 all-gather.20
  363.9 55.2 all-gather.24
  422.1 55.2 all-gather.26
  480.2 76.3 all-gather.28
  559.4 76.1 all-gather.30
  785.0 23.3 reduce-scatter.15
  811.3 141.7 reduce-scatter.25
  1007.8 140.6 reduce-scatter.17
  1151.3 138.7 reduce-scatter.19
  1293.0 139.8 reduce-scatter.21
  1435.6 139.1 reduce-scatter.23
  1577.6 139.2 reduce-scatter.27
  1719.7 139.3 reduce-scatter.33
  1862.1 140.0 reduce-scatter.35
  2005.0 356.0 reduce-scatter.29
  2364.1 359.0 reduce-scatter.31
where the time goes:
time: 2740 us; the launch traced here: 2730 us
  waiting for transfers between devices  1790 us (65%)
  matrix products  443 us (16%)
  local copies, waits for them, and re-layouts  236 us (9%)
  blocking collectives  158 us (6%)
  other arithmetic  79 us (3%)
    reduce_scatter x1, waiting for transfers between devices, on_device(): lax.psum_scatter(mlp_terms[4], ('wide', 'narrow'), scatter_dimension=0, t...  362 us
    reduce_scatter x1, waiting for transfers between devices, on_device(): lax.psum_scatter(mlp_terms[2], ('wide', 'narrow'), scatter_dimension=0, t...  359 us
    unnamed x23, waiting for transfers between devices  292 us
    reduce_scatter x1, waiting for transfers between devices, on_device(): lax.psum_scatter(self_terms[4], ('wide', 'narrow'), scatter_dimension=0,...  143 us
    reduce_scatter x1, waiting for transfers between devices, on_device(): lax.psum_scatter(cross_terms[5], ('wide', 'narrow'), scatter_dimension=0,...  142 us
    reduce_scatter x1, waiting for transfers between devices, on_device(): lax.psum_scatter(self_terms[5], ('wide', 'narrow'), scatter_dimension=0,...  142 us
    reduce_scatter x1, waiting for transfers between devices, on_device(): lax.psum_scatter(self_terms[3], ('wide', 'narrow'), scatter_dimension=0,...  112 us
    dot_general x10, matrix products, matmul(): return jnp.dot(leading, trailing, preferred_element_type=jnp.float32)  101 us
  transfers between devices with their start and end apart: 21, of which 14 were waited for; matrix products, arithmetic and copies ran while one was open for 21% of the time, Pallas kernels for 0%

commit v1 on v0

v1 whole, which is shorter than its diff:
```python
import jax
import jax.numpy as jnp
from jax import lax
from jax.sharding import PartitionSpec as P

HEAD_DIM = 64


EPSILON = 1e-05
NEGATIVE = -1e30


def matmul(leading, trailing):
    return jnp.dot(leading, trailing, preferred_element_type=jnp.float32)


def matmul_nt(leading, trailing):
    return lax.dot_general(
        leading, trailing, (((1,), (1,)), ((), ())), preferred_element_type=jnp.float32
    )


def matmul_tn(leading, trailing):
    return lax.dot_general(
        leading, trailing, (((0,), (0,)), ((), ())), preferred_element_type=jnp.float32
    )


def layer_norm(values, norm_gain, norm_bias):
    center = jnp.mean(values, axis=-1, keepdims=True)
    offset = values - center
    spread = jnp.mean(offset * offset, axis=-1, keepdims=True)
    return offset * lax.rsqrt(spread + EPSILON) * norm_gain + norm_bias


def exact_gelu(values):
    return jax.nn.gelu(values, approximate=False)


AXES = ("wide", "narrow")


def axis_bits(axis):
    return lax.axis_size(axis).bit_length() - 1


def halving_order(kind):
    wide = [("wide", k) for k in range(1, axis_bits("wide"))]
    narrow = [("narrow", k) for k in range(axis_bits("narrow"))]
    core = [("wide", 0)]
    if kind == 0:
        return core + narrow + wide
    if kind == 1:
        return core + narrow[1:] + wide[:1] + narrow[:1] + wide[1:]
    return core + wide[:1] + narrow + wide[1:]


def swap_with(block, axis, bit):
    count = lax.axis_size(axis)
    return lax.ppermute(block, axis, [(i, i ^ (1 << bit)) for i in range(count)])


def scatter_sum(term, kind, sent=jnp.bfloat16):
    left = [("wide", k) for k in reversed(range(axis_bits("wide")))]
    left += [("narrow", k) for k in reversed(range(axis_bits("narrow")))]
    owners = 1 << len(left)
    tail = (term.shape[0] // owners,) + term.shape[1:]
    state = term
    for axis, bit in halving_order(kind):
        at = left.index((axis, bit))
        left.pop(at)
        state = state.reshape((1 << at, 2, 1 << (len(left) - at)) + tail)
        mine = (lax.axis_index(axis) >> bit) & 1
        away = lax.dynamic_index_in_dim(state, 1 - mine, 1, keepdims=False).astype(sent)
        kept = lax.dynamic_index_in_dim(state, mine, 1, keepdims=False)
        arrived = swap_with(away, axis, bit)
        state = kept.astype(jnp.float32) + arrived.astype(jnp.float32)
        if left:
            state = state.astype(sent)
    return state.reshape(tail)


def gather_rows(packed):
    whole = lax.all_gather(packed, AXES, axis=0, tiled=True)
    return whole.reshape((-1,) + packed.shape)


def pack_vectors(vectors):
    flat = jnp.concatenate(vectors)
    room = -flat.shape[0] % 1024
    return jnp.pad(flat, (0, room)).reshape(-1, 1024)


def take_vectors(rows, sizes):
    flat = rows.reshape(rows.shape[0], -1)
    out, at = [], 0
    for size in sizes:
        out.append(flat[:, at : at + size].reshape(-1).astype(jnp.float32))
        at += size
    return out


def text_partners():
    return range(1, lax.axis_size("narrow"))


def swap_narrow(block, offset):
    count = lax.axis_size("narrow")
    return lax.ppermute(block, "narrow", [(i, i ^ offset) for i in range(count)])


def head_slices(source, column, pair_width):
    return lax.dynamic_slice_in_dim(source, column, pair_width, 1).reshape(
        source.shape[0], 2, HEAD_DIM
    )


def attend_forward(queries, key_rows, value_rows, allowed):
    row_count = queries.shape[0]
    pair_width = 2 * HEAD_DIM
    groups = queries.shape[1] // pair_width
    scaling = HEAD_DIM ** (-0.5)

    def per_group(group_index, running):
        result, log_sums = running
        column = group_index * pair_width
        query_pair = head_slices(queries, column, pair_width)
        key_pair = head_slices(key_rows, column, pair_width)
        value_pair = head_slices(value_rows, column, pair_width)
        scores = (
            jnp.einsum("qhe,khe->hqk", query_pair, key_pair, preferred_element_type=jnp.float32)
            * scaling
        )
        scores = jnp.where(allowed, scores, NEGATIVE)
        row_max = jnp.max(scores, axis=2, keepdims=True)
        exp_scores = jnp.exp(scores - row_max)
        row_total = jnp.sum(exp_scores, axis=2, keepdims=True)
        weights = (exp_scores / row_total).astype(jnp.bfloat16)
        mixture = jnp.einsum(
            "hqk,khe->qhe", weights, value_pair, preferred_element_type=jnp.float32
        )
        result = lax.dynamic_update_slice_in_dim(
            result, mixture.reshape(row_count, pair_width).astype(jnp.bfloat16), column, 1
        )
        log_sums = lax.dynamic_update_slice_in_dim(
            log_sums, (row_max + jnp.log(row_total))[:, :, 0], 2 * group_index, 0
        )
        return (result, log_sums)

    initial = (
        jnp.zeros((row_count, queries.shape[1]), jnp.bfloat16),
        jnp.zeros((2 * groups, row_count), jnp.float32),
    )
    return lax.fori_loop(0, groups, per_group, initial)


def attend_backward(queries, key_rows, value_rows, allowed, log_sums, grad_mix):
    row_count = queries.shape[0]
    pair_width = 2 * HEAD_DIM
    groups = queries.shape[1] // pair_width
    scaling = HEAD_DIM ** (-0.5)

    def per_group(group_index, running):
        grad_queries, grad_keys, grad_values = running
        column = group_index * pair_width
        query_pair = head_slices(queries, column, pair_width)
        key_pair = head_slices(key_rows, column, pair_width)
        value_pair = head_slices(value_rows, column, pair_width)
        grad_pair = head_slices(grad_mix, column, pair_width)
        pair_sums = lax.dynamic_slice_in_dim(log_sums, 2 * group_index, 2, 0)
        scores = (
            jnp.einsum("qhe,khe->hqk", query_pair, key_pair, preferred_element_type=jnp.float32)
            * scaling
        )
        scores = jnp.where(allowed, scores, NEGATIVE)
        softmax_out = jnp.exp(scores - pair_sums[:, :, None])
        grad_value_pair = jnp.einsum(
            "hqk,qhe->khe",
            softmax_out.astype(jnp.bfloat16),
            grad_pair,
            preferred_element_type=jnp.float32,
        )
        grad_probs = jnp.einsum(
            "qhe,khe->hqk", grad_pair, value_pair, preferred_element_type=jnp.float32
        )
        inner_sum = jnp.sum(softmax_out * grad_probs, axis=2, keepdims=True)
        grad_scores = (softmax_out * (grad_probs - inner_sum)).astype(jnp.bfloat16)
        grad_query_pair = (
            jnp.einsum("hqk,khe->qhe", grad_scores, key_pair, preferred_element_type=jnp.float32)
            * scaling
        )
        grad_key_pair = (
            jnp.einsum("hqk,qhe->khe", grad_scores, query_pair, preferred_element_type=jnp.float32)
            * scaling
        )
        grad_queries = lax.dynamic_update_slice_in_dim(
            grad_queries,
            grad_query_pair.reshape(row_count, pair_width).astype(jnp.bfloat16),
            column,
            1,
        )
        grad_keys = lax.dynamic_update_slice_in_dim(
            grad_keys,
            grad_key_pair.reshape(key_rows.shape[0], pair_width).astype(jnp.bfloat16),
            column,
            1,
        )
        grad_values = lax.dynamic_update_slice_in_dim(
            grad_values,
            grad_value_pair.reshape(key_rows.shape[0], pair_width).astype(jnp.bfloat16),
            column,
            1,
        )
        return (grad_queries, grad_keys, grad_values)

    initial = (
        jnp.zeros(queries.shape, jnp.bfloat16),
        jnp.zeros(key_rows.shape, jnp.bfloat16),
        jnp.zeros(value_rows.shape, jnp.bfloat16),
    )
    return lax.fori_loop(0, groups, per_group, initial)


def on_device(
    image_tokens,
    text_states,
    text_segments,
    image_segment,
    out_grad,
    norm1_gain,
    norm1_bias,
    self_query,
    self_key,
    self_value,
    self_output,
    norm2_gain,
    norm2_bias,
    cross_query,
    cross_key,
    cross_value,
    cross_output,
    norm3_gain,
    norm3_bias,
    mlp_in,
    mlp_in_bias,
    mlp_out,
    mlp_out_bias,
):
    tokens = image_tokens[0].astype(jnp.float32)
    row_count = tokens.shape[0]
    vectors = (
        norm1_gain,
        norm1_bias,
        norm2_gain,
        norm2_bias,
        norm3_gain,
        norm3_bias,
        mlp_in_bias,
        mlp_out_bias,
    )
    sizes = [v.shape[0] for v in vectors]
    shard = self_query.shape[0]
    wide_parts = mlp_in.shape[1] // 1024
    first = gather_rows(
        jnp.concatenate([self_query, self_key, self_value, pack_vectors(vectors)], axis=0)
    )
    second = gather_rows(
        jnp.concatenate(
            [self_output, cross_query, cross_key, cross_value, cross_output]
            + [mlp_in[:, 1024 * k : 1024 * (k + 1)] for k in range(wide_parts)]
            + [mlp_out],
            axis=0,
        )
    )

    def matrix(source, index):
        return source[:, shard * index : shard * (index + 1)].reshape(-1, 1024)

    w_query, w_key, w_value = (matrix(first, k) for k in range(3))
    gain_one, bias_one, gain_two, bias_two, gain_three, bias_three, up_bias, down_bias = (
        take_vectors(first[:, 3 * shard :], sizes)
    )
    w_output, c_query, c_key, c_value, c_output = (matrix(second, k) for k in range(5))
    up_matrix = jnp.concatenate([matrix(second, 5 + k) for k in range(wide_parts)], axis=1)
    down_matrix = second[:, (5 + wide_parts) * shard :].reshape(-1, 1024)

    own_text = text_states[0]
    slots = own_text.shape[0]
    text_full = jnp.concatenate(
        [own_text] + [swap_narrow(own_text, k) for k in text_partners()], axis=0
    )
    narrow_at = lax.axis_index("narrow")
    segments = jnp.concatenate(
        [
            lax.dynamic_slice_in_dim(text_segments[0], (narrow_at ^ k) * slots, slots, 0)
            for k in range(lax.axis_size("narrow"))
        ]
    )
    matches = (segments == image_segment[0, 0])[None, None, :]

    normed_one = layer_norm(tokens, gain_one, bias_one).astype(jnp.bfloat16)
    queries = matmul(normed_one, w_query).astype(jnp.bfloat16)
    key_rows = matmul(normed_one, w_key).astype(jnp.bfloat16)
    value_rows = matmul(normed_one, w_value).astype(jnp.bfloat16)
    row_pos = lax.broadcasted_iota(jnp.int32, (row_count, row_count), 0)
    column_pos = lax.broadcasted_iota(jnp.int32, (row_count, row_count), 1)
    causal = (row_pos >= column_pos)[None]
    mixed_self, sums_self = attend_forward(queries, key_rows, value_rows, causal)
    after_self = tokens + matmul(mixed_self, w_output)
    normed_two = layer_norm(after_self, gain_two, bias_two).astype(jnp.bfloat16)
    cross_queries = matmul(normed_two, c_query).astype(jnp.bfloat16)
    cross_keys = matmul(text_full, c_key).astype(jnp.bfloat16)
    cross_values = matmul(text_full, c_value).astype(jnp.bfloat16)
    mixed_cross, sums_cross = attend_forward(cross_queries, cross_keys, cross_values, matches)
    after_cross = after_self + matmul(mixed_cross, c_output)
    normed_three = layer_norm(after_cross, gain_three, bias_three).astype(jnp.bfloat16)
    hidden_pre = matmul(normed_three, up_matrix) + up_bias
    hidden_act, gelu_pull = jax.vjp(exact_gelu, hidden_pre)
    hidden = hidden_act.astype(jnp.bfloat16)
    block_out = after_cross + matmul(hidden, down_matrix) + down_bias
    grad_out = out_grad[0]
    grad_tail = grad_out.astype(jnp.float32)
    grad_down = scatter_sum(matmul_tn(hidden, grad_out).astype(jnp.bfloat16), 0)
    grad_down_bias = jnp.sum(grad_tail, axis=0)
    grad_hidden = matmul_nt(grad_out, down_matrix)
    grad_pre = gelu_pull(grad_hidden)[0].astype(jnp.bfloat16)
    grad_up = scatter_sum(matmul_tn(normed_three, grad_pre).astype(jnp.bfloat16), 1)
    grad_up_bias = jnp.sum(grad_pre.astype(jnp.float32), axis=0)
    grad_normed = matmul_nt(grad_pre, up_matrix)
    unused_three, norm_pull = jax.vjp(layer_norm, after_cross, gain_three, bias_three)
    grad_middle, grad_gain_three, grad_bias_three = norm_pull(grad_normed)
    grad_after_cross = grad_tail + grad_middle
    grad_mix_out = grad_after_cross.astype(jnp.bfloat16)
    grad_cross_out = scatter_sum(matmul_tn(mixed_cross, grad_mix_out).astype(jnp.bfloat16), 2)
    grad_mixed = matmul_nt(grad_mix_out, c_output).astype(jnp.bfloat16)
    query_grad_two, key_grad_two, value_grad_two = attend_backward(
        cross_queries, cross_keys, cross_values, matches, sums_cross, grad_mixed
    )
    grad_cross_query = scatter_sum(matmul_tn(normed_two, query_grad_two).astype(jnp.bfloat16), 2)
    grad_normed = matmul_nt(query_grad_two, c_query)
    grad_cross_key = scatter_sum(matmul_tn(text_full, key_grad_two).astype(jnp.bfloat16), 0)
    grad_cross_value = scatter_sum(matmul_tn(text_full, value_grad_two).astype(jnp.bfloat16), 1)
    text_term = matmul_nt(key_grad_two, c_key) + matmul_nt(value_grad_two, c_value)
    text_grad = text_term[:slots]
    for k in text_partners():
        text_grad = text_grad + swap_narrow(text_term[k * slots : (k + 1) * slots], k)
    unused_two, norm_pull = jax.vjp(layer_norm, after_self, gain_two, bias_two)
    grad_middle, grad_gain_two, grad_bias_two = norm_pull(grad_normed)
    grad_after_self = grad_after_cross + grad_middle
    grad_self_mix = grad_after_self.astype(jnp.bfloat16)
    grad_self_out = scatter_sum(matmul_tn(mixed_self, grad_self_mix).astype(jnp.bfloat16), 2)
    grad_mixed = matmul_nt(grad_self_mix, w_output).astype(jnp.bfloat16)
    query_grad_one, key_grad_one, value_grad_one = attend_backward(
        queries, key_rows, value_rows, causal, sums_self, grad_mixed
    )
    grad_self_query = scatter_sum(matmul_tn(normed_one, query_grad_one).astype(jnp.bfloat16), 0)
    grad_self_key = scatter_sum(matmul_tn(normed_one, key_grad_one).astype(jnp.bfloat16), 1)
    grad_self_value = scatter_sum(matmul_tn(normed_one, value_grad_one).astype(jnp.bfloat16), 2)
    grad_normed = (
        matmul_nt(query_grad_one, w_query)
        + matmul_nt(key_grad_one, w_key)
        + matmul_nt(value_grad_one, w_value)
    )
    unused_one, norm_pull = jax.vjp(layer_norm, tokens, gain_one, bias_one)
    grad_middle, grad_gain_one, grad_bias_one = norm_pull(grad_normed)
    image_grad = grad_after_self + grad_middle
    vector_terms = (
        grad_gain_one,
        grad_bias_one,
        grad_gain_two,
        grad_bias_two,
        grad_gain_three,
        grad_bias_three,
        grad_up_bias,
        grad_down_bias,
    )
    owners = lax.axis_size("wide") * lax.axis_size("narrow")
    stacked = jnp.concatenate([v.reshape(owners, -1) for v in vector_terms], axis=1)
    width = stacked.shape[1]
    stacked = jnp.pad(stacked, ((0, 0), (0, -width % 1024))).reshape(owners, -1, 128)
    summed = scatter_sum(stacked, 0, jnp.float32).reshape(-1)
    vector_grads, at = [], 0
    for size in sizes:
        vector_grads.append(summed[at : at + size])
        at += size
    return (
        block_out.astype(jnp.bfloat16)[None],
        image_grad[None],
        text_grad[None],
        vector_grads[0],
        vector_grads[1],
        grad_self_query,
        grad_self_key,
        grad_self_value,
        grad_self_out,
        vector_grads[2],
        vector_grads[3],
        grad_cross_query,
        grad_cross_key,
        grad_cross_value,
        grad_cross_out,
        vector_grads[4],
        vector_grads[5],
        grad_up,
        vector_grads[6],
        grad_down,
        vector_grads[7],
    )


def solution(mesh):
    placed = (
        P(("wide", "narrow"), None, None),
        P("wide", "narrow", None),
        P("wide", None),
        P("wide", "narrow"),
        P(("wide", "narrow"), None, None),
        P(("wide", "narrow")),
        P(("wide", "narrow")),
        P(("wide", "narrow"), None),
        P(("wide", "narrow"), None),
        P(("wide", "narrow"), None),
        P(("wide", "narrow"), None),
        P(("wide", "narrow")),
        P(("wide", "narrow")),
        P(("wide", "narrow"), None),
        P(("wide", "narrow"), None),
        P(("wide", "narrow"), None),
        P(("wide", "narrow"), None),
        P(("wide", "narrow")),
        P(("wide", "narrow")),
        P(("wide", "narrow"), None),
        P(("wide", "narrow")),
        P(("wide", "narrow"), None),
        P(("wide", "narrow")),
    )
    return jax.shard_map(
        on_device,
        mesh=mesh,
        in_specs=placed,
        out_specs=(
            P(("wide", "narrow"), None, None),
            P(("wide", "narrow"), None, None),
            P("wide", "narrow", None),
            P(("wide", "narrow")),
            P(("wide", "narrow")),
            P(("wide", "narrow"), None),
            P(("wide", "narrow"), None),
            P(("wide", "narrow"), None),
            P(("wide", "narrow"), None),
            P(("wide", "narrow")),
            P(("wide", "narrow")),
            P(("wide", "narrow"), None),
            P(("wide", "narrow"), None),
            P(("wide", "narrow"), None),
            P(("wide", "narrow"), None),
            P(("wide", "narrow")),
            P(("wide", "narrow")),
            P(("wide", "narrow"), None),
            P(("wide", "narrow")),
            P(("wide", "narrow"), None),
            P(("wide", "narrow")),
        ),
        check_vma=False,
    )
```

time: 2740 us -> 1050 us (0.38)
  waiting for transfers between devices: 1790 us -> 227 us
  blocking collectives: 158 us -> 0 us
  matrix products: 443 us -> 355 us
  starting transfers between devices: 1.22 us -> 63.9 us
    reduce_scatter x9 -> x0, waiting for transfers between devices: 1260 us -> none  [the longest x1 362 us: on_device(): lax.psum_scatter(mlp_terms[4], ('wide', 'narrow'), scatter_dimension=0, t...]
    unnamed x23 -> x2, waiting for transfers between devices: 292 us -> 0.03 us
    all_gather x10 -> x2, waiting for transfers between devices: 243 us -> 101 us  [gather_rows(): whole = lax.all_gather(packed, AXES, axis=0, tiled=True)]
    ppermute x0 -> x61, waiting for transfers between devices: none -> 127 us  [the longest x55 127 us: swap_with(): return lax.ppermute(block, axis, [(i, i ^ 1 << bit) for i in range(count)])]
    unnamed x2 -> x0, blocking collectives: 83.6 us -> none
    all_gather x2 -> x0, blocking collectives: 74.7 us -> none  [the longest x1 64.1 us: fetch_mlp(): lax.all_gather(mlp_in_bias, ('wide', 'narrow'), axis=0, tiled=True)]
    ppermute x0 -> x61, starting transfers between devices: none -> 63.8 us  [the longest x55 55.7 us: swap_with(): return lax.ppermute(block, axis, [(i, i ^ 1 << bit) for i in range(count)])]
    slice x0 -> x7, local copies, waits for them, and re-layouts: none -> 31.6 us  [the longest x2 19.4 us: matrix(): return source[:, shard * index:shard * (index + 1)].reshape(-1, 1024)]
  transfers between devices with their start and end apart: 21 -> 63, of which waited for: 14 -> 26; matrix products, arithmetic and copies ran while one was open for 21% -> 23% of each run, Pallas kernels for 0% -> 0%
where the time goes in v1:
time: 1050 us; the launch traced here: 1030 us
  matrix products  355 us (34%)
  local copies, waits for them, and re-layouts  263 us (25%)
  waiting for transfers between devices  227 us (22%)
  other arithmetic  105 us (10%)
  starting transfers between devices  63.9 us (6%)
  between operations  17.2 us (2%)
    ppermute x55, waiting for transfers between devices, swap_with(): return lax.ppermute(block, axis, [(i, i ^ 1 << bit) for i in range(count)])  127 us
    all_gather x2, waiting for transfers between devices, gather_rows(): whole = lax.all_gather(packed, AXES, axis=0, tiled=True)  101 us
    dot_general x10, matrix products, matmul(): return jnp.dot(leading, trailing, preferred_element_type=jnp.float32)  99 us
    dynamic_slice x112, local copies, waits for them, and re-layouts, head_slices(): lax.dynamic_slice_in_dim(source, column, pair_width, 1)  77.6 us
    dot_general x10, matrix products, matmul_nt(): lax.dot_general(leading, trailing, (((1,), (1,)), ((), ())), preferred_el...  67.1 us
    dot_general x10, matrix products, matmul_tn(): lax.dot_general(leading, trailing, (((0,), (0,)), ((), ())), preferred_el...  56.7 us
    ppermute x55, starting transfers between devices, swap_with(): return lax.ppermute(block, axis, [(i, i ^ 1 << bit) for i in range(count)])  55.7 us
    unnamed x265, local copies, waits for them, and re-layouts  54.7 us
  transfers between devices with their start and end apart: 63, of which 26 were waited for; matrix products, arithmetic and copies ran while one was open for 23% of the time, Pallas kernels for 0%

profile of v1, /device:TPU:0, one launch (start us, length us, event | category | flops | bytes accessed | tf_op | source)
XLA Modules:
  0.0 1034.5 jit_solution(12272770089677037327)
XLA Ops:
  7.2 5.4 concatenate.36
  23.9 4.0 collective-permute-start.2
  32.0 4.6 copy.210
  37.8 52.9 %all-gather.6.cloned.1.call-done = bf16[32,97,1024]{2,1,0:T(8,128)(2,1)} async-done(((bf16[1,97,1024]{2,1,0:T(8,128)(2,1)}), bf16[32,97,1024]{2,1,0:T(8,128)(2,1)}) %all-gather.6.cloned.1.call-update) | async-done | bytes 6357008 | tf_op jit(solution)/shard_map/all_gather | solution.py:84
  94.3 6.2 fusion.141
  101.8 4.0 convolution_convert_fusion.14
  105.8 4.0 copy.204
  109.8 5.6 convolution_convert_fusion.13
  115.4 4.0 copy.205
  119.4 5.6 convolution_convert_fusion.15
  124.9 4.0 copy.203
  130.6 79.2 %while.68 = (s32[]{:T(128)}, bf16[1024,1024]{0,1:T(8,128)(2,1)}, f32[16,1024]{1,0:T(8,128)S(1)}, bf16[1024,1024]{0,1:T(8,128)(2,1)}, bf16[1024,1024]{0,1:T(8,128...) while((s32[]{:T(128)}, bf16[1024,1024]{0,1:T(8,128)(2,1)}, ...), condition=%wide.region_5.6_spmd.clone, body=%wide.region_2.5_spmd.clone.sunk | while | flops 563214336 | bytes 32571624 | solution.py:154
  209.7 47.6 %all-gather.4.cloned.1.call-done = bf16[13312,1024]{1,0:T(8,128)(2,1)} async-done(((bf16[416,1024]{1,0:T(8,128)(2,1)}), bf16[13312,1024]{1,0:T(8,128)(2,1)}) %all-gather.4.cloned.1.call-update) | async-done | bytes 27262992 | tf_op jit(solution)/shard_map/all_gather | solution.py:84
  257.4 13.2 %fusion.140 = (bf16[32,32,1024]{2,1,0:T(8,128)(2,1)}, bf16[32,32,1024]{2,1,0:T(8,128)(2,1)}, bf16[32,32,1024]{2,1,0:T(8,128)(2,1)}, bf16[32,32,1024]{2,1,0:T(8,1...) fusion(bf16[32,416,1024]{2,1,0:T(8,128)(2,1)} %bitcast.625), kind=kLoop, calls=%fused_computation.378 | loop fusion | bytes 37748736 | tf_op jit(solution)/shard_map/slice | solution.py:277
  270.6 9.1 slice.172
  282.6 4.7 fusion.144
  290.4 4.0 convolution_convert_fusion.12
  299.0 13.4 %while.66 = (s32[]{:T(128)}, bf16[1024,1024]{0,1:T(8,128)(2,1)}, f32[16,1024]{1,0:T(8,128)S(1)}, bf16[128,1024]{0,1:T(8,128)(2,1)S(1)}, pred[1,1,128]{2,1,0:T(4,...) while((s32[]{:T(128)}, bf16[1024,1024]{0,1:T(8,128)(2,1)}, ...), condition=%wide.region_11.12_spmd, body=%wide.region_8.11_spmd.sunk | while | flops 69335040 | bytes 4981105 | solution.py:154
  312.4 6.8 fusion.145
  324.3 51.1 %multiply_convert_fusion.2 = (bf16[1024,4096]{1,0:T(8,128)(2,1)}, f32[1024,4096]{1,0:T(8,128)}, f32[1024,4096]{1,0:T(8,128)}) fusion(f32[4096]{0:T(1024)S(1)} %fusion.117, bf16[1024,1024]{1,0:T(8,128)(2,1)S(1)} %bitcast.698, bf16[1024,1024]{1,0:T(8,128)(2,1)S(1)} %bitcast.700, bf16[1024,1024]{1,0:T(8,128)(2,1)S(1)} %bitcast.702, ...), kind=kOutput, calls=%fused_computation.84 | convolution fusion | flops 8900313088 | bytes 52445184 | tf_op jit(solution)/shard_map/dot_general | solution.py:14
  375.4 21.7 %convert_reduce_fusion = (f32[4096]{0:T(1024)}, bf16[1024,4096]{1,0:T(8,128)(2,1)}) fusion(f32[1024,4096]{1,0:T(8,128)} %get-tuple-element.997, bf16[4096,1024]{1,0:T(8,128)(2,1)S(1)} %bitcast.658, bf16[1,1024,1024]{2,1,0:T(8,128)(2,1)} %param.35, f32[1024,4096]{1,0:T(8,128)} %get-tuple-element.1053, f32[4096]{0:T(1024)S(1)} %fusion.117), kind=kOutput, calls=%fused_computation.83 | convolution fusion | flops 8661233664 | bytes 52461568 | tf_op jit(solution)/shard_map/dot_general | solution.py:18
  397.0 16.1 %fusion.147 = (f32[1024]{0:T(1024)}, f32[1024,1024]{1,0:T(8,128)}) fusion(bf16[1024,4096]{1,0:T(8,128)(2,1)} %get-tuple-element.1060, bf16[1024,1024]{1,0:T(8,128)(2,1)} %bitcast.697, bf16[1024,1024]{1,0:T(8,128)(2,1)} %bitcast.699, bf16[1024,1024]{1,0:T(8,128)(2,1)} %bitcast.701, bf16[1024,1024]{1,0:T(8,128)(2,1)} %bitcast.695), kind=kOutput, calls=%fused_computation.385 | convolution fusion | flops 8624536576 | bytes 20975616 | tf_op jit(solution)/shard_map/dot_general | solution.py:18
  413.2 15.0 %convolution_convert_fusion.3 = bf16[1024,4096]{1,0:T(8,128)(2,1)} fusion(bf16[1024,4096]{1,0:T(8,128)(2,1)} %get-tuple-element.1060, f32[1024,1024]{0,1:T(8,128)S(1)} %copy-done.1, f32[1024]{0:T(1024)S(1)} %copy-done.104, f32[1024]{0:T(1024)S(1)} %copy-done.78, f32[1024]{0:T(1024)S(1)} %copy-done.82, f32[1024]{0:T(1024)S(1)} %copy-done.74), kind=kOutput, calls=%fused_computation.104 | convolution fusion | flops 8599371776 | bytes 20987904 | tf_op jit(solution)/shard_map/dot_general | solution.py:24
  428.1 5.7 copy.211
  433.9 5.4 multiply_reduce_fusion.2
  443.9 3.7 convolution_convert_fusion.4
  447.6 3.7 convolution_convert_fusion.11
  453.1 56.6 %while.67 = (s32[]{:T(128)}, bf16[1024,1024]{0,1:T(8,128)(2,1)}, bf16[128,1024]{0,1:T(8,128)(2,1)S(1)}, bf16[128,1024]{0,1:T(8,128)(2,1)S(1)}, bf16[128,1024]{0,...) while((s32[]{:T(128)}, bf16[1024,1024]{0,1:T(8,128)(2,1)}, ...), condition=%wide.region_18.19_spmd, body=%wide.region_16.18_spmd.sunk | while | flops 170440704 | bytes 11739541 | solution.py:221
  509.8 6.7 convolution_convert_fusion.5
  516.5 5.1 fusion.146
  521.6 5.4 copy.216
  527.0 4.2 multiply_reduce_fusion.4
  538.8 3.7 convolution_convert_fusion.6
  542.6 3.8 convolution_convert_fusion.10
  551.2 151.9 %while.69 = (s32[]{:T(128)}, bf16[1024,1024]{0,1:T(8,128)(2,1)}, bf16[1024,1024]{0,1:T(8,128)(2,1)}, bf16[1024,1024]{0,1:T(8,128)(2,1)}, bf16[1024,1024]{0,1:T(8...) while((s32[]{:T(128)}, bf16[1024,1024]{0,1:T(8,128)(2,1)}, ...), condition=%wide.region_23.24_spmd.clone, body=%wide.region_21.23_spmd.clone.sunk | while | flops 1375336448 | bytes 73982224 | solution.py:221
  560.5 3.4 multiply_reduce_fusion.11
  579.4 3.4 multiply_reduce_fusion.11
  617.1 3.4 multiply_reduce_fusion.11
  654.9 3.4 multiply_reduce_fusion.11
  692.7 3.4 multiply_reduce_fusion.11
  703.1 5.5 convolution_convert_fusion.9
  708.6 4.3 fusion.151
  712.9 3.8 convolution_convert_fusion.8
  716.7 4.4 fusion.152
  721.1 11.3 %convolution_convert_fusion.2 = bf16[4096,1024]{1,0:T(8,128)(2,1)} fusion(bf16[1024,4096]{1,0:T(8,128)(2,1)S(1)} %bitcast.771, bf16[1,1024,1024]{2,1,0:T(8,128)(2,1)S(1)} %copy-done.52), kind=kOutput, calls=%fused_computation.103 | convolution fusion | flops 8594128896 | bytes 18874368 | tf_op jit(solution)/shard_map/dot_general | solution.py:24
  732.4 14.8 %fusion.66 = bf16[1,1024,1024]{1,2,0:T(8,128)(2,1)} fusion(f32[1024,1024]{0,1:T(8,128)S(1)} %copy-done.3, f32[1024]{0:T(1024)S(1)} %copy-done.110, bf16[1024,4096]{1,0:T(8,128)(2,1)} %get-tuple-element.996, bf16[4096,1024]{1,0:T(8,128)(2,1)} %bitcast.655), kind=kOutput, calls=%fused_computation.149 | convolution fusion | flops 8593080320 | bytes 23072768 | tf_op jit(solution)/shard_map/dot_general | solution.py:14
  747.2 4.1 copy.236
  768.6 5.5 convolution_convert_fusion.7
  783.8 4.7 dynamic-slice_bitcast_fusion.1
  788.5 5.0 dynamic-slice_bitcast_fusion
  808.7 5.7 copy.237
  830.9 10.1 collective-permute-done.47
  845.2 10.7 %collective-permute-done.32 = bf16[2,4,32,1024]{3,2,1,0:T(8,128)(2,1)S(1)} collective-permute-done((bf16[2,4,32,1024]{3,2,1,0:T(8,128)(2,1)S(1)}, bf16[2,4,32,1024]{3,2,1,0:T(8,128)(2,1)S(1)}, u32[]{:S(2)}, u32[]{:S(2)}) %collective-permute-start.32) | collective-permute-done | bytes 524320 | tf_op jit(solution)/shard_map/ppermute | solution.py:60
  857.5 9.6 collective-permute-done.27
  868.9 8.0 collective-permute-done.22
  880.3 3.6 collective-permute-done.48
  887.7 5.4 collective-permute-done.33
  894.8 3.6 collective-permute-done.28
  918.6 5.8 fusion.44
  943.4 24.2 %collective-permute-done.57 = bf16[8,1,128,1024]{3,2,0,1:T(8,128)(2,1)} collective-permute-done((bf16[8,1,128,1024]{3,2,0,1:T(8,128)(2,1)}, bf16[8,1,128,1024]{3,2,0,1:T(8,128)(2,1)}, u32[]{:S(2)}, u32[]{:S(2)}) %collective-permute-start.57) | collective-permute-done | bytes 2097184 | tf_op jit(solution)/shard_map/ppermute | solution.py:60
  981.3 11.5 %collective-permute-done.58 = bf16[4,1,128,1024]{3,2,0,1:T(8,128)(2,1)S(1)} collective-permute-done((bf16[4,1,128,1024]{3,2,0,1:T(8,128)(2,1)S(1)}, bf16[4,1,128,1024]{3,2,0,1:T(8,128)(2,1)S(1)}, u32[]{:S(2)}, u32[]{:S(2)}) %collective-permute-start.58) | collective-permute-done | bytes 1048608 | tf_op jit(solution)/shard_map/ppermute | solution.py:60
  1000.6 4.6 collective-permute-done.59
  1009.3 12.6 %collective-permute-done.60 = bf16[1,1,128,1024]{3,2,0,1:T(8,128)(2,1)S(1)} collective-permute-done((bf16[1,1,128,1024]{3,2,0,1:T(8,128)(2,1)S(1)}, bf16[1,1,128,1024]{3,2,0,1:T(8,128)(2,1)S(1)}, u32[]{:S(2)}, u32[]{:S(2)}) %collective-permute-start.60) | collective-permute-done | bytes 262176 | tf_op jit(solution)/shard_map/ppermute | solution.py:60
  1022.7 3.6 collective-permute-done.55
  (900 shorter events, 478.4 us)
Async XLA Ops:
  7.2 83.5 %all-gather.6.cloned.1.call-start = ((), (), s32[]{:S(2)}) async-start(), calls=%async_computation.1 | async-start | bytes 7028736 | tf_op jit(solution)/shard_map/all_gather | solution.py:84
  14.3 243.0 %all-gather.4.cloned.1.call-start = ((), (), s32[]{:S(2)}) async-start(), calls=%async_computation | async-start | bytes 28114944 | tf_op jit(solution)/shard_map/all_gather | solution.py:84
  23.9 255.8 %collective-permute-start.2 = (bf16[32,1024]{1,0:T(8,128)(2,1)}, bf16[32,1024]{1,0:T(8,128)(2,1)S(1)}, u32[]{:S(2)}, u32[]{:S(2)}) collective-permute-start(bf16[32,1024]{1,0:T(8,128)(2,1)} %bitcast.752), channel_id=1, source_target_pairs={{0,3},{1,2},{2,1},{3,0},{4,7},{5,6},{6,5},{7,4},{8,11},{9,10},{10,... | collective-permute-start | bytes 196616 | tf_op jit(solution)/shard_map/ppermute | solution.py:109
  27.8 251.9 %collective-permute-start.1 = (bf16[32,1024]{1,0:T(8,128)(2,1)}, bf16[32,1024]{1,0:T(8,128)(2,1)S(1)}, u32[]{:S(2)}, u32[]{:S(2)}) collective-permute-start(bf16[32,1024]{1,0:T(8,128)(2,1)} %bitcast.753), channel_id=1, source_target_pairs={{0,2},{1,3},{2,0},{3,1},{4,6},{5,7},{6,4},{7,5},{8,10},{9,11},{10,... | collective-permute-start | bytes 196616 | tf_op jit(solution)/shard_map/ppermute | solution.py:109
  28.3 251.4 %collective-permute-start = (bf16[32,1024]{1,0:T(8,128)(2,1)}, bf16[32,1024]{1,0:T(8,128)(2,1)S(1)}, u32[]{:S(2)}, u32[]{:S(2)}) collective-permute-start(bf16[32,1024]{1,0:T(8,128)(2,1)} %bitcast.754), channel_id=1, source_target_pairs={{0,1},{1,0},{2,3},{3,2},{4,5},{5,4},{6,7},{7,6},{8,9},{9,8},{10,11... | collective-permute-start | bytes 196616 | tf_op jit(solution)/shard_map/ppermute | solution.py:109
  32.0 250.6 %copy-start.7 = (bf16[1,1024,1024]{1,2,0:T(8,128)(2,1)}, bf16[1,1024,1024]{1,2,0:T(8,128)(2,1)S(1)}, u32[]{:S(2)}) copy-start(bf16[1,1024,1024]{1,2,0:T(8,128)(2,1)S(1)} %copy.201) | copy-start | bytes 6291460
  757.4 57.8 %collective-permute-start.3 = (f32[32,1024]{1,0:T(8,128)}, f32[32,1024]{1,0:T(8,128)S(1)}, u32[]{:S(2)}, u32[]{:S(2)}) collective-permute-start(f32[32,1024]{1,0:T(8,128)} %get-tuple-element.1028), channel_id=1, source_target_pairs={{0,1},{1,0},{2,3},{3,2},{4,5},{5,4},{6,7},{7,6},{8,9},{9,8},{10,11... | collective-permute-start | bytes 393224 | tf_op jit(solution)/shard_map/ppermute | solution.py:109
  758.8 57.4 %collective-permute-start.5 = (f32[32,1024]{1,0:T(8,128)}, f32[32,1024]{1,0:T(8,128)S(1)}, u32[]{:S(2)}, u32[]{:S(2)}) collective-permute-start(f32[32,1024]{1,0:T(8,128)} %get-tuple-element.1029), channel_id=1, source_target_pairs={{0,3},{1,2},{2,1},{3,0},{4,7},{5,6},{6,5},{7,4},{8,11},{9,10},{10,... | collective-permute-start | bytes 393224 | tf_op jit(solution)/shard_map/ppermute | solution.py:109
  760.3 56.0 %collective-permute-start.4 = (f32[32,1024]{1,0:T(8,128)}, f32[32,1024]{1,0:T(8,128)S(1)}, u32[]{:S(2)}, u32[]{:S(2)}) collective-permute-start(f32[32,1024]{1,0:T(8,128)} %get-tuple-element.1030), channel_id=1, source_target_pairs={{0,2},{1,3},{2,0},{3,1},{4,6},{5,7},{6,4},{7,5},{8,10},{9,11},{10,... | collective-permute-start | bytes 393224 | tf_op jit(solution)/shard_map/ppermute | solution.py:109
  762.0 56.5 %collective-permute-start.46 = (bf16[4,4,32,1024]{3,2,1,0:T(8,128)(2,1)}, bf16[4,4,32,1024]{3,2,1,0:T(8,128)(2,1)}, u32[]{:S(2)}, u32[]{:S(2)}) collective-permute-start(bf16[4,4,32,1024]{3,2,1,0:T(8,128)(2,1)} %dynamic-slice_bitcast_fusion.6), channel_id=1, source_target_pairs={{0,4},{4,0},{8,12},{12,8},{16,20},{20,16},{24,28},{28,24},{1,5},{5... | collective-permute-start | bytes 3145736 | tf_op jit(solution)/shard_map/ppermute | solution.py:60
  783.2 11.3 %collective-permute-start.6 = (f32[4,4,1,8,128]{4,3,1,0,2:T(8,128)S(1)}, f32[4,4,1,8,128]{4,3,1,0,2:T(8,128)S(1)}, u32[]{:S(2)}, u32[]{:S(2)}) collective-permute-start(f32[4,4,1,8,128]{4,3,1,0,2:T(8,128)S(1)} %dynamic-slice_bitcast_fusion.37), channel_id=1, source_target_pairs={{0,4},{4,0},{8,12},{12,8},{16,20},{20,16},{24,28},{28,24},{1,5},{5... | collective-permute-start | bytes 196616 | tf_op jit(solution)/shard_map/ppermute | solution.py:60
  794.6 4.0 collective-permute-start.7
  798.6 3.8 collective-permute-start.8
  802.4 3.7 collective-permute-start.9
  806.1 8.4 collective-permute-start.10
  814.5 5.7 collective-permute-start.41
  815.2 6.0 collective-permute-start.36
  816.2 5.6 collective-permute-start.31
  816.3 7.2 collective-permute-start.26
  818.4 8.2 collective-permute-start.21
  820.2 7.4 collective-permute-start.11
  821.2 8.4 collective-permute-start.16
  822.4 96.2 %collective-permute-start.56 = (bf16[4,4,128,1024]{3,2,1,0:T(8,128)(2,1)S(1)}, bf16[4,4,128,1024]{3,2,1,0:T(8,128)(2,1)}, u32[]{:S(2)}, u32[]{:S(2)}) collective-permute-start(bf16[4,4,128,1024]{3,2,1,0:T(8,128)(2,1)S(1)} %copy-done.22), channel_id=1, source_target_pairs={{0,4},{4,0},{8,12},{12,8},{16,20},{20,16},{24,28},{28,24},{1,5},{5... | collective-permute-start | bytes 12582920 | tf_op jit(solution)/shard_map/ppermute | solution.py:60
  824.5 103.2 %collective-permute-start.51 = (bf16[4,4,32,4096]{3,2,1,0:T(8,128)(2,1)S(1)}, bf16[4,4,32,4096]{3,2,1,0:T(8,128)(2,1)S(1)}, u32[]{:S(2)}, u32[]{:S(2)}) collective-permute-start(bf16[4,4,32,4096]{3,2,1,0:T(8,128)(2,1)S(1)} %copy-done.21), channel_id=1, source_target_pairs={{0,4},{4,0},{8,12},{12,8},{16,20},{20,16},{24,28},{28,24},{1,5},{5... | collective-permute-start | bytes 12582920 | tf_op jit(solution)/shard_map/ppermute | solution.py:60
  826.7 14.3 %collective-permute-start.47 = (bf16[2,4,32,1024]{3,2,1,0:T(8,128)(2,1)S(1)}, bf16[2,4,32,1024]{3,2,1,0:T(8,128)(2,1)S(1)}, u32[]{:S(2)}, u32[]{:S(2)}) collective-permute-start(bf16[2,4,32,1024]{3,2,1,0:T(8,128)(2,1)S(1)} %dynamic-slice_bitcast_fusion.15), channel_id=1, source_target_pairs={{0,8},{4,12},{8,0},{12,4},{16,24},{20,28},{24,16},{28,20},{1,9},{5... | collective-permute-start | bytes 1572872 | tf_op jit(solution)/shard_map/ppermute | solution.py:60
  827.6 14.1 %collective-permute-start.42 = (bf16[4,2,32,1024]{3,2,1,0:T(8,128)(2,1)S(1)}, bf16[4,2,32,1024]{3,2,1,0:T(8,128)(2,1)S(1)}, u32[]{:S(2)}, u32[]{:S(2)}) collective-permute-start(bf16[4,2,32,1024]{3,2,1,0:T(8,128)(2,1)S(1)} %dynamic-slice_bitcast_fusion.16), channel_id=1, source_target_pairs={{0,2},{1,3},{2,0},{3,1},{4,6},{5,7},{6,4},{7,5},{8,10},{9,11},{10,... | collective-permute-start | bytes 1572872 | tf_op jit(solution)/shard_map/ppermute | solution.py:60
  829.6 13.9 %collective-permute-start.37 = (bf16[8,1,32,1024]{3,2,0,1:T(8,128)(2,1)S(1)}, bf16[8,1,32,1024]{3,2,0,1:T(8,128)(2,1)S(1)}, u32[]{:S(2)}, u32[]{:S(2)}) collective-permute-start(bf16[8,1,32,1024]{3,2,0,1:T(8,128)(2,1)S(1)} %dynamic-slice_bitcast_fusion.17), channel_id=1, source_target_pairs={{0,1},{1,0},{2,3},{3,2},{4,5},{5,4},{6,7},{7,6},{8,9},{9,8},{10,11... | collective-permute-start | bytes 1572872 | tf_op jit(solution)/shard_map/ppermute | solution.py:60
  841.0 14.8 %collective-permute-start.32 = (bf16[2,4,32,1024]{3,2,1,0:T(8,128)(2,1)S(1)}, bf16[2,4,32,1024]{3,2,1,0:T(8,128)(2,1)S(1)}, u32[]{:S(2)}, u32[]{:S(2)}) collective-permute-start(bf16[2,4,32,1024]{3,2,1,0:T(8,128)(2,1)S(1)} %dynamic-slice_bitcast_fusion.18), channel_id=1, source_target_pairs={{0,8},{4,12},{8,0},{12,4},{16,24},{20,28},{24,16},{28,20},{1,9},{5... | collective-permute-start | bytes 1572872 | tf_op jit(solution)/shard_map/ppermute | solution.py:60
  841.7 25.4 %collective-permute-start.27 = (bf16[2,4,32,1024]{3,2,1,0:T(8,128)(2,1)S(1)}, bf16[2,4,32,1024]{3,2,1,0:T(8,128)(2,1)S(1)}, u32[]{:S(2)}, u32[]{:S(2)}) collective-permute-start(bf16[2,4,32,1024]{3,2,1,0:T(8,128)(2,1)S(1)} %dynamic-slice_bitcast_fusion.19), channel_id=1, source_target_pairs={{0,8},{4,12},{8,0},{12,4},{16,24},{20,28},{24,16},{28,20},{1,9},{5... | collective-permute-start | bytes 1572872 | tf_op jit(solution)/shard_map/ppermute | solution.py:60
  843.5 33.4 %collective-permute-start.22 = (bf16[2,4,32,1024]{3,2,1,0:T(8,128)(2,1)S(1)}, bf16[2,4,32,1024]{3,2,1,0:T(8,128)(2,1)S(1)}, u32[]{:S(2)}, u32[]{:S(2)}) collective-permute-start(bf16[2,4,32,1024]{3,2,1,0:T(8,128)(2,1)S(1)} %dynamic-slice_bitcast_fusion.20), channel_id=1, source_target_pairs={{0,8},{4,12},{8,0},{12,4},{16,24},{20,28},{24,16},{28,20},{1,9},{5... | collective-permute-start | bytes 1572872 | tf_op jit(solution)/shard_map/ppermute | solution.py:60
  855.8 22.7 %collective-permute-start.12 = (bf16[8,1,32,1024]{3,2,0,1:T(8,128)(2,1)S(1)}, bf16[8,1,32,1024]{3,2,0,1:T(8,128)(2,1)S(1)}, u32[]{:S(2)}, u32[]{:S(2)}) collective-permute-start(bf16[8,1,32,1024]{3,2,0,1:T(8,128)(2,1)S(1)} %dynamic-slice_bitcast_fusion.22), channel_id=1, source_target_pairs={{0,1},{1,0},{2,3},{3,2},{4,5},{5,4},{6,7},{7,6},{8,9},{9,8},{10,11... | collective-permute-start | bytes 1572872 | tf_op jit(solution)/shard_map/ppermute | solution.py:60
  867.1 12.2 %collective-permute-start.17 = (bf16[4,2,32,1024]{3,2,1,0:T(8,128)(2,1)S(1)}, bf16[4,2,32,1024]{3,2,1,0:T(8,128)(2,1)S(1)}, u32[]{:S(2)}, u32[]{:S(2)}) collective-permute-start(bf16[4,2,32,1024]{3,2,1,0:T(8,128)(2,1)S(1)} %dynamic-slice_bitcast_fusion.21), channel_id=1, source_target_pairs={{0,2},{1,3},{2,0},{3,1},{4,6},{5,7},{6,4},{7,5},{8,10},{9,11},{10,... | collective-permute-start | bytes 1572872 | tf_op jit(solution)/shard_map/ppermute | solution.py:60
  876.9 7.0 collective-permute-start.48
  878.6 6.8 collective-permute-start.43
  879.3 6.8 collective-permute-start.38
  883.9 9.2 collective-permute-start.33
  885.4 13.0 %collective-permute-start.28 = (bf16[4,1,32,1024]{3,2,0,1:T(8,128)(2,1)S(1)}, bf16[4,1,32,1024]{3,2,0,1:T(8,128)(2,1)S(1)}, u32[]{:S(2)}, u32[]{:S(2)}) collective-permute-start(bf16[4,1,32,1024]{3,2,0,1:T(8,128)(2,1)S(1)} %dynamic-slice_bitcast_fusion.27), channel_id=1, source_target_pairs={{0,1},{1,0},{2,3},{3,2},{4,5},{5,4},{6,7},{7,6},{8,9},{9,8},{10,11... | collective-permute-start | bytes 786440 | tf_op jit(solution)/shard_map/ppermute | solution.py:60
  886.2 15.0 %collective-permute-start.23 = (bf16[4,1,32,1024]{3,2,0,1:T(8,128)(2,1)S(1)}, bf16[4,1,32,1024]{3,2,0,1:T(8,128)(2,1)S(1)}, u32[]{:S(2)}, u32[]{:S(2)}) collective-permute-start(bf16[4,1,32,1024]{3,2,0,1:T(8,128)(2,1)S(1)} %dynamic-slice_bitcast_fusion.28), channel_id=1, source_target_pairs={{0,1},{1,0},{2,3},{3,2},{4,5},{5,4},{6,7},{7,6},{8,9},{9,8},{10,11... | collective-permute-start | bytes 786440 | tf_op jit(solution)/shard_map/ppermute | solution.py:60
  893.1 9.7 collective-permute-start.13
  898.4 7.8 collective-permute-start.18
  901.2 6.3 collective-permute-start.49
  902.8 6.2 collective-permute-start.44
  906.1 5.9 collective-permute-start.39
  907.5 6.1 collective-permute-start.34
  909.0 5.8 collective-permute-start.29
  912.0 5.0 collective-permute-start.24
  913.6 16.8 %collective-permute-start.14 = (bf16[2,1,32,1024]{3,2,0,1:T(8,128)(2,1)S(1)}, bf16[2,1,32,1024]{3,2,0,1:T(8,128)(2,1)}, u32[]{:S(2)}, u32[]{:S(2)}) collective-permute-start(bf16[2,1,32,1024]{3,2,0,1:T(8,128)(2,1)S(1)} %dynamic-slice_bitcast_fusion.36), channel_id=1, source_target_pairs={{0,8},{4,12},{8,0},{12,4},{16,24},{20,28},{24,16},{28,20},{1,9},{5... | collective-permute-start | bytes 393224 | tf_op jit(solution)/shard_map/ppermute | solution.py:60
  914.8 18.0 %collective-permute-start.19 = (bf16[2,1,32,1024]{3,2,1,0:T(8,128)(2,1)S(1)}, bf16[2,1,32,1024]{3,2,1,0:T(8,128)(2,1)}, u32[]{:S(2)}, u32[]{:S(2)}) collective-permute-start(bf16[2,1,32,1024]{3,2,1,0:T(8,128)(2,1)S(1)} %constant_dynamic-slice_fusion.27), channel_id=1, source_target_pairs={{0,1},{1,0},{2,3},{3,2},{4,5},{5,4},{6,7},{7,6},{8,9},{9,8},{10,11... | collective-permute-start | bytes 393224 | tf_op jit(solution)/shard_map/ppermute | solution.py:60
  917.0 18.5 %collective-permute-start.50 = (bf16[1,1,32,1024]{3,2,0,1:T(8,128)(2,1)}, bf16[1,1,32,1024]{3,2,0,1:T(8,128)(2,1)}, u32[]{:S(2)}, u32[]{:S(2)}) collective-permute-start(bf16[1,1,32,1024]{3,2,0,1:T(8,128)(2,1)} %constant_dynamic-slice_fusion.19), channel_id=1, source_target_pairs={{0,16},{4,20},{8,24},{12,28},{16,0},{20,4},{24,8},{28,12},{1,17},{... | collective-permute-start | bytes 196616 | tf_op jit(solution)/shard_map/ppermute | solution.py:60
  925.9 41.7 %collective-permute-start.57 = (bf16[8,1,128,1024]{3,2,0,1:T(8,128)(2,1)}, bf16[8,1,128,1024]{3,2,0,1:T(8,128)(2,1)}, u32[]{:S(2)}, u32[]{:S(2)}) collective-permute-start(bf16[8,1,128,1024]{3,2,0,1:T(8,128)(2,1)} %dynamic-slice_bitcast_fusion.2), channel_id=1, source_target_pairs={{0,1},{1,0},{2,3},{3,2},{4,5},{5,4},{6,7},{7,6},{8,9},{9,8},{10,11... | collective-permute-start | bytes 6291464 | tf_op jit(solution)/shard_map/ppermute | solution.py:60
  930.0 43.3 %collective-permute-start.52 = (bf16[4,2,32,4096]{3,2,1,0:T(8,128)(2,1)S(1)}, bf16[4,2,32,4096]{3,2,1,0:T(8,128)(2,1)S(1)}, u32[]{:S(2)}, u32[]{:S(2)}) collective-permute-start(bf16[4,2,32,4096]{3,2,1,0:T(8,128)(2,1)S(1)} %dynamic-slice_bitcast_fusion.3), channel_id=1, source_target_pairs={{0,2},{1,3},{2,0},{3,1},{4,6},{5,7},{6,4},{7,5},{8,10},{9,11},{10,... | collective-permute-start | bytes 6291464 | tf_op jit(solution)/shard_map/ppermute | solution.py:60
  930.6 8.6 collective-permute-start.45
  932.9 7.8 collective-permute-start.40
  935.5 40.9 %collective-permute-start.35 = (bf16[1,1,32,1024]{3,2,0,1:T(8,128)(2,1)S(1)}, bf16[1,1,32,1024]{3,2,0,1:T(8,128)(2,1)S(1)}, u32[]{:S(2)}, u32[]{:S(2)}) collective-permute-start(bf16[1,1,32,1024]{3,2,0,1:T(8,128)(2,1)S(1)} %constant_dynamic-slice_fusion.23), channel_id=1, source_target_pairs={{0,16},{4,20},{8,24},{12,28},{16,0},{20,4},{24,8},{28,12},{1,17},{... | collective-permute-start | bytes 196616 | tf_op jit(solution)/shard_map/ppermute | solution.py:60
  939.2 39.2 %collective-permute-start.30 = (bf16[1,1,32,1024]{3,2,0,1:T(8,128)(2,1)S(1)}, bf16[1,1,32,1024]{3,2,0,1:T(8,128)(2,1)S(1)}, u32[]{:S(2)}, u32[]{:S(2)}) collective-permute-start(bf16[1,1,32,1024]{3,2,0,1:T(8,128)(2,1)S(1)} %constant_dynamic-slice_fusion.24), channel_id=1, source_target_pairs={{0,16},{4,20},{8,24},{12,28},{16,0},{20,4},{24,8},{28,12},{1,17},{... | collective-permute-start | bytes 196616 | tf_op jit(solution)/shard_map/ppermute | solution.py:60
  940.7 39.9 %collective-permute-start.25 = (bf16[1,1,32,1024]{3,2,0,1:T(8,128)(2,1)S(1)}, bf16[1,1,32,1024]{3,2,0,1:T(8,128)(2,1)S(1)}, u32[]{:S(2)}, u32[]{:S(2)}) collective-permute-start(bf16[1,1,32,1024]{3,2,0,1:T(8,128)(2,1)S(1)} %constant_dynamic-slice_fusion.25), channel_id=1, source_target_pairs={{0,16},{4,20},{8,24},{12,28},{16,0},{20,4},{24,8},{28,12},{1,17},{... | collective-permute-start | bytes 196616 | tf_op jit(solution)/shard_map/ppermute | solution.py:60
  967.7 32.2 %collective-permute-start.15 = (bf16[1,1,32,1024]{3,2,0,1:T(8,128)(2,1)S(1)}, bf16[1,1,32,1024]{3,2,0,1:T(8,128)(2,1)S(1)}, u32[]{:S(2)}, u32[]{:S(2)}) collective-permute-start(bf16[1,1,32,1024]{3,2,0,1:T(8,128)(2,1)S(1)} %constant_dynamic-slice_fusion.28), channel_id=1, source_target_pairs={{0,16},{4,20},{8,24},{12,28},{16,0},{20,4},{24,8},{28,12},{1,17},{... | collective-permute-start | bytes 196616 | tf_op jit(solution)/shard_map/ppermute | solution.py:60
  973.3 19.5 %collective-permute-start.58 = (bf16[4,1,128,1024]{3,2,0,1:T(8,128)(2,1)S(1)}, bf16[4,1,128,1024]{3,2,0,1:T(8,128)(2,1)S(1)}, u32[]{:S(2)}, u32[]{:S(2)}) collective-permute-start(bf16[4,1,128,1024]{3,2,0,1:T(8,128)(2,1)S(1)} %dynamic-slice_bitcast_fusion.4), channel_id=1, source_target_pairs={{0,2},{1,3},{2,0},{3,1},{4,6},{5,7},{6,4},{7,5},{8,10},{9,11},{10,... | collective-permute-start | bytes 3145736 | tf_op jit(solution)/shard_map/ppermute | solution.py:60
  976.5 20.0 %collective-permute-start.53 = (bf16[2,2,32,4096]{3,2,1,0:T(8,128)(2,1)S(1)}, bf16[2,2,32,4096]{3,2,1,0:T(8,128)(2,1)S(1)}, u32[]{:S(2)}, u32[]{:S(2)}) collective-permute-start(bf16[2,2,32,4096]{3,2,1,0:T(8,128)(2,1)S(1)} %dynamic-slice_bitcast_fusion.5), channel_id=1, source_target_pairs={{0,8},{4,12},{8,0},{12,4},{16,24},{20,28},{24,16},{28,20},{1,9},{5... | collective-permute-start | bytes 3145736 | tf_op jit(solution)/shard_map/ppermute | solution.py:60
  978.4 30.2 %collective-permute-start.20 = (bf16[1,1,32,1024]{3,2,1,0:T(8,128)(2,1)S(1)}, bf16[1,1,32,1024]{3,2,1,0:T(8,128)(2,1)S(1)}, u32[]{:S(2)}, u32[]{:S(2)}) collective-permute-start(bf16[1,1,32,1024]{3,2,1,0:T(8,128)(2,1)S(1)} %constant_dynamic-slice_fusion.26), channel_id=1, source_target_pairs={{0,16},{4,20},{8,24},{12,28},{16,0},{20,4},{24,8},{28,12},{1,17},{... | collective-permute-start | bytes 196616 | tf_op jit(solution)/shard_map/ppermute | solution.py:60
  993.2 11.9 %collective-permute-start.59 = (bf16[2,1,128,1024]{3,2,0,1:T(8,128)(2,1)S(1)}, bf16[2,1,128,1024]{3,2,0,1:T(8,128)(2,1)S(1)}, u32[]{:S(2)}, u32[]{:S(2)}) collective-permute-start(bf16[2,1,128,1024]{3,2,0,1:T(8,128)(2,1)S(1)} %dynamic-slice_bitcast_fusion.14), channel_id=1, source_target_pairs={{0,8},{4,12},{8,0},{12,4},{16,24},{20,28},{24,16},{28,20},{1,9},{5... | collective-permute-start | bytes 1572872 | tf_op jit(solution)/shard_map/ppermute | solution.py:60
  996.7 10.3 collective-permute-start.54
  1005.4 16.5 %collective-permute-start.60 = (bf16[1,1,128,1024]{3,2,0,1:T(8,128)(2,1)S(1)}, bf16[1,1,128,1024]{3,2,0,1:T(8,128)(2,1)S(1)}, u32[]{:S(2)}, u32[]{:S(2)}) collective-permute-start(bf16[1,1,128,1024]{3,2,0,1:T(8,128)(2,1)S(1)} %constant_dynamic-slice_fusion.16), channel_id=1, source_target_pairs={{0,16},{4,20},{8,24},{12,28},{16,0},{20,4},{24,8},{28,12},{1,17},{... | collective-permute-start | bytes 786440 | tf_op jit(solution)/shard_map/ppermute | solution.py:60
  1007.2 19.1 %collective-permute-start.55 = (bf16[1,1,32,4096]{3,2,1,0:T(8,128)(2,1)S(1)}, bf16[1,1,32,4096]{3,2,1,0:T(8,128)(2,1)S(1)}, u32[]{:S(2)}, u32[]{:S(2)}) collective-permute-start(bf16[1,1,32,4096]{3,2,1,0:T(8,128)(2,1)S(1)} %constant_dynamic-slice_fusion.17), channel_id=1, source_target_pairs={{0,16},{4,20},{8,24},{12,28},{16,0},{20,4},{24,8},{28,12},{1,17},{... | collective-permute-start | bytes 786440 | tf_op jit(solution)/shard_map/ppermute | solution.py:60
  (122 other events, 2428.8 us)
Sparse Core Ops, SparseCore 0:
  14.4 76.2 all-gather.5
  94.1 163.1 all-gather.3

commit v2 on v1

v2 whole, which is shorter than its diff:
```python
import functools
import math

import jax
import jax.numpy as jnp
from jax import lax
from jax.experimental import pallas as pl
from jax.experimental.pallas import tpu as pltpu
from jax.sharding import PartitionSpec as P

HEAD_DIM = 64
TILE = 256
BF16 = jnp.bfloat16
VMEM_LIMIT = 60 * 1024 * 1024

EPSILON = 1e-05
NEGATIVE = -1e30

AXES = ("wide", "narrow")


def axis_bits(axis):
    return lax.axis_size(axis).bit_length() - 1


def halving_order(kind):
    wide = [("wide", k) for k in range(1, axis_bits("wide"))]
    narrow = [("narrow", k) for k in range(axis_bits("narrow"))]
    core = [("wide", 0)]
    if kind == 0:
        return core + narrow + wide
    if kind == 1:
        return core + narrow[1:] + wide[:1] + narrow[:1] + wide[1:]
    return core + wide[:1] + narrow + wide[1:]


def gather_rows(packed):
    whole = lax.all_gather(packed, AXES, axis=0, tiled=True)
    return whole.reshape((-1,) + packed.shape)


def pack_vectors(vectors):
    flat = jnp.concatenate(vectors)
    room = -flat.shape[0] % (16 * 1024)
    return jnp.pad(flat, (0, room)).reshape(-1, 1024)


def take_vectors(rows, sizes):
    flat = rows.reshape(rows.shape[0], -1)
    out, at = [], 0
    for size in sizes:
        out.append(flat[:, at : at + size].reshape(1, -1).astype(jnp.float32))
        at += size
    return out


def text_partners():
    return range(1, lax.axis_size("narrow"))


def swap_narrow(block, offset):
    count = lax.axis_size("narrow")
    return lax.ppermute(block, "narrow", [(i, i ^ offset) for i in range(count)])


def nn(a, b):
    return lax.dot_general(a, b, (((1,), (0,)), ((), ())), preferred_element_type=jnp.float32)


def nt(a, b):
    return lax.dot_general(a, b, (((1,), (1,)), ((), ())), preferred_element_type=jnp.float32)


def tn(a, b):
    return lax.dot_general(a, b, (((0,), (0,)), ((), ())), preferred_element_type=jnp.float32)


def standardize(values):
    center = jnp.mean(values, axis=-1, keepdims=True)
    offset = values - center
    rate = lax.rsqrt(jnp.mean(offset * offset, axis=-1, keepdims=True) + EPSILON)
    return offset * rate, rate


def norm_back(standard, rate, gain, grad):
    scaled = grad * gain
    return rate * (
        scaled
        - jnp.mean(scaled, axis=-1, keepdims=True)
        - standard * jnp.mean(scaled * standard, axis=-1, keepdims=True)
    )


def column_sum(values):
    return jnp.sum(values, axis=0, keepdims=True)


def square(ref):
    return ref[...].reshape(-1, ref.shape[-1])


def head_lanes(block, head):
    lane = lax.broadcasted_iota(jnp.int32, block.shape, 1)
    inside = (lane >= HEAD_DIM) if head else (lane < HEAD_DIM)
    return jnp.where(inside, block, jnp.zeros_like(block))


def whole_block(shape):
    zeros = (0,) * len(shape)
    return pl.BlockSpec(shape, lambda *_: zeros, pipeline_mode=pl.Buffered(1))


def params(**extra):
    return pltpu.CompilerParams(vmem_limit_bytes=VMEM_LIMIT, **extra)


def project_kernel(x_ref, gain_ref, bias_ref, wq_ref, wk_ref, wv_ref, h_ref, q_ref, k_ref, v_ref):
    standard, _ = standardize(x_ref[...].astype(jnp.float32))
    normed = (standard * gain_ref[...] + bias_ref[...]).astype(BF16)
    h_ref[...] = normed
    q_ref[...] = nn(normed, square(wq_ref)).astype(BF16)
    k_ref[...] = nn(normed, square(wk_ref)).astype(BF16)
    v_ref[...] = nn(normed, square(wv_ref)).astype(BF16)


def project(tokens, gain, bias, weights):
    rows, width = tokens.shape
    tile = pl.BlockSpec((TILE, width), lambda i: (i, 0))
    arrays, specs = zip(*weights)
    return pl.pallas_call(
        project_kernel,
        grid=(rows // TILE,),
        in_specs=[tile, whole_block(gain.shape), whole_block(bias.shape), *specs],
        out_specs=[tile] * 4,
        out_shape=[jax.ShapeDtypeStruct(tokens.shape, BF16)] * 4,
        compiler_params=params(),
        cost_estimate=pl.CostEstimate(
            flops=6 * rows * width * width, bytes_accessed=16 * width * width, transcendentals=0
        ),
        name="self_project",
    )(tokens, gain, bias, *arrays)


def attend_kernel(q_ref, k_ref, v_ref, o_ref, sums_ref):
    rows, width = q_ref.shape
    flipped = v_ref[...].T
    for start in range(0, rows, TILE):
        span = start + TILE
        queries = q_ref[start:span, :] * (HEAD_DIM**-0.5)
        keys = k_ref[:span, :]
        mixed, sums = [], []
        for head in range(2):
            scores = nt(keys, head_lanes(queries, head))
            key_at = lax.broadcasted_iota(jnp.int32, (TILE, TILE), 0)
            query_at = lax.broadcasted_iota(jnp.int32, (TILE, TILE), 1)
            corner = jnp.where(key_at <= query_at, scores[start:], NEGATIVE)
            scores = jnp.concatenate([scores[:start], corner], axis=0) if start else corner
            top = jnp.max(scores, axis=0, keepdims=True)
            powers = jnp.exp(scores - top)
            total = jnp.sum(powers, axis=0, keepdims=True)
            part = nn(flipped[HEAD_DIM * head : HEAD_DIM * (head + 1), :span], powers.astype(BF16))
            mixed.append(part * (1.0 / total))
            sums.append(top + jnp.log(total))
        o_ref[start:span, :] = jnp.concatenate(mixed, axis=0).T.astype(BF16)
        sums_ref[0, :, start:span] = jnp.concatenate(sums, axis=0)


def attend(queries, keys, values):
    rows, width = queries.shape
    pairs = width // 128
    block = pl.BlockSpec((rows, 128), lambda p: (0, p))
    return pl.pallas_call(
        attend_kernel,
        grid=(pairs,),
        in_specs=[block] * 3,
        out_specs=[block, pl.BlockSpec((1, 2, rows), lambda p: (p, 0, 0))],
        out_shape=[
            jax.ShapeDtypeStruct(queries.shape, BF16),
            jax.ShapeDtypeStruct((pairs, 2, rows), jnp.float32),
        ],
        compiler_params=params(),
        cost_estimate=pl.CostEstimate(
            flops=24 * rows * rows * width,
            bytes_accessed=8 * rows * width,
            transcendentals=rows * rows * 16,
        ),
        name="self_attend",
    )(queries, keys, values)


def attend_back_kernel(q_ref, k_ref, v_ref, da_ref, sums_ref, dq_ref, dk_ref, dv_ref, dk_sum, dv_sum):
    rows, width = q_ref.shape
    flipped = k_ref[...].T
    for start in reversed(range(0, rows, TILE)):
        span = start + TILE
        queries = q_ref[start:span, :] * (HEAD_DIM**-0.5)
        grads = da_ref[start:span, :]
        keys = k_ref[:span, :]
        values = v_ref[:span, :]
        parts = []
        for head in range(2):
            own_queries = head_lanes(queries, head)
            own_grads = head_lanes(grads, head)
            scores = nt(keys, own_queries)
            key_at = lax.broadcasted_iota(jnp.int32, (TILE, TILE), 0)
            query_at = lax.broadcasted_iota(jnp.int32, (TILE, TILE), 1)
            corner = jnp.where(key_at <= query_at, scores[start:], NEGATIVE)
            scores = jnp.concatenate([scores[:start], corner], axis=0) if start else corner
            probs = jnp.exp(scores - sums_ref[0, head : head + 1, start:span])
            grad_probs = nt(values, own_grads)
            inner = jnp.sum(probs * grad_probs, axis=0, keepdims=True)
            grad_scores = (probs * (grad_probs - inner)).astype(BF16)
            value_term = nn(probs.astype(BF16), own_grads)
            key_term = nn(grad_scores, own_queries)
            if span == rows and head == 0:
                dv_sum[...] = value_term
                dk_sum[...] = key_term
            else:
                dv_sum[:span, :] += value_term
                dk_sum[:span, :] += key_term
            parts.append(nn(flipped[HEAD_DIM * head : HEAD_DIM * (head + 1), :span], grad_scores))
        dq = jnp.concatenate(parts, axis=0).T * (HEAD_DIM**-0.5)
        dq_ref[start:span, :] = dq.astype(BF16)
    dk_ref[...] = dk_sum[...].astype(BF16)
    dv_ref[...] = dv_sum[...].astype(BF16)


def attend_back(queries, keys, values, grads, sums, first, count):
    rows = queries.shape[0]
    block = pl.BlockSpec((rows, 128), lambda p: (0, p + first))
    out = pl.BlockSpec((rows, 128), lambda p: (0, p))
    return pl.pallas_call(
        attend_back_kernel,
        grid=(count,),
        in_specs=[block] * 4 + [pl.BlockSpec((1, 2, rows), lambda p: (p + first, 0, 0))],
        out_specs=[out] * 3,
        out_shape=[jax.ShapeDtypeStruct((rows, 128 * count), BF16)] * 3,
        scratch_shapes=[pltpu.VMEM((rows, 128), jnp.float32)] * 2,
        compiler_params=params(),
        cost_estimate=pl.CostEstimate(
            flops=48 * rows * rows * 128 * count,
            bytes_accessed=14 * rows * 128 * count,
            transcendentals=rows * rows * 2 * count,
        ),
        name="self_attend_back",
    )(queries, keys, values, grads, sums)


def gelu_both(values):
    phi = 0.5 + 0.5 * lax.erf(values * (0.5**0.5))
    density = jnp.exp(-0.5 * values * values) * ((2.0 * math.pi) ** -0.5)
    return values * phi, phi + values * density


def mlp_kernel(
    x_ref, h_ref, g_ref, gain_ref, up_ref, ub_ref, down_ref, db_ref,
    out_ref, dx_ref, dup_ref, dub_ref, ddown_ref, dgain_ref, dbias_ref, gsum_ref,
    out_sum, dh_sum, h_flip, act, grad_act,
):
    step, steps = pl.program_id(0), pl.num_programs(0)
    rows = h_ref.shape[0]

    @pl.when(step == 0)
    def _():
        h_flip[...] = h_ref[...].T
        out_sum[...] = x_ref[...] + db_ref[...]
        dh_sum[...] = jnp.zeros_like(dh_sum)

    up = square(up_ref)
    down = square(down_ref)
    bias_sum = jnp.zeros_like(dub_ref)
    for start in range(0, rows, TILE):
        at = slice(start, start + TILE)
        hidden, slope = gelu_both(nn(h_ref[at, :], up) + ub_ref[...])
        act[at, :] = hidden.astype(BF16)
        grad_pre = (nt(g_ref[at, :], down) * slope).astype(BF16)
        grad_act[at, :] = grad_pre
        bias_sum += column_sum(grad_pre.astype(jnp.float32))
        out_sum[at, :] += nn(act[at, :], down)
        dh_sum[at, :] += nt(grad_pre, up)
    dub_ref[...] = bias_sum
    dup_ref[...] = nn(h_flip[...], grad_act[...]).astype(BF16)
    ddown_ref[...] = tn(act[...], g_ref[...]).astype(BF16)

    @pl.when(step == steps - 1)
    def _():
        gain_sum = jnp.zeros_like(dgain_ref)
        grad_sum = jnp.zeros_like(dbias_ref)
        tail_sum = jnp.zeros_like(gsum_ref)
        for start in range(0, rows, TILE):
            at = slice(start, start + TILE)
            out_ref[at, :] = out_sum[at, :].astype(BF16)
            standard, rate = standardize(x_ref[at, :])
            grad = dh_sum[at, :]
            tail = g_ref[at, :].astype(jnp.float32)
            dx_ref[at, :] = tail + norm_back(standard, rate, gain_ref[...], grad)
            gain_sum += column_sum(grad * standard)
            grad_sum += column_sum(grad)
            tail_sum += column_sum(tail)
        dgain_ref[...] = gain_sum
        dbias_ref[...] = grad_sum
        gsum_ref[...] = tail_sum


def mlp(x, h, g, gain, up, up_bias, down, down_bias, chunk):
    rows, width = x.shape
    hidden = up_bias.shape[1]
    f32 = jnp.float32
    row = (1, width)
    return pl.pallas_call(
        mlp_kernel,
        grid=(hidden // chunk,),
        in_specs=[
            whole_block(x.shape), whole_block(h.shape), whole_block(g.shape), whole_block(row),
            up[1], pl.BlockSpec((1, chunk), lambda c: (0, c)), down[1], whole_block(row),
        ],
        out_specs=[
            whole_block(x.shape), whole_block(x.shape),
            pl.BlockSpec((width, chunk), lambda c: (0, c)),
            pl.BlockSpec((1, chunk), lambda c: (0, c)),
            pl.BlockSpec((chunk, width), lambda c: (c, 0)),
            whole_block(row), whole_block(row), whole_block(row),
        ],
        out_shape=[
            jax.ShapeDtypeStruct(x.shape, BF16), jax.ShapeDtypeStruct(x.shape, f32),
            jax.ShapeDtypeStruct((width, hidden), BF16),
            jax.ShapeDtypeStruct((1, hidden), f32),
            jax.ShapeDtypeStruct((hidden, width), BF16),
            jax.ShapeDtypeStruct(row, f32), jax.ShapeDtypeStruct(row, f32), jax.ShapeDtypeStruct(row, f32),
        ],
        scratch_shapes=[
            pltpu.VMEM(x.shape, f32), pltpu.VMEM(x.shape, f32), pltpu.VMEM((width, rows), BF16),
            pltpu.VMEM((rows, chunk), BF16), pltpu.VMEM((rows, chunk), BF16),
        ],
        compiler_params=params(),
        cost_estimate=pl.CostEstimate(
            flops=12 * rows * width * hidden,
            bytes_accessed=8 * width * hidden + 14 * rows * width,
            transcendentals=2 * rows * hidden,
        ),
        name="mlp_both_ways",
    )(x, h, g, gain, up[0], up_bias, down[0], down_bias)


def caption_probs(keys, own_queries, mask):
    scores = jnp.where(mask != 0, nt(keys, own_queries), NEGATIVE)
    powers = jnp.exp(scores - jnp.max(scores, axis=0, keepdims=True))
    return powers * (1.0 / jnp.sum(powers, axis=0, keepdims=True))


def middle_kernel(
    x_ref, a_ref, text_ref, mask_ref, gain2_ref, bias2_ref, gain3_ref, bias3_ref,
    wo_ref, cq_ref, ck_ref, cv_ref, co_ref,
    x1_ref, h2_ref, q2_ref, a2_ref, x2_ref, h3_ref, k2_ref, v2_ref,
):
    @pl.when(pl.program_id(0) == 0)
    def _():
        k2_ref[...] = nn(text_ref[...], square(ck_ref)).astype(BF16)
        v2_ref[...] = nn(text_ref[...], square(cv_ref)).astype(BF16)

    after_self = x_ref[...].astype(jnp.float32) + nn(a_ref[...], square(wo_ref))
    x1_ref[...] = after_self
    standard, _ = standardize(after_self)
    normed = (standard * gain2_ref[...] + bias2_ref[...]).astype(BF16)
    h2_ref[...] = normed
    q2_ref[...] = nn(normed, square(cq_ref)).astype(BF16)
    mask = mask_ref[...]
    for pair in range(q2_ref.shape[1] // 128):
        at = slice(128 * pair, 128 * (pair + 1))
        queries = q2_ref[:, at] * (HEAD_DIM**-0.5)
        keys = k2_ref[:, at]
        flipped = v2_ref[:, at].T
        mixed = []
        for head in range(2):
            probs = caption_probs(keys, head_lanes(queries, head), mask).astype(BF16)
            mixed.append(nn(flipped[HEAD_DIM * head : HEAD_DIM * (head + 1)], probs))
        a2_ref[:, at] = jnp.concatenate(mixed, axis=0).T.astype(BF16)
    after_cross = after_self + nn(a2_ref[...], square(co_ref))
    x2_ref[...] = after_cross
    standard, _ = standardize(after_cross)
    h3_ref[...] = (standard * gain3_ref[...] + bias3_ref[...]).astype(BF16)


def middle(tokens, mixed, text, mask, vectors, weights):
    rows, width = tokens.shape
    slots = text.shape[0]
    tile = pl.BlockSpec((TILE, width), lambda i: (i, 0))
    arrays, specs = zip(*weights)
    f32 = jnp.float32
    like = lambda dtype: jax.ShapeDtypeStruct(tokens.shape, dtype)
    return pl.pallas_call(
        middle_kernel,
        grid=(rows // TILE,),
        in_specs=[
            tile, tile, whole_block(text.shape), whole_block(mask.shape),
            *[whole_block(v.shape) for v in vectors], *specs,
        ],
        out_specs=[tile] * 6 + [whole_block(text.shape)] * 2,
        out_shape=[like(f32), like(BF16), like(BF16), like(BF16), like(f32), like(BF16)]
        + [jax.ShapeDtypeStruct(text.shape, BF16)] * 2,
        compiler_params=params(),
        cost_estimate=pl.CostEstimate(
            flops=6 * rows * width * width + 16 * rows * slots * width,
            bytes_accessed=28 * rows * width,
            transcendentals=16 * rows * slots,
        ),
        name="output_and_cross",
    )(tokens, mixed, text, mask, *vectors, *arrays)


def middle_back_kernel(
    dx2_ref, x1_ref, a1_ref, h2_ref, q2_ref, a2_ref, k2_ref, v2_ref, text_ref, mask_ref, gain2_ref,
    wo_ref, cq_ref, ck_ref, cv_ref, co_ref,
    dx1_ref, da1_ref, dwo_ref, dcq_ref, dck_ref, dcv_ref, dco_ref, dtext_ref, dgain_ref, dbias_ref,
    wo_sum, cq_sum, co_sum, dk_sum, dv_sum, dq2,
):
    step, steps = pl.program_id(0), pl.num_programs(0)

    @pl.when(step == 0)
    def _():
        for ref in (wo_sum, cq_sum, co_sum, dk_sum, dv_sum, dgain_ref, dbias_ref):
            ref[...] = jnp.zeros_like(ref)

    grad_out = dx2_ref[...].astype(BF16)
    co_sum[...] += tn(a2_ref[...], grad_out)
    grad_mixed = nt(grad_out, square(co_ref)).astype(BF16)
    mask = mask_ref[...]
    for pair in range(q2_ref.shape[1] // 128):
        at = slice(128 * pair, 128 * (pair + 1))
        queries = q2_ref[:, at] * (HEAD_DIM**-0.5)
        keys = k2_ref[:, at]
        flipped = keys.T
        values = v2_ref[:, at]
        grads = grad_mixed[:, at]
        parts = []
        for head in range(2):
            own_queries = head_lanes(queries, head)
            own_grads = head_lanes(grads, head)
            probs = caption_probs(keys, own_queries, mask)
            grad_probs = nt(values, own_grads)
            inner = jnp.sum(probs * grad_probs, axis=0, keepdims=True)
            grad_scores = (probs * (grad_probs - inner)).astype(BF16)
            dv_sum[:, at] += nn(probs.astype(BF16), own_grads)
            dk_sum[:, at] += nn(grad_scores, own_queries)
            parts.append(nn(flipped[HEAD_DIM * head : HEAD_DIM * (head + 1)], grad_scores))
        dq2[:, at] = (jnp.concatenate(parts, axis=0).T * (HEAD_DIM**-0.5)).astype(BF16)
    cq_sum[...] += tn(h2_ref[...], dq2[...])
    grad_normed = nt(dq2[...], square(cq_ref))
    standard, rate = standardize(x1_ref[...])
    grad_after = dx2_ref[...] + norm_back(standard, rate, gain2_ref[...], grad_normed)
    dgain_ref[...] += column_sum(grad_normed * standard)
    dbias_ref[...] += column_sum(grad_normed)
    dx1_ref[...] = grad_after
    grad_self = grad_after.astype(BF16)
    wo_sum[...] += tn(a1_ref[...], grad_self)
    da1_ref[...] = nt(grad_self, square(wo_ref)).astype(BF16)

    @pl.when(step == steps - 1)
    def _():
        dwo_ref[...] = wo_sum[...].astype(BF16)
        dcq_ref[...] = cq_sum[...].astype(BF16)
        dco_ref[...] = co_sum[...].astype(BF16)
        grad_keys = dk_sum[...].astype(BF16)
        grad_values = dv_sum[...].astype(BF16)
        dck_ref[...] = tn(text_ref[...], grad_keys).astype(BF16)
        dcv_ref[...] = tn(text_ref[...], grad_values).astype(BF16)
        dtext_ref[...] = nt(grad_keys, square(ck_ref)) + nt(grad_values, square(cv_ref))


def middle_back(dx2, x1, a1, h2, q2, a2, k2, v2, text, mask, gain, weights):
    rows, width = x1.shape
    slots = text.shape[0]
    tile = pl.BlockSpec((TILE, width), lambda i: (i, 0))
    arrays, specs = zip(*weights)
    f32 = jnp.float32
    matrix = (width, width)
    return pl.pallas_call(
        middle_back_kernel,
        grid=(rows // TILE,),
        in_specs=[tile] * 6
        + [whole_block(v.shape) for v in (k2, v2, text, mask, gain)]
        + list(specs),
        out_specs=[tile] * 2
        + [whole_block(matrix)] * 5
        + [whole_block(text.shape)]
        + [whole_block(gain.shape)] * 2,
        out_shape=[jax.ShapeDtypeStruct(x1.shape, f32), jax.ShapeDtypeStruct(x1.shape, BF16)]
        + [jax.ShapeDtypeStruct(matrix, BF16)] * 5
        + [jax.ShapeDtypeStruct(text.shape, f32)]
        + [jax.ShapeDtypeStruct(gain.shape, f32)] * 2,
        scratch_shapes=[pltpu.VMEM(matrix, f32)] * 3
        + [pltpu.VMEM(text.shape, f32)] * 2
        + [pltpu.VMEM((TILE, width), BF16)],
        compiler_params=params(),
        cost_estimate=pl.CostEstimate(
            flops=12 * rows * width * width + 8 * slots * width * width,
            bytes_accessed=40 * rows * width,
            transcendentals=16 * rows * slots,
        ),
        name="cross_back",
    )(dx2, x1, a1, h2, q2, a2, k2, v2, text, mask, gain, *arrays)


def weight_grads_kernel(h_ref, dq_ref, dk_ref, dv_ref, q_ref, k_ref, v_ref):
    normed = h_ref[...]
    q_ref[...] = tn(normed, dq_ref[...]).astype(BF16)
    k_ref[...] = tn(normed, dk_ref[...]).astype(BF16)
    v_ref[...] = tn(normed, dv_ref[...]).astype(BF16)


def weight_grads(normed, grads):
    rows, width = normed.shape
    columns = grads[0].shape[1]
    out = pl.BlockSpec((TILE, columns), lambda i: (i, 0))
    return pl.pallas_call(
        weight_grads_kernel,
        grid=(width // TILE,),
        in_specs=[pl.BlockSpec((rows, TILE), lambda i: (0, i))]
        + [whole_block(g.shape) for g in grads],
        out_specs=[out] * 3,
        out_shape=[jax.ShapeDtypeStruct((width, columns), BF16)] * 3,
        compiler_params=params(),
        cost_estimate=pl.CostEstimate(
            flops=6 * rows * width * columns, bytes_accessed=14 * rows * width, transcendentals=0
        ),
        name="self_weight_grads",
    )(normed, *grads)


def first_back_kernel(x_ref, dx1_ref, gain_ref, wq_ref, wk_ref, wv_ref, *rest):
    grads, (dx_ref, dgain_ref, dbias_ref) = rest[:-3], rest[-3:]

    @pl.when(pl.program_id(0) == 0)
    def _():
        dgain_ref[...] = jnp.zeros_like(dgain_ref)
        dbias_ref[...] = jnp.zeros_like(dbias_ref)

    grad_normed, at = None, 0
    for first in range(0, len(grads), 3):
        columns = grads[first].shape[1]
        for grad, weight in zip(grads[first : first + 3], (wq_ref, wk_ref, wv_ref)):
            term = nt(grad[...], square(weight)[:, at : at + columns])
            grad_normed = term if grad_normed is None else grad_normed + term
        at += columns
    standard, rate = standardize(x_ref[...].astype(jnp.float32))
    dx_ref[...] = dx1_ref[...] + norm_back(standard, rate, gain_ref[...], grad_normed)
    dgain_ref[...] += column_sum(grad_normed * standard)
    dbias_ref[...] += column_sum(grad_normed)


def first_back(tokens, dx1, gain, weights, grads):
    rows, width = tokens.shape
    tile = lambda columns: pl.BlockSpec((TILE, columns), lambda i: (i, 0))
    arrays, specs = zip(*weights)
    f32 = jnp.float32
    return pl.pallas_call(
        first_back_kernel,
        grid=(rows // TILE,),
        in_specs=[tile(width)] * 2
        + [whole_block(gain.shape)]
        + list(specs)
        + [tile(g.shape[1]) for g in grads],
        out_specs=[tile(width)] + [whole_block(gain.shape)] * 2,
        out_shape=[jax.ShapeDtypeStruct(tokens.shape, f32)]
        + [jax.ShapeDtypeStruct(gain.shape, f32)] * 2,
        compiler_params=params(),
        cost_estimate=pl.CostEstimate(
            flops=6 * rows * width * width, bytes_accessed=22 * rows * width, transcendentals=0
        ),
        name="self_norm_back",
    )(tokens, dx1, gain, *arrays, *grads)


def cube_dims():
    wide = [("wide", k) for k in reversed(range(axis_bits("wide")))]
    return wide + [("narrow", k) for k in reversed(range(axis_bits("narrow")))]


def my_bits(dims):
    return [(lax.axis_index(axis) >> bit) & 1 for axis, bit in dims]


def partner(axis, bit):
    return {axis: lax.axis_index(axis) ^ (1 << bit)}


def greet_partners(dims):
    barrier = pltpu.get_barrier_semaphore()
    for axis, bit in dims:
        pl.semaphore_signal(
            barrier, inc=1, device_id=partner(axis, bit), device_id_type=pl.DeviceIdType.MESH
        )
    pl.semaphore_wait(barrier, len(dims))


def skewed(plan, stages):
    slots = [(plan[p][2] + s, -s, p) for p in range(len(plan)) for s in range(stages)]
    return [(p, -minus) for _, minus, p in sorted(slots)]


def gather_kernel(dims, plan, src_ref, out_ref, send_sems, recv_sems, own_sem):
    mine = my_bits(dims)
    greet_partners(dims)
    own = pltpu.make_async_copy(src_ref, out_ref.at[tuple(mine)], own_sem)
    own.start()
    copies = {}
    for part, stage in skewed(plan, len(dims)):
        rows, order, _ = plan[part]
        if stage:
            copies[part, stage - 1].wait_recv()
        if stage == 1 and part == 0:
            own.wait()
        held = order[:stage]
        at = tuple(slice(None) if d in held else b for d, b in zip(dims, mine)) + (rows,)
        copy = pltpu.make_async_remote_copy(
            src_ref=out_ref.at[at] if stage else src_ref.at[rows],
            dst_ref=out_ref.at[at],
            send_sem=send_sems.at[part, stage],
            recv_sem=recv_sems.at[part, stage],
            device_id=partner(*order[stage]),
            device_id_type=pl.DeviceIdType.MESH,
        )
        copy.start()
        copies[part, stage] = copy
    for (part, stage), copy in copies.items():
        if stage == len(dims) - 1:
            copy.wait_recv()
        copy.wait_send()


SHARES = (2, 2, 1)


def split_rows(rows, shares, step=16):
    ends = [sum(shares[: k + 1]) for k in range(len(shares))]
    cuts = [0] + [(rows * e + ends[-1] * step // 2) // (ends[-1] * step) * step for e in ends]
    cuts[-1] = rows
    return [slice(a, b) for a, b in zip(cuts[:-1], cuts[1:])]


def gather_all(packed, collective_id, rounds):
    dims = cube_dims()
    rows, width = packed.shape
    shares = SHARES * rounds
    pieces = split_rows(rows, shares)
    plan = [(piece, halving_order(k % 3)[::-1], k // 3) for k, piece in enumerate(pieces)]
    out = pl.pallas_call(
        functools.partial(gather_kernel, dims, plan),
        in_specs=[pl.BlockSpec(memory_space=pl.ANY)],
        out_specs=pl.BlockSpec(memory_space=pl.ANY),
        out_shape=jax.ShapeDtypeStruct((2,) * len(dims) + packed.shape, packed.dtype),
        scratch_shapes=[
            pltpu.SemaphoreType.DMA((len(plan), len(dims))),
            pltpu.SemaphoreType.DMA((len(plan), len(dims))),
            pltpu.SemaphoreType.DMA,
        ],
        compiler_params=pltpu.CompilerParams(collective_id=collective_id, has_side_effects=True),
        name="gather_weights",
    )(packed)
    return out.reshape((-1,) + packed.shape)


def drop(items, index):
    return items[:index] + items[index + 1 :]


class Halving:
    def __init__(self, dims, orders, terms, kept, landed, outs, send_sems, recv_sems, kept_sems):
        self.dims, self.orders, self.terms = dims, orders, terms
        self.kept, self.landed, self.outs = kept, landed, outs
        self.send_sems, self.recv_sems, self.kept_sems = send_sems, recv_sems, kept_sems
        self.mine = dict(zip(dims, my_bits(dims)))

    def half(self, term, stage, other):
        order = self.orders[term]
        left = [d for d in self.dims if d not in order[:stage]]
        bit = self.mine[order[stage]]
        return tuple((1 - bit if other else bit) if d == order[stage] else slice(None) for d in left)

    def send(self, term, stage):
        source = self.terms[term] if stage == 0 else self.landed[term][stage - 1]
        return pltpu.make_async_remote_copy(
            src_ref=source.at[self.half(term, stage, True)],
            dst_ref=self.landed[term][stage],
            send_sem=self.send_sems.at[term, stage],
            recv_sem=self.recv_sems.at[term, stage],
            device_id=partner(*self.orders[term][stage]),
            device_id_type=pl.DeviceIdType.MESH,
        )

    def keep(self, term):
        source = self.terms[term].at[self.half(term, 0, False)]
        return pltpu.make_async_copy(source, self.kept[term], self.kept_sems.at[term])

    def start(self, stage, terms=None):
        for term in range(len(self.terms)) if terms is None else terms:
            self.send(term, stage).start()
            if stage == 0:
                self.keep(term).start()

    def finish(self, stage, terms=None):
        last = stage == len(self.dims) - 1
        for term in range(len(self.terms)) if terms is None else terms:
            self.send(term, stage).wait_recv()
            if stage == 0:
                self.keep(term).wait()
            landed = self.landed[term][stage]
            other = self.kept[term] if stage == 0 else self.landed[term][stage - 1]
            chosen = (slice(None),) * (len(self.dims) - 1) if stage == 0 else self.half(term, stage, False)
            depth = len(self.dims) - 1 - stage
            if last:
                total = landed[...].astype(jnp.float32) + other[chosen].astype(jnp.float32)
                self.outs[term][...] = total
                continue

            def add(block, carry, landed=landed, other=other, chosen=chosen, depth=depth):
                at = [(block >> k) & 1 for k in reversed(range(depth))]
                rest = iter(at)
                there = tuple(next(rest) if isinstance(c, slice) else c for c in chosen)
                total = landed[tuple(at)].astype(jnp.float32) + other[there].astype(jnp.float32)
                landed[tuple(at)] = total.astype(landed.dtype)
                return carry

            lax.fori_loop(0, 1 << depth, add, 0)

    def settle(self):
        for term in range(len(self.terms)):
            for stage in range(len(self.dims)):
                self.send(term, stage).wait_send()


def halving_scratch(dims, shapes, dtypes):
    count = len(dims)
    like = list(zip(shapes, dtypes))
    kept = [pltpu.VMEM((2,) * (count - 1) + s, d) for s, d in like]
    landed = [pltpu.VMEM((2,) * (count - 1 - k) + s, d) for s, d in like for k in range(count)]
    sems = [
        pltpu.SemaphoreType.DMA((len(shapes), count)),
        pltpu.SemaphoreType.DMA((len(shapes), count)),
        pltpu.SemaphoreType.DMA((len(shapes),)),
    ]
    return kept + landed + sems


def halving_of(dims, orders, terms, outs, scratch):
    count, stages = len(terms), len(dims)
    kept, rest = scratch[:count], scratch[count:]
    landed = [rest[stages * t : stages * (t + 1)] for t in range(count)]
    return Halving(dims, orders, terms, kept, landed, outs, *rest[stages * count :])


def scatter_kernel(dims, orders, *refs):
    count = len(orders)
    terms, outs, scratch = refs[:count], refs[count : 2 * count], refs[2 * count :]
    halving = halving_of(dims, orders, terms, outs, scratch)
    greet_partners(dims)
    for stage in range(len(dims)):
        halving.start(stage)
        halving.finish(stage)
    halving.settle()


def block_shape(term, dims):
    return (term.size // term.shape[-1] >> len(dims), term.shape[-1])


def scatter_all(terms, kinds, collective_id):
    dims = cube_dims()
    shapes = [block_shape(t, dims) for t in terms]
    cubes = [t.reshape((2,) * len(dims) + s) for t, s in zip(terms, shapes)]
    return pl.pallas_call(
        functools.partial(scatter_kernel, dims, [halving_order(k) for k in kinds]),
        in_specs=[pl.BlockSpec(memory_space=pl.ANY)] * len(cubes),
        out_specs=[pl.BlockSpec(memory_space=pltpu.VMEM)] * len(cubes),
        out_shape=[jax.ShapeDtypeStruct(s, jnp.float32) for s in shapes],
        scratch_shapes=halving_scratch(dims, shapes, [t.dtype for t in terms]),
        compiler_params=pltpu.CompilerParams(
            collective_id=collective_id, has_side_effects=True, vmem_limit_bytes=VMEM_LIMIT
        ),
        name="scatter_gradients",
    )(*cubes)


def on_device(
    image_tokens, text_states, text_segments, image_segment, out_grad,
    norm1_gain, norm1_bias, self_query, self_key, self_value, self_output,
    norm2_gain, norm2_bias, cross_query, cross_key, cross_value, cross_output,
    norm3_gain, norm3_bias, mlp_in, mlp_in_bias, mlp_out, mlp_out_bias,
):
    tokens = image_tokens[0]
    rows, width = tokens.shape
    hidden = mlp_in.shape[1]
    chunk = 512
    vectors = (
        norm1_gain, norm1_bias, norm2_gain, norm2_bias,
        norm3_gain, norm3_bias, mlp_in_bias, mlp_out_bias,
    )
    sizes = [v.shape[0] for v in vectors]
    shard = self_query.shape[0]
    owners = width // shard
    parts = hidden // width
    first = gather_all(
        jnp.concatenate([self_query, self_key, self_value, pack_vectors(vectors)], axis=0), 1, 2
    )
    second = gather_rows(
        jnp.concatenate(
            [mlp_out]
            + [mlp_in[:, width * k : width * (k + 1)] for k in range(parts)]
            + [self_output, cross_query, cross_key, cross_value, cross_output],
            axis=0,
        )
    )

    def matrix(source, index):
        if shard % 16 == 0:
            spec = pl.BlockSpec(
                (owners, shard, width), lambda *_: (0, index, 0), pipeline_mode=pl.Buffered(1)
            )
            return source, spec
        taken = source[:, shard * index : shard * (index + 1)].reshape(1, width, width)
        return taken, whole_block(taken.shape)

    weights_one = [matrix(first, k) for k in range(3)]
    gain_one, bias_one, gain_two, bias_two, gain_three, bias_three, up_bias, down_bias = (
        take_vectors(first[:, 3 * shard :], sizes)
    )
    weights_two = [matrix(second, 2 * parts + k) for k in range(5)]
    down_shard = mlp_out.shape[0]
    if shard % 16 == 0:
        per = width // chunk
        up = (
            second,
            pl.BlockSpec((owners, shard, chunk), lambda c: (0, parts + c // per, c % per)),
        )
        down = (
            second,
            pl.BlockSpec((chunk // down_shard, down_shard, width), lambda c: (c, 0, 0)),
        )
    else:
        taken = [
            second[:, shard * (parts + k) : shard * (parts + k + 1)].reshape(1, width, width)
            for k in range(parts)
        ]
        up = (
            jnp.concatenate(taken, axis=2),
            pl.BlockSpec((1, width, chunk), lambda c: (0, 0, c)),
        )
        down = (
            second[:, :down_shard].reshape(1, hidden, width),
            pl.BlockSpec((1, chunk, width), lambda c: (0, c, 0)),
        )

    own_text = text_states[0]
    slots = own_text.shape[0]
    text_full = jnp.concatenate(
        [own_text] + [swap_narrow(own_text, k) for k in text_partners()], axis=0
    )
    narrow_at = lax.axis_index("narrow")
    segments = jnp.concatenate(
        [
            lax.dynamic_slice_in_dim(text_segments[0], (narrow_at ^ k) * slots, slots, 0)
            for k in range(lax.axis_size("narrow"))
        ]
    )
    mask = (segments == image_segment[0, 0]).astype(jnp.int32).reshape(-1, 1)

    normed_one, queries, keys, values = project(tokens, gain_one, bias_one, weights_one)
    mixed_self, sums_self = attend(queries, keys, values)
    x1, h2, q2, a2, x2, h3, k2, v2 = middle(
        tokens, mixed_self, text_full, mask, (gain_two, bias_two, gain_three, bias_three), weights_two
    )
    (
        block_out, dx2, grad_up, grad_up_bias, grad_down,
        grad_gain_three, grad_bias_three, grad_down_bias,
    ) = mlp(x2, h3, out_grad[0], gain_three, up, up_bias, down, down_bias, chunk)
    (
        dx1, grad_mixed, grad_self_out, grad_cross_query, grad_cross_key, grad_cross_value,
        grad_cross_out, text_term, grad_gain_two, grad_bias_two,
    ) = middle_back(
        dx2, x1, mixed_self, h2, q2, a2, k2, v2, text_full, mask, gain_two, weights_two
    )
    text_grad = text_term[:slots]
    for k in text_partners():
        text_grad = text_grad + swap_narrow(text_term[k * slots : (k + 1) * slots], k)
    pairs = width // 128
    half = pairs // 2
    self_terms, self_grads = [], []
    for start in (0, half):
        terms = attend_back(queries, keys, values, grad_mixed, sums_self, start, half)
        self_terms.extend(terms)
        self_grads.extend(weight_grads(normed_one, terms))
    image_grad, grad_gain_one, grad_bias_one = first_back(
        tokens, dx1, gain_one, weights_one, self_terms
    )
    vector_terms = (
        grad_gain_one, grad_bias_one, grad_gain_two, grad_bias_two,
        grad_gain_three, grad_bias_three, grad_up_bias, grad_down_bias,
    )
    stacked = jnp.concatenate([v.reshape(owners, -1) for v in vector_terms], axis=1)
    stacked = jnp.pad(stacked, ((0, 0), (0, -stacked.shape[1] % 1024))).reshape(owners, -1, 128)
    (
        grad_down, grad_up, grad_cross_out, grad_cross_query, grad_self_out, grad_cross_key,
        grad_cross_value, *self_sums, summed,
    ) = scatter_all(
        [
            grad_down, grad_up, grad_cross_out, grad_cross_query, grad_self_out, grad_cross_key,
            grad_cross_value, *self_grads, stacked,
        ],
        [0, 1, 2, 2, 2, 0, 1, 2, 2, 0, 2, 2, 1, 0],
        2,
    )
    grad_self_query, grad_self_key, grad_self_value = (
        jnp.concatenate([self_sums[k], self_sums[k + 3]], axis=1) for k in range(3)
    )
    summed = summed.reshape(-1)
    vector_grads, at = [], 0
    for size in sizes:
        vector_grads.append(summed[at : at + size])
        at += size
    return (
        block_out[None], image_grad[None], text_grad[None],
        vector_grads[0], vector_grads[1],
        grad_self_query, grad_self_key, grad_self_value, grad_self_out,
        vector_grads[2], vector_grads[3],
        grad_cross_query, grad_cross_key, grad_cross_value, grad_cross_out,
        vector_grads[4], vector_grads[5],
        grad_up, vector_grads[6], grad_down, vector_grads[7],
    )


def solution(mesh):
    placed = (
        P(("wide", "narrow"), None, None),
        P("wide", "narrow", None),
        P("wide", None),
        P("wide", "narrow"),
        P(("wide", "narrow"), None, None),
        P(("wide", "narrow")),
        P(("wide", "narrow")),
        P(("wide", "narrow"), None),
        P(("wide", "narrow"), None),
        P(("wide", "narrow"), None),
        P(("wide", "narrow"), None),
        P(("wide", "narrow")),
        P(("wide", "narrow")),
        P(("wide", "narrow"), None),
        P(("wide", "narrow"), None),
        P(("wide", "narrow"), None),
        P(("wide", "narrow"), None),
        P(("wide", "narrow")),
        P(("wide", "narrow")),
        P(("wide", "narrow"), None),
        P(("wide", "narrow")),
        P(("wide", "narrow"), None),
        P(("wide", "narrow")),
    )
    return jax.shard_map(
        on_device,
        mesh=mesh,
        in_specs=placed,
        out_specs=(
            P(("wide", "narrow"), None, None),
            P(("wide", "narrow"), None, None),
            P("wide", "narrow", None),
            P(("wide", "narrow")),
            P(("wide", "narrow")),
            P(("wide", "narrow"), None),
            P(("wide", "narrow"), None),
            P(("wide", "narrow"), None),
            P(("wide", "narrow"), None),
            P(("wide", "narrow")),
            P(("wide", "narrow")),
            P(("wide", "narrow"), None),
            P(("wide", "narrow"), None),
            P(("wide", "narrow"), None),
            P(("wide", "narrow"), None),
            P(("wide", "narrow")),
            P(("wide", "narrow")),
            P(("wide", "narrow"), None),
            P(("wide", "narrow")),
            P(("wide", "narrow"), None),
            P(("wide", "narrow")),
        ),
        check_vma=False,
    )
```

time: 1050 us -> 646 us (0.62)
  Pallas kernels: 0 us -> 530 us
  matrix products: 355 us -> 0 us
  local copies, waits for them, and re-layouts: 263 us -> 26.1 us
  waiting for transfers between devices: 227 us -> 44.3 us
  other arithmetic: 105 us -> 12.8 us
  starting transfers between devices: 63.9 us -> 8.14 us
    pallas_call x0 -> x12, Pallas kernels: none -> 530 us  [the longest x1 191 us: scatter_all(): pl.pallas_call(functools.partial(scatter_kernel, dims, [halving_order(k)...]
    dot_general x142 -> x0, matrix products: 355 us -> none  [the longest x10 99 us: matmul(): return jnp.dot(leading, trailing, preferred_element_type=jnp.float32)]
    ppermute x55 -> x0, waiting for transfers between devices: 127 us -> none  [swap_with(): return lax.ppermute(block, axis, [(i, i ^ 1 << bit) for i in range(count)])]
    dynamic_slice x128 -> x0, local copies, waits for them, and re-layouts: 90 us -> none  [the longest x112 77.6 us: head_slices(): lax.dynamic_slice_in_dim(source, column, pair_width, 1)]
    all_gather x2 -> x1, waiting for transfers between devices: 101 us -> 43.7 us  [gather_rows(): whole = lax.all_gather(packed, AXES, axis=0, tiled=True)]
    ppermute x55 -> x0, starting transfers between devices: 55.7 us -> none  [swap_with(): return lax.ppermute(block, axis, [(i, i ^ 1 << bit) for i in range(count)])]
    convert_element_type x60 -> x3, other arithmetic: 47.4 us -> 1.4 us  [the longest x2 0.76 us: take_vectors(): out.append(flat[:, at:at + size].reshape(1, -1).astype(jnp.float32))]
    unnamed x265 -> x75, local copies, waits for them, and re-layouts: 54.7 us -> 15 us
  transfers between devices with their start and end apart: 63 -> 7, of which waited for: 26 -> 2; matrix products, arithmetic and copies ran while one was open for 23% -> 2% of each run, Pallas kernels for 0% -> 20%
where the time goes in v2:
time: 646 us; the launch traced here: 637 us
  Pallas kernels  530 us (82%)
  waiting for transfers between devices  44.3 us (7%)
  local copies, waits for them, and re-layouts  26.1 us (4%)
  between operations  15.6 us (2%)
  other arithmetic  12.8 us (2%)
  starting transfers between devices  8.14 us (1%)
    pallas_call x1, Pallas kernels, scatter_all(): pl.pallas_call(functools.partial(scatter_kernel, dims, [halving_order(k)...  191 us
    pallas_call x1, Pallas kernels, gather_all(): pl.pallas_call(functools.partial(gather_kernel, dims, plan), in_specs=[pl...  79.4 us
    pallas_call x1, Pallas kernels, mlp(): pl.pallas_call(mlp_kernel, grid=(hidden // chunk,), in_specs=[whole_block...  67.9 us
    pallas_call x1, Pallas kernels, middle_back(): pl.pallas_call(middle_back_kernel, grid=(rows // TILE,), in_specs=[tile]...  48.5 us
    all_gather x1, waiting for transfers between devices, gather_rows(): whole = lax.all_gather(packed, AXES, axis=0, tiled=True)  43.7 us
    pallas_call x2, Pallas kernels, attend_back(): pl.pallas_call(attend_back_kernel, grid=(count,), in_specs=[block] * 4 +...  43.3 us
    pallas_call x1, Pallas kernels, attend(): pl.pallas_call(attend_kernel, grid=(pairs,), in_specs=[block] * 3, out_sp...  33.3 us
    pallas_call x1, Pallas kernels, middle(): pl.pallas_call(middle_kernel, grid=(rows // TILE,), in_specs=[tile, tile,...  26.6 us
  transfers between devices with their start and end apart: 7, of which 2 were waited for; matrix products, arithmetic and copies ran while one was open for 2% of the time, Pallas kernels for 20%

profile of v2, /device:TPU:0, one launch (start us, length us, event | category | flops | bytes accessed | tf_op | source)
XLA Modules:
  0.0 637.3 jit_solution(12805984583646676369)
XLA Ops:
  7.4 1.1 constant_dynamic-update-slice_fusion.5
  8.4 0.8 slice_dynamic-update-slice_fusion.3
  9.3 0.8 slice_dynamic-update-slice_fusion.2
  10.1 0.8 slice_dynamic-update-slice_fusion.1
  11.0 0.8 slice_dynamic-update-slice_fusion
  11.8 0.8 constant_dynamic-update-slice_fusion.4
  12.6 0.8 constant_dynamic-update-slice_fusion.3
  13.5 0.8 constant_dynamic-update-slice_fusion.2
  14.3 0.8 constant_dynamic-update-slice_fusion.1
  15.2 0.8 constant_dynamic-update-slice_fusion
  16.0 0.9 copy-done
  17.0 3.0 collective-permute-start
  20.0 1.5 collective-permute-start.1
  22.4 0.7 pad_maximum_fusion.1.src_ref
  23.1 79.4 %gather_weights.1 = bf16[2,2,2,2,2,112,1024]{6,5,4,3,2,1,0:T(8,128)(2,1)} custom-call(bf16[112,1024]{1,0:T(8,128)(2,1)} %pad_maximum_fusion.1.src_ref), custom_call_target="tpu_custom_call" | custom-call | tf_op jit(solution)/shard_map/gather_weights/pallas_call | solution.py:647
  102.5 1.3 slice.100
  103.8 0.6 copy.51
  104.5 0.7 reshape.333.gain_ref
  105.2 0.7 reshape.334.bias_ref
  105.9 0.7 slice_convert_fusion.1
  106.6 12.4 %self_project.1 = (bf16[1024,1024]{1,0:T(8,128)(2,1)}, bf16[1024,1024]{1,0:T(8,128)(2,1)}, bf16[1024,1024]{1,0:T(8,128)(2,1)}, bf16[1024,1024]{1,0:T(8,128)(2,1)}) custom-call(bf16[1024,1024]{1,0:T(8,128)(2,1)} %bitcast.60, f32[1,1024]{1,0:T(1,128)} %reshape.333.gain_ref, f32[1,1024]{1,0:T(1,128)} %reshape.334.bias_ref, bf16[32,112,1024]{2,1,0:T(8,128)(2,1)} %bitcast.54, ...), custom_call_target="tpu_custom_call" | custom-call | flops 6442450944 | bytes 16777216 | tf_op jit(solution)/shard_map/self_project/pallas_call | solution.py:130
  119.0 33.3 %self_attend.1 = (bf16[1024,1024]{1,0:T(8,128)(2,1)}, f32[8,2,1024]{2,1,0:T(2,128)}) custom-call(bf16[1024,1024]{1,0:T(8,128)(2,1)} %get-tuple-element.82.q_ref, bf16[1024,1024]{1,0:T(8,128)(2,1)} %get-tuple-element.83.k_ref, bf16[1024,1024]{1,0:T(8,128)(2,1)} %get-tuple-element.84.v_ref), custom_call_target="tpu_custom_call" | custom-call | flops 25769803776 | bytes 8388608 | tf_op jit(solution)/shard_map/self_attend/pallas_call | solution.py:172
  152.5 0.6 convert_element_type.58.mask_ref
  153.1 0.7 reshape.335.gain2_ref
  153.8 0.7 reshape.337.gain3_ref.gain_ref
  154.5 0.7 reshape.336.bias2_ref
  155.2 0.7 reshape.338.bias3_ref
  155.8 0.7 reshape.340.db_ref
  156.5 0.7 pad_maximum_fusion.text_ref
  157.2 43.7 %all-gather.2.cloned.1.call-done = bf16[13312,1024]{1,0:T(8,128)(2,1)} async-done(((bf16[416,1024]{1,0:T(8,128)(2,1)}), bf16[13312,1024]{1,0:T(8,128)(2,1)}) %all-gather.2.cloned.1.call-update) | async-done | bytes 27262992 | tf_op jit(solution)/shard_map/all_gather | solution.py:38
  200.9 26.6 %output_and_cross.1 = (f32[1024,1024]{1,0:T(8,128)}, bf16[1024,1024]{1,0:T(8,128)(2,1)}, bf16[1024,1024]{1,0:T(8,128)(2,1)}, bf16[1024,1024]{1,0:T(8,128)(2,1)},...) custom-call(bf16[1024,1024]{1,0:T(8,128)(2,1)} %bitcast.61, ...), custom_call_target="tpu_custom_call" | custom-call | flops 8589934592 | bytes 29360128 | tf_op jit(solution)/shard_map/output_and_cross/pallas_call | solution.py:391
  227.5 67.9 %mlp_both_ways.1 = (bf16[1024,1024]{1,0:T(8,128)(2,1)}, f32[1024,1024]{1,0:T(8,128)}, bf16[1024,4096]{1,0:T(8,128)(2,1)}, f32[1,4096]{1,0:T(1,128)}, bf16[4096,1...) custom-call(f32[1024,1024]{1,0:T(8,128)} %get-tuple-element.86.x_ref, ...), custom_call_target="tpu_custom_call" | custom-call | flops 51539607552 | bytes 48234496 | tf_op jit(solution)/shard_map/mlp_both_ways/pallas_call | solution.py:310
  295.4 48.5 %cross_back.1 = (f32[1024,1024]{1,0:T(8,128)}, bf16[1024,1024]{1,0:T(8,128)(2,1)}, bf16[1024,1024]{1,0:T(8,128)(2,1)}, bf16[1024,1024]{1,0:T(8,128)(2,1)}, bf16[...) custom-call(f32[1024,1024]{1,0:T(8,128)} %get-tuple-element.89.dx2_r, ...), custom_call_target="tpu_custom_call" | custom-call | flops 13958643712 | bytes 41943040 | tf_op jit(solution)/shard_map/cross_back/pallas_call | solution.py:477
  343.9 21.8 %self_attend_back.3 = (bf16[1024,512]{1,0:T(8,128)(2,1)}, bf16[1024,512]{1,0:T(8,128)(2,1)}, bf16[1024,512]{1,0:T(8,128)(2,1)}) custom-call(bf16[1024,1024]{1,0:T(8,128)(2,1)} %get-tuple-element.82.q_ref, bf16[1024,1024]{1,0:T(8,128)(2,1)} %get-tuple-element.83.k_ref, bf16[1024,1024]{1,0:T(8,128)(2,1)} %get-tuple-element.84.v_ref, ...), custom_call_target="tpu_custom_call" | custom-call | flops 25769803776 | bytes 7340032 | tf_op jit(solution)/shard_map/self_attend_back/pallas_call | solution.py:232
  365.7 21.5 %self_attend_back.2 = (bf16[1024,512]{1,0:T(8,128)(2,1)}, bf16[1024,512]{1,0:T(8,128)(2,1)}, bf16[1024,512]{1,0:T(8,128)(2,1)}) custom-call(bf16[1024,1024]{1,0:T(8,128)(2,1)} %get-tuple-element.82.q_ref, bf16[1024,1024]{1,0:T(8,128)(2,1)} %get-tuple-element.83.k_ref, bf16[1024,1024]{1,0:T(8,128)(2,1)} %get-tuple-element.84.v_ref, ...), custom_call_target="tpu_custom_call" | custom-call | flops 25769803776 | bytes 7340032 | tf_op jit(solution)/shard_map/self_attend_back/pallas_call | solution.py:232
  387.2 7.0 %self_weight_grads.3 = (bf16[1024,512]{1,0:T(8,128)(2,1)}, bf16[1024,512]{1,0:T(8,128)(2,1)}, bf16[1024,512]{1,0:T(8,128)(2,1)}) custom-call(bf16[1024,1024]{1,0:T(8,128)(2,1)} %get-tuple-element.114.h_ref, bf16[1024,512]{1,0:T(8,128)(2,1)} %get-tuple-element.102.rest_3_.dq_ref, bf16[1024,512]{1,0:T(8,128)(2,1)} %get-tuple-element.103.rest_4_.dk_ref, ...), custom_call_target="tpu_custom_call" | custom-call | flops 3221225472 | bytes 14680064 | tf_op jit(solution)/shard_map/self_weight_grads/pallas_call | solution.py:515
  394.2 7.0 %self_weight_grads.2 = (bf16[1024,512]{1,0:T(8,128)(2,1)}, bf16[1024,512]{1,0:T(8,128)(2,1)}, bf16[1024,512]{1,0:T(8,128)(2,1)}) custom-call(bf16[1024,1024]{1,0:T(8,128)(2,1)} %get-tuple-element.114.h_ref, bf16[1024,512]{1,0:T(8,128)(2,1)} %get-tuple-element.99.rest_0_.dq_ref, bf16[1024,512]{1,0:T(8,128)(2,1)} %get-tuple-element.100.rest_1_.dk_ref, ...), custom_call_target="tpu_custom_call" | custom-call | flops 3221225472 | bytes 14680064 | tf_op jit(solution)/shard_map/self_weight_grads/pallas_call | solution.py:515
  401.2 14.2 %self_norm_back.1 = (f32[1024,1024]{1,0:T(8,128)}, f32[1,1024]{1,0:T(1,128)}, f32[1,1024]{1,0:T(1,128)}) custom-call(bf16[1024,1024]{1,0:T(8,128)(2,1)} %bitcast.62, f32[1024,1024]{1,0:T(8,128)} %get-tuple-element.96.dx1_ref, f32[1,1024]{1,0:T(1,128)} %reshape.333.gain_ref, bf16[32,112,1024]{2,1,0:T(8,128)(2,1)} %bitcast.57, ...), custom_call_target="tpu_custom_call" | custom-call | flops 6442450944 | bytes 23068672 | tf_op jit(solution)/shard_map/self_norm_back/pallas_call | solution.py:556
  415.5 0.5 broadcast.32
  416.0 1.3 reduce.21
  417.4 1.3 reduce.22
  418.8 0.7 reduce.23
  419.6 0.7 reduce.24
  420.3 0.7 reduce.25
  421.0 0.7 reduce.26
  421.8 0.7 reduce.27
  422.6 0.7 copy.52
  423.3 190.8 %scatter_gradients.1 = (f32[128,1024]{1,0:T(8,128)}, f32[32,4096]{1,0:T(8,128)}, f32[32,1024]{1,0:T(8,128)}, f32[32,1024]{1,0:T(8,128)}, f32[32,1024]{1,0:T(8,12...) custom-call(bf16[2,2,2,2,2,128,1024]{6,5,4,3,2,1,0:T(8,128)(2,1)} %b, ...), custom_call_target="tpu_custom_call" | custom-call | tf_op jit(solution)/shard_map/scatter_gradients/pallas_call | solution.py:771
  614.2 1.5 fusion.5
  615.8 0.8 collective-permute-start.3
  616.6 1.3 collective-permute-start.4
  617.9 1.4 collective-permute-start.5
  619.4 1.5 pad_maximum_fusion.4
  620.9 1.3 slice.98
  622.2 1.7 pad_maximum_fusion.2
  623.8 0.6 collective-permute-done.4
  624.4 0.7 add_bitcast_fusion
  625.1 0.7 copy.70
  625.8 0.7 copy.71
  626.4 0.7 copy.72
  627.1 0.7 copy.73
  627.7 0.7 copy.74
  628.4 0.8 copy.75
  629.2 0.8 copy.76
  (80 shorter events, 1.3 us)
Async XLA Ops:
  7.2 9.8 %copy-start.12 = (bf16[1,32,1024]{2,1,0:T(8,128)(2,1)S(1)}, bf16[1,32,1024]{2,1,0:T(8,128)(2,1)}, u32[]{:S(2)}) copy-start(bf16[1,32,1024]{2,1,0:T(8,128)(2,1)} %param.24) | copy-start | bytes 196612
  7.2 14.9 %copy-start.20 = (bf16[32]{0:T(256)(128)(2,1)S(1)}, bf16[32]{0:T(256)(128)(2,1)}, u32[]{:S(2)}) copy-start(bf16[32]{0:T(256)(128)(2,1)} %param.28) | copy-start | bytes 196
  7.2 14.9 %copy-start.21 = (bf16[32]{0:T(256)(128)(2,1)S(1)}, bf16[32]{0:T(256)(128)(2,1)}, u32[]{:S(2)}) copy-start(bf16[32]{0:T(256)(128)(2,1)} %param.29) | copy-start | bytes 196
  7.2 14.9 %copy-start.22 = (bf16[32]{0:T(256)(128)(2,1)S(1)}, bf16[32]{0:T(256)(128)(2,1)}, u32[]{:S(2)}) copy-start(bf16[32]{0:T(256)(128)(2,1)} %param.34) | copy-start | bytes 196
  7.2 14.9 %copy-start.23 = (bf16[32]{0:T(256)(128)(2,1)S(1)}, bf16[32]{0:T(256)(128)(2,1)}, u32[]{:S(2)}) copy-start(bf16[32]{0:T(256)(128)(2,1)} %param.35) | copy-start | bytes 196
  7.2 14.9 %copy-start.24 = (bf16[32]{0:T(256)(128)(2,1)S(1)}, bf16[32]{0:T(256)(128)(2,1)}, u32[]{:S(2)}) copy-start(bf16[32]{0:T(256)(128)(2,1)} %param.40) | copy-start | bytes 196
  7.3 14.9 %copy-start.25 = (bf16[32]{0:T(256)(128)(2,1)S(1)}, bf16[32]{0:T(256)(128)(2,1)}, u32[]{:S(2)}) copy-start(bf16[32]{0:T(256)(128)(2,1)} %param.41) | copy-start | bytes 196
  7.3 14.9 %copy-start.26 = (bf16[128]{0:T(256)(128)(2,1)S(1)}, bf16[128]{0:T(256)(128)(2,1)}, u32[]{:S(2)}) copy-start(bf16[128]{0:T(256)(128)(2,1)} %param.43) | copy-start | bytes 772
  7.3 14.9 %copy-start.27 = (bf16[32]{0:T(256)(128)(2,1)S(1)}, bf16[32]{0:T(256)(128)(2,1)}, u32[]{:S(2)}) copy-start(bf16[32]{0:T(256)(128)(2,1)} %param.45) | copy-start | bytes 196
  7.3 15.1 %copy-start.11 = (bf16[32,1024]{1,0:T(8,128)(2,1)S(1)}, bf16[32,1024]{1,0:T(8,128)(2,1)}, u32[]{:S(2)}) copy-start(bf16[32,1024]{1,0:T(8,128)(2,1)} %param.30) | copy-start | bytes 196612
  7.3 15.1 %copy-start.10 = (bf16[32,1024]{1,0:T(8,128)(2,1)S(1)}, bf16[32,1024]{1,0:T(8,128)(2,1)}, u32[]{:S(2)}) copy-start(bf16[32,1024]{1,0:T(8,128)(2,1)} %param.31) | copy-start | bytes 196612
  7.3 15.1 %copy-start.9 = (bf16[32,1024]{1,0:T(8,128)(2,1)S(1)}, bf16[32,1024]{1,0:T(8,128)(2,1)}, u32[]{:S(2)}) copy-start(bf16[32,1024]{1,0:T(8,128)(2,1)} %param.32) | copy-start | bytes 196612
  7.3 193.6 %all-gather.2.cloned.1.call-start = ((), (), s32[]{:S(2)}) async-start(), calls=%async_computation | async-start | bytes 28114944 | tf_op jit(solution)/shard_map/all_gather | solution.py:38
  16.0 0.9 copy-start
  17.0 139.6 %collective-permute-start = (bf16[32,1024]{1,0:T(8,128)(2,1)S(1)}, bf16[32,1024]{1,0:T(8,128)(2,1)S(1)}, u32[]{:S(2)}, u32[]{:S(2)}) collective-permute-start(bf16[32,1024]{1,0:T(8,128)(2,1)S(1)} %bitcast.80), channel_id=1, source_target_pairs={{0,1},{1,0},{2,3},{3,2},{4,5},{5,4},{6,7},{7,6},{8,9},{9,8},{10,11... | collective-permute-start | bytes 196616 | tf_op jit(solution)/shard_map/ppermute | solution.py:63
  20.0 136.5 %collective-permute-start.1 = (bf16[32,1024]{1,0:T(8,128)(2,1)S(1)}, bf16[32,1024]{1,0:T(8,128)(2,1)S(1)}, u32[]{:S(2)}, u32[]{:S(2)}) collective-permute-start(bf16[32,1024]{1,0:T(8,128)(2,1)S(1)} %bitcast.81), channel_id=1, source_target_pairs={{0,2},{1,3},{2,0},{3,1},{4,6},{5,7},{6,4},{7,5},{8,10},{9,11},{10,... | collective-permute-start | bytes 196616 | tf_op jit(solution)/shard_map/ppermute | solution.py:63
  21.5 135.0 %collective-permute-start.2 = (bf16[32,1024]{1,0:T(8,128)(2,1)S(1)}, bf16[32,1024]{1,0:T(8,128)(2,1)S(1)}, u32[]{:S(2)}, u32[]{:S(2)}) collective-permute-start(bf16[32,1024]{1,0:T(8,128)(2,1)S(1)} %bitcast.82), channel_id=1, source_target_pairs={{0,3},{1,2},{2,1},{3,0},{4,7},{5,6},{6,5},{7,4},{8,11},{9,10},{10,... | collective-permute-start | bytes 196616 | tf_op jit(solution)/shard_map/ppermute | solution.py:63
  102.5 3.4 copy-start.14
  401.2 17.6 %copy-start.19 = (f32[1,1024]{1,0:T(1,128)S(1)}, f32[1,1024]{1,0:T(1,128)}, u32[]{:S(2)}) copy-start(f32[1,1024]{1,0:T(1,128)} %get-tuple-element.123) | copy-start | bytes 12292
  401.2 18.4 %copy-start.18 = (f32[1,1024]{1,0:T(1,128)S(1)}, f32[1,1024]{1,0:T(1,128)}, u32[]{:S(2)}) copy-start(f32[1,1024]{1,0:T(1,128)} %get-tuple-element.124) | copy-start | bytes 12292
  401.2 19.1 %copy-start.17 = (f32[1,1024]{1,0:T(1,128)S(1)}, f32[1,1024]{1,0:T(1,128)}, u32[]{:S(2)}) copy-start(f32[1,1024]{1,0:T(1,128)} %get-tuple-element.125) | copy-start | bytes 12292
  401.2 19.8 %copy-start.16 = (f32[1,1024]{1,0:T(1,128)S(1)}, f32[1,1024]{1,0:T(1,128)}, u32[]{:S(2)}) copy-start(f32[1,1024]{1,0:T(1,128)} %get-tuple-element.126) | copy-start | bytes 12292
  401.2 20.6 %copy-start.15 = (f32[1,1024]{1,0:T(1,128)S(1)}, f32[1,1024]{1,0:T(1,128)}, u32[]{:S(2)}) copy-start(f32[1,1024]{1,0:T(1,128)} %get-tuple-element.128) | copy-start | bytes 12292
  401.2 21.3 %copy-start.13 = (f32[1,4096]{1,0:T(1,128)S(1)}, f32[1,4096]{1,0:T(1,128)}, u32[]{:S(2)}) copy-start(f32[1,4096]{1,0:T(1,128)} %get-tuple-element.127) | copy-start | bytes 49156
  423.3 192.5 %copy-start.1 = (f32[128,1024]{1,0:T(8,128)S(1)}, f32[128,1024]{1,0:T(8,128)}, u32[]{:S(2)}) copy-start(f32[128,1024]{1,0:T(8,128)} %get-tuple-element.106) | copy-start | bytes 1572868
  614.2 10.9 %copy-start.8 = (f32[32,1024]{1,0:T(8,128)S(1)}, f32[32,1024]{1,0:T(8,128)}, u32[]{:S(2)}) copy-start(f32[32,1024]{1,0:T(8,128)} %get-tuple-element.195) | copy-start | bytes 393220
  614.2 11.6 %copy-start.7 = (f32[32,1024]{1,0:T(8,128)S(1)}, f32[32,1024]{1,0:T(8,128)}, u32[]{:S(2)}) copy-start(f32[32,1024]{1,0:T(8,128)} %get-tuple-element.198) | copy-start | bytes 393220
  614.2 12.2 %copy-start.6 = (f32[32,1024]{1,0:T(8,128)S(1)}, f32[32,1024]{1,0:T(8,128)}, u32[]{:S(2)}) copy-start(f32[32,1024]{1,0:T(8,128)} %get-tuple-element.199) | copy-start | bytes 393220
  614.2 12.9 %copy-start.5 = (f32[32,1024]{1,0:T(8,128)S(1)}, f32[32,1024]{1,0:T(8,128)}, u32[]{:S(2)}) copy-start(f32[32,1024]{1,0:T(8,128)} %get-tuple-element.200) | copy-start | bytes 393220
  614.2 13.5 %copy-start.4 = (f32[32,1024]{1,0:T(8,128)S(1)}, f32[32,1024]{1,0:T(8,128)}, u32[]{:S(2)}) copy-start(f32[32,1024]{1,0:T(8,128)} %get-tuple-element.201) | copy-start | bytes 393220
  614.2 14.2 %copy-start.3 = (f32[32,4096]{1,0:T(8,128)S(1)}, f32[32,4096]{1,0:T(8,128)}, u32[]{:S(2)}) copy-start(f32[32,4096]{1,0:T(8,128)} %get-tuple-element.204) | copy-start | bytes 1572868
  615.8 13.4 %copy-start.2 = (f32[128,1024]{1,0:T(8,128)S(1)}, f32[128,1024]{1,0:T(8,128)}, u32[]{:S(2)}) copy-start(f32[128,1024]{1,0:T(8,128)} %get-tuple-element.206) | copy-start | bytes 1572868
  615.8 8.0 %collective-permute-start.3 = (f32[32,1024]{1,0:T(8,128)S(1)}, f32[32,1024]{1,0:T(8,128)S(1)}, u32[]{:S(2)}, u32[]{:S(2)}) collective-permute-start(f32[32,1024]{1,0:T(8,128)S(1)} %get-tuple-element.150), channel_id=1, source_target_pairs={{0,1},{1,0},{2,3},{3,2},{4,5},{5,4},{6,7},{7,6},{8,9},{9,8},{10,11... | collective-permute-start | bytes 393224 | tf_op jit(solution)/shard_map/ppermute | solution.py:63
  616.6 7.8 %collective-permute-start.4 = (f32[32,1024]{1,0:T(8,128)S(1)}, f32[32,1024]{1,0:T(8,128)S(1)}, u32[]{:S(2)}, u32[]{:S(2)}) collective-permute-start(f32[32,1024]{1,0:T(8,128)S(1)} %get-tuple-element.152), channel_id=1, source_target_pairs={{0,2},{1,3},{2,0},{3,1},{4,6},{5,7},{6,4},{7,5},{8,10},{9,11},{10,... | collective-permute-start | bytes 393224 | tf_op jit(solution)/shard_map/ppermute | solution.py:63
  617.9 6.5 %collective-permute-start.5 = (f32[32,1024]{1,0:T(8,128)S(1)}, f32[32,1024]{1,0:T(8,128)S(1)}, u32[]{:S(2)}, u32[]{:S(2)}) collective-permute-start(f32[32,1024]{1,0:T(8,128)S(1)} %get-tuple-element.151), channel_id=1, source_target_pairs={{0,3},{1,2},{2,1},{3,0},{4,7},{5,6},{6,5},{7,4},{8,11},{9,10},{10,... | collective-permute-start | bytes 393224 | tf_op jit(solution)/shard_map/ppermute | solution.py:63
Sparse Core Ops, SparseCore 0:
  17.1 183.7 all-gather.1

commit v3 on v2

v3 whole, which is shorter than its diff:
```python
import functools
import math

import jax
import jax.numpy as jnp
from jax import lax
from jax.experimental import pallas as pl
from jax.experimental.pallas import tpu as pltpu
from jax.sharding import PartitionSpec as P

HEAD_DIM = 64
TILE = 256
BF16 = jnp.bfloat16
VMEM_LIMIT = 60 * 1024 * 1024
MLP_STEPS = 8

EPSILON = 1e-05
NEGATIVE = -1e30

AXES = ("wide", "narrow")


def axis_bits(axis):
    return lax.axis_size(axis).bit_length() - 1


def pack_vectors(vectors):
    flat = jnp.concatenate(vectors)
    room = -flat.shape[0] % (16 * 1024)
    return jnp.pad(flat, (0, room)).reshape(-1, 1024)


def take_vectors(rows, sizes):
    flat = rows.reshape(rows.shape[0], -1)
    out, at = [], 0
    for size in sizes:
        out.append(flat[:, at : at + size].reshape(1, -1).astype(jnp.float32))
        at += size
    return out


def nn(a, b):
    return lax.dot_general(a, b, (((1,), (0,)), ((), ())), preferred_element_type=jnp.float32)


def nt(a, b):
    return lax.dot_general(a, b, (((1,), (1,)), ((), ())), preferred_element_type=jnp.float32)


def tn(a, b):
    return lax.dot_general(a, b, (((0,), (0,)), ((), ())), preferred_element_type=jnp.float32)


def standardize(values):
    center = jnp.mean(values, axis=-1, keepdims=True)
    offset = values - center
    rate = lax.rsqrt(jnp.mean(offset * offset, axis=-1, keepdims=True) + EPSILON)
    return offset * rate, rate


def norm_back(standard, rate, gain, grad):
    scaled = grad * gain
    return rate * (
        scaled
        - jnp.mean(scaled, axis=-1, keepdims=True)
        - standard * jnp.mean(scaled * standard, axis=-1, keepdims=True)
    )


def column_sum(values):
    return jnp.sum(values, axis=0, keepdims=True)


def square(ref):
    return ref[...].reshape(-1, ref.shape[-1])


def head_lanes(block, head):
    lane = lax.broadcasted_iota(jnp.int32, block.shape, 1)
    inside = (lane >= HEAD_DIM) if head else (lane < HEAD_DIM)
    return jnp.where(inside, block, jnp.zeros_like(block))


def whole_block(shape):
    zeros = (0,) * len(shape)
    return pl.BlockSpec(shape, lambda *_: zeros, pipeline_mode=pl.Buffered(1))


def params(**extra):
    return pltpu.CompilerParams(vmem_limit_bytes=VMEM_LIMIT, **extra)


def attend_kernel(
    x_ref, gain_ref, bias_ref, wq_ref, wk_ref, wv_ref, h_ref, q_ref, k_ref, v_ref, o_ref, sums_ref
):
    rows = x_ref.shape[0]

    @pl.when(pl.program_id(0) == 0)
    def _():
        for start in range(0, rows, TILE):
            at = slice(start, start + TILE)
            standard, _ = standardize(x_ref[at, :].astype(jnp.float32))
            h_ref[at, :] = (standard * gain_ref[...] + bias_ref[...]).astype(BF16)

    weights = jnp.concatenate([square(w) for w in (wq_ref, wk_ref, wv_ref)], axis=1)
    mapped = nn(h_ref[...], weights).astype(BF16)
    q_ref[...] = mapped[:, :128]
    k_ref[...] = mapped[:, 128:256]
    v_ref[...] = mapped[:, 256:]
    flipped = v_ref[...].T
    for start in range(0, rows, TILE):
        span = start + TILE
        queries = q_ref[start:span, :] * (HEAD_DIM**-0.5)
        keys = k_ref[:span, :]
        mixed, sums = [], []
        for head in range(2):
            scores = nt(keys, head_lanes(queries, head))
            key_at = lax.broadcasted_iota(jnp.int32, (TILE, TILE), 0)
            query_at = lax.broadcasted_iota(jnp.int32, (TILE, TILE), 1)
            corner = jnp.where(key_at <= query_at, scores[start:], NEGATIVE)
            scores = jnp.concatenate([scores[:start], corner], axis=0) if start else corner
            top = jnp.max(scores, axis=0, keepdims=True)
            powers = jnp.exp(scores - top)
            total = jnp.sum(powers, axis=0, keepdims=True)
            part = nn(flipped[HEAD_DIM * head : HEAD_DIM * (head + 1), :span], powers.astype(BF16))
            mixed.append(part * (1.0 / total))
            sums.append(top + jnp.log(total))
        o_ref[start:span, :] = jnp.concatenate(mixed, axis=0).T.astype(BF16)
        sums_ref[0, :, start:span] = jnp.concatenate(sums, axis=0)


def attend(tokens, gain, bias, weights, work, schedule, collective_id):
    rows, width = tokens.shape
    pairs = width // 128
    block = pl.BlockSpec((rows, 128), lambda p: (0, p))
    arrays, specs = zip(*weights)
    like = jax.ShapeDtypeStruct(tokens.shape, BF16)
    results = pl.pallas_call(
        beside(attend_kernel, work, (6, 6, 0), schedule, pairs),
        grid=(pairs,),
        in_specs=[whole_block(tokens.shape), whole_block(gain.shape), whole_block(bias.shape)]
        + list(specs)
        + work.in_specs,
        out_specs=[whole_block(tokens.shape)]
        + [block] * 4
        + [pl.BlockSpec((1, 2, rows), lambda p: (p, 0, 0))]
        + work.out_specs,
        out_shape=[like] * 5
        + [jax.ShapeDtypeStruct((pairs, 2, rows), jnp.float32)]
        + work.out_shape,
        scratch_shapes=work.scratch,
        compiler_params=params(collective_id=collective_id, has_side_effects=True),
        name="self_attend",
    )(tokens, gain, bias, *arrays, *work.arrays)
    return results[:6], work.results(results[6:])


def attend_back_kernel(
    q_ref, k_ref, v_ref, da_ref, sums_ref, h_ref,
    dq_ref, dk_ref, dv_ref, dwq_ref, dwk_ref, dwv_ref, dk_sum, dv_sum, h_flip,
):
    rows, width = q_ref.shape

    @pl.when(pl.program_id(0) == 0)
    def _():
        h_flip[...] = h_ref[...].T

    flipped = k_ref[...].T
    for start in reversed(range(0, rows, TILE)):
        span = start + TILE
        queries = q_ref[start:span, :] * (HEAD_DIM**-0.5)
        grads = da_ref[start:span, :]
        keys = k_ref[:span, :]
        values = v_ref[:span, :]
        parts = []
        for head in range(2):
            own_queries = head_lanes(queries, head)
            own_grads = head_lanes(grads, head)
            scores = nt(keys, own_queries)
            key_at = lax.broadcasted_iota(jnp.int32, (TILE, TILE), 0)
            query_at = lax.broadcasted_iota(jnp.int32, (TILE, TILE), 1)
            corner = jnp.where(key_at <= query_at, scores[start:], NEGATIVE)
            scores = jnp.concatenate([scores[:start], corner], axis=0) if start else corner
            probs = jnp.exp(scores - sums_ref[0, head : head + 1, start:span])
            grad_probs = nt(values, own_grads)
            inner = jnp.sum(probs * grad_probs, axis=0, keepdims=True)
            grad_scores = (probs * (grad_probs - inner)).astype(BF16)
            value_term = nn(probs.astype(BF16), own_grads)
            key_term = nn(grad_scores, own_queries)
            if span == rows and head == 0:
                dv_sum[...] = value_term
                dk_sum[...] = key_term
            else:
                dv_sum[:span, :] += value_term
                dk_sum[:span, :] += key_term
            parts.append(nn(flipped[HEAD_DIM * head : HEAD_DIM * (head + 1), :span], grad_scores))
        dq = jnp.concatenate(parts, axis=0).T * (HEAD_DIM**-0.5)
        dq_ref[start:span, :] = dq.astype(BF16)
    dk_ref[...] = dk_sum[...].astype(BF16)
    dv_ref[...] = dv_sum[...].astype(BF16)
    grads = jnp.concatenate([dq_ref[...], dk_ref[...], dv_ref[...]], axis=1)
    weights = nn(h_flip[...], grads).astype(BF16)
    dwq_ref[...] = weights[:, :128]
    dwk_ref[...] = weights[:, 128:256]
    dwv_ref[...] = weights[:, 256:]


def attend_back(queries, keys, values, grads, sums, normed, work, schedule, collective_id):
    rows, width = queries.shape
    steps = width // 128
    block = pl.BlockSpec((rows, 128), lambda p: (0, p))
    results = pl.pallas_call(
        beside(attend_back_kernel, work, (6, 6, 3), schedule, steps),
        grid=(steps,),
        in_specs=[block] * 4
        + [pl.BlockSpec((1, 2, rows), lambda p: (p, 0, 0)), whole_block(normed.shape)]
        + work.in_specs,
        out_specs=[block] * 6 + work.out_specs,
        out_shape=[jax.ShapeDtypeStruct(queries.shape, BF16)] * 3
        + [jax.ShapeDtypeStruct((width, width), BF16)] * 3
        + work.out_shape,
        scratch_shapes=[pltpu.VMEM((rows, 128), jnp.float32)] * 2
        + [pltpu.VMEM((width, rows), BF16)]
        + work.scratch,
        compiler_params=params(collective_id=collective_id, has_side_effects=True),
        name="self_attend_back",
    )(queries, keys, values, grads, sums, normed, *work.arrays)
    return results[:6], work.results(results[6:])


def gelu_both(values):
    phi = 0.5 + 0.5 * lax.erf(values * (0.5**0.5))
    density = jnp.exp(-0.5 * values * values) * ((2.0 * math.pi) ** -0.5)
    return values * phi, phi + values * density


def mlp_kernel(
    near, far, work, x_ref, h_ref, g_ref, gain_ref, up_ref, ub_ref, down_ref, db_ref,
    out_ref, dx_ref, dub_ref, dgain_ref, dbias_ref, gsum_ref, ddown_ref, *refs,
):
    far_refs, refs = refs[:far], refs[far:]
    sums, refs = refs[: len(work.out_specs)], refs[len(work.out_specs) :]
    out_sum, dh_sum, h_flip, act, grad_act = refs[:5]
    near_refs, refs = refs[5 : 5 + near], refs[5 + near :]
    step, steps = pl.program_id(0), pl.num_programs(0)
    rows = h_ref.shape[0]
    parts = near + far
    per = MLP_STEPS // parts
    moving = work.bind(near_refs, sums, refs) if near else None

    @pl.when(step == 0)
    def _():
        if near:
            greet_partners()
        h_flip[...] = h_ref[...].T
        out_sum[...] = x_ref[...] + db_ref[...]
        dh_sum[...] = jnp.zeros_like(dh_sum)

    left = []
    for part in range(near):
        terms = [k for k, t in enumerate(work.terms) if t[0] == part]
        for stage in range(-1, moving.stages):
            place = per * (part + 1) + stage + 1
            if place >= MLP_STEPS:
                left.append((stage, terms))
                continue

            @pl.when(step == place)
            def _(stage=stage, terms=terms):
                moving.step(stage, terms)

    up = square(up_ref)
    down = square(down_ref)
    bias_sum = jnp.zeros_like(dub_ref)
    for start in range(0, rows, TILE):
        at = slice(start, start + TILE)
        hidden, slope = gelu_both(nn(h_ref[at, :], up) + ub_ref[...])
        act[at, :] = hidden.astype(BF16)
        grad_pre = (nt(g_ref[at, :], down) * slope).astype(BF16)
        grad_act[at, :] = grad_pre
        bias_sum += column_sum(grad_pre.astype(jnp.float32))
        out_sum[at, :] += nn(act[at, :], down)
        dh_sum[at, :] += nt(grad_pre, up)
    dub_ref[...] = bias_sum
    grad_up = nn(h_flip[...], grad_act[...]).astype(BF16)
    chunk = grad_up.shape[1]
    for part, ref in enumerate(far_refs):

        @pl.when(step // per == near + part)
        def _(ref=ref):
            ref[...] = grad_up

    for place in range(near * per):

        @pl.when(step == place)
        def _(place=place):
            ref = near_refs[place // per]
            first = chunk * (place % per)
            ref[..., first : first + chunk] = grad_up.reshape(ref.shape[:-1] + (chunk,))

    ddown_ref[...] = tn(act[...], g_ref[...]).astype(BF16)

    @pl.when(step == steps - 1)
    def _():
        gain_sum = jnp.zeros_like(dgain_ref)
        grad_sum = jnp.zeros_like(dbias_ref)
        tail_sum = jnp.zeros_like(gsum_ref)
        for start in range(0, rows, TILE):
            at = slice(start, start + TILE)
            out_ref[at, :] = out_sum[at, :].astype(BF16)
            standard, rate = standardize(x_ref[at, :])
            grad = dh_sum[at, :]
            tail = g_ref[at, :].astype(jnp.float32)
            dx_ref[at, :] = tail + norm_back(standard, rate, gain_ref[...], grad)
            gain_sum += column_sum(grad * standard)
            grad_sum += column_sum(grad)
            tail_sum += column_sum(tail)
        dgain_ref[...] = gain_sum
        dbias_ref[...] = grad_sum
        gsum_ref[...] = tail_sum
        for stage, terms in left:
            moving.step(stage, terms)
        if near:
            moving.settle()


def mlp(x, h, g, gain, up, up_bias, down, down_bias, near, runs, orders, collective_id):
    rows, width = x.shape
    hidden = up_bias.shape[1]
    chunk = hidden // MLP_STEPS
    f32 = jnp.float32
    row = (1, width)
    parts = hidden // width
    per = width // chunk
    lead = (2,) * len(cube_dims())
    block = lead + (width >> len(lead), width)
    source = jax.ShapeDtypeStruct(block, BF16)
    work = Scatter([(source, runs, orders)] * near, near=True)
    far = parts - near
    results = pl.pallas_call(
        functools.partial(mlp_kernel, near, far, work),
        grid=(MLP_STEPS,),
        in_specs=[
            whole_block(x.shape), whole_block(h.shape), whole_block(g.shape), whole_block(row),
            up[1], pl.BlockSpec((1, chunk), lambda c: (0, c)), down[1], whole_block(row),
        ],
        out_specs=[
            whole_block(x.shape), whole_block(x.shape),
            pl.BlockSpec((1, chunk), lambda c: (0, c)),
            whole_block(row), whole_block(row), whole_block(row),
            pl.BlockSpec((chunk, width), lambda c: (c, 0)),
        ]
        + [
            pl.BlockSpec((width, chunk), lambda c, k=k: (0, jnp.clip(c - per * k, 0, per - 1)))
            for k in range(near, parts)
        ]
        + work.out_specs,
        out_shape=[
            jax.ShapeDtypeStruct(x.shape, BF16), jax.ShapeDtypeStruct(x.shape, f32),
            jax.ShapeDtypeStruct((1, hidden), f32),
            jax.ShapeDtypeStruct(row, f32), jax.ShapeDtypeStruct(row, f32), jax.ShapeDtypeStruct(row, f32),
            jax.ShapeDtypeStruct((hidden, width), BF16),
        ]
        + [jax.ShapeDtypeStruct((width, width), BF16)] * far
        + work.out_shape,
        scratch_shapes=[
            pltpu.VMEM(x.shape, f32), pltpu.VMEM(x.shape, f32), pltpu.VMEM((width, rows), BF16),
            pltpu.VMEM((rows, chunk), BF16), pltpu.VMEM((rows, chunk), BF16),
        ]
        + [pltpu.VMEM(block, BF16)] * near
        + (work.scratch if near else []),
        compiler_params=params(collective_id=collective_id, has_side_effects=True) if near else params(),
        name="mlp_both_ways",
    )(x, h, g, gain, up[0], up_bias, down[0], down_bias)
    sums = work.results(results[7 + far :]) if near else []
    return *results[:7], results[7 : 7 + far], sums


def caption_probs(keys, own_queries, mask):
    scores = jnp.where(mask != 0, nt(keys, own_queries), NEGATIVE)
    powers = jnp.exp(scores - jnp.max(scores, axis=0, keepdims=True))
    return powers * (1.0 / jnp.sum(powers, axis=0, keepdims=True))


def middle_kernel(
    x_ref, a_ref, text_ref, mask_ref, gain2_ref, bias2_ref, gain3_ref, bias3_ref,
    wo_ref, cq_ref, ck_ref, cv_ref, co_ref,
    x1_ref, h2_ref, q2_ref, a2_ref, x2_ref, h3_ref, k2_ref, v2_ref,
):
    @pl.when(pl.program_id(0) == 0)
    def _():
        k2_ref[...] = nn(text_ref[...], square(ck_ref)).astype(BF16)
        v2_ref[...] = nn(text_ref[...], square(cv_ref)).astype(BF16)

    after_self = x_ref[...].astype(jnp.float32) + nn(a_ref[...], square(wo_ref))
    x1_ref[...] = after_self
    standard, _ = standardize(after_self)
    normed = (standard * gain2_ref[...] + bias2_ref[...]).astype(BF16)
    h2_ref[...] = normed
    q2_ref[...] = nn(normed, square(cq_ref)).astype(BF16)
    mask = mask_ref[...]
    for pair in range(q2_ref.shape[1] // 128):
        at = slice(128 * pair, 128 * (pair + 1))
        queries = q2_ref[:, at] * (HEAD_DIM**-0.5)
        keys = k2_ref[:, at]
        flipped = v2_ref[:, at].T
        mixed = []
        for head in range(2):
            probs = caption_probs(keys, head_lanes(queries, head), mask).astype(BF16)
            mixed.append(nn(flipped[HEAD_DIM * head : HEAD_DIM * (head + 1)], probs))
        a2_ref[:, at] = jnp.concatenate(mixed, axis=0).T.astype(BF16)
    after_cross = after_self + nn(a2_ref[...], square(co_ref))
    x2_ref[...] = after_cross
    standard, _ = standardize(after_cross)
    h3_ref[...] = (standard * gain3_ref[...] + bias3_ref[...]).astype(BF16)


def middle(tokens, mixed, text, mask, vectors, weights, work, schedule, collective_id):
    rows, width = tokens.shape
    slots = text.shape[0]
    tile = pl.BlockSpec((TILE, width), lambda i: (i, 0))
    arrays, specs = zip(*weights)
    f32 = jnp.float32
    like = lambda dtype: jax.ShapeDtypeStruct(tokens.shape, dtype)
    results = pl.pallas_call(
        beside(middle_kernel, work, (13, 8, 0), schedule, rows // TILE),
        grid=(rows // TILE,),
        in_specs=[
            tile, tile, whole_block(text.shape), whole_block(mask.shape),
            *[whole_block(v.shape) for v in vectors], *specs, *work.in_specs,
        ],
        out_specs=[tile] * 6 + [whole_block(text.shape)] * 2 + work.out_specs,
        out_shape=[like(f32), like(BF16), like(BF16), like(BF16), like(f32), like(BF16)]
        + [jax.ShapeDtypeStruct(text.shape, BF16)] * 2
        + work.out_shape,
        scratch_shapes=work.scratch,
        compiler_params=params(collective_id=collective_id, has_side_effects=True),
        name="output_and_cross",
    )(tokens, mixed, text, mask, *vectors, *arrays, *work.arrays)
    return results[:8], work.results(results[8:])


def middle_back_kernel(
    dx2_ref, x1_ref, a1_ref, h2_ref, q2_ref, a2_ref, k2_ref, v2_ref, text_ref, mask_ref, gain2_ref,
    wo_ref, cq_ref, ck_ref, cv_ref, co_ref,
    dx1_ref, da1_ref, dwo_ref, dcq_ref, dck_ref, dcv_ref, dco_ref, dtext_ref, dgain_ref, dbias_ref,
    wo_sum, cq_sum, co_sum, dk_sum, dv_sum, dq2,
):
    step, steps = pl.program_id(0), pl.num_programs(0)

    @pl.when(step == 0)
    def _():
        for ref in (wo_sum, cq_sum, co_sum, dk_sum, dv_sum, dgain_ref, dbias_ref):
            ref[...] = jnp.zeros_like(ref)

    grad_out = dx2_ref[...].astype(BF16)
    co_sum[...] += tn(a2_ref[...], grad_out)
    grad_mixed = nt(grad_out, square(co_ref)).astype(BF16)
    mask = mask_ref[...]
    for pair in range(q2_ref.shape[1] // 128):
        at = slice(128 * pair, 128 * (pair + 1))
        queries = q2_ref[:, at] * (HEAD_DIM**-0.5)
        keys = k2_ref[:, at]
        flipped = keys.T
        values = v2_ref[:, at]
        grads = grad_mixed[:, at]
        parts = []
        for head in range(2):
            own_queries = head_lanes(queries, head)
            own_grads = head_lanes(grads, head)
            probs = caption_probs(keys, own_queries, mask)
            grad_probs = nt(values, own_grads)
            inner = jnp.sum(probs * grad_probs, axis=0, keepdims=True)
            grad_scores = (probs * (grad_probs - inner)).astype(BF16)
            dv_sum[:, at] += nn(probs.astype(BF16), own_grads)
            dk_sum[:, at] += nn(grad_scores, own_queries)
            parts.append(nn(flipped[HEAD_DIM * head : HEAD_DIM * (head + 1)], grad_scores))
        dq2[:, at] = (jnp.concatenate(parts, axis=0).T * (HEAD_DIM**-0.5)).astype(BF16)
    cq_sum[...] += tn(h2_ref[...], dq2[...])
    grad_normed = nt(dq2[...], square(cq_ref))
    standard, rate = standardize(x1_ref[...])
    grad_after = dx2_ref[...] + norm_back(standard, rate, gain2_ref[...], grad_normed)
    dgain_ref[...] += column_sum(grad_normed * standard)
    dbias_ref[...] += column_sum(grad_normed)
    dx1_ref[...] = grad_after
    grad_self = grad_after.astype(BF16)
    wo_sum[...] += tn(a1_ref[...], grad_self)
    da1_ref[...] = nt(grad_self, square(wo_ref)).astype(BF16)

    @pl.when(step == steps - 1)
    def _():
        dwo_ref[...] = wo_sum[...].astype(BF16)
        dcq_ref[...] = cq_sum[...].astype(BF16)
        dco_ref[...] = co_sum[...].astype(BF16)
        grad_keys = dk_sum[...].astype(BF16)
        grad_values = dv_sum[...].astype(BF16)
        dck_ref[...] = tn(text_ref[...], grad_keys).astype(BF16)
        dcv_ref[...] = tn(text_ref[...], grad_values).astype(BF16)
        dtext_ref[...] = nt(grad_keys, square(ck_ref)) + nt(grad_values, square(cv_ref))


def middle_back(
    dx2, x1, a1, h2, q2, a2, k2, v2, text, mask, gain, weights, work, schedule, collective_id
):
    rows, width = x1.shape
    slots = text.shape[0]
    tile = pl.BlockSpec((TILE, width), lambda i: (i, 0))
    arrays, specs = zip(*weights)
    f32 = jnp.float32
    matrix = (width, width)
    results = pl.pallas_call(
        beside(middle_back_kernel, work, (16, 10, 6), schedule, rows // TILE),
        grid=(rows // TILE,),
        in_specs=[tile] * 6
        + [whole_block(v.shape) for v in (k2, v2, text, mask, gain)]
        + list(specs)
        + work.in_specs,
        out_specs=[tile] * 2
        + [whole_block(matrix)] * 5
        + [whole_block(text.shape)]
        + [whole_block(gain.shape)] * 2
        + work.out_specs,
        out_shape=[jax.ShapeDtypeStruct(x1.shape, f32), jax.ShapeDtypeStruct(x1.shape, BF16)]
        + [jax.ShapeDtypeStruct(matrix, BF16)] * 5
        + [jax.ShapeDtypeStruct(text.shape, f32)]
        + [jax.ShapeDtypeStruct(gain.shape, f32)] * 2
        + work.out_shape,
        scratch_shapes=[pltpu.VMEM(matrix, f32)] * 3
        + [pltpu.VMEM(text.shape, f32)] * 2
        + [pltpu.VMEM((TILE, width), BF16)]
        + work.scratch,
        compiler_params=params(collective_id=collective_id, has_side_effects=True),
        name="cross_back",
    )(dx2, x1, a1, h2, q2, a2, k2, v2, text, mask, gain, *arrays, *work.arrays)
    return results[:10], work.results(results[10:])


def first_back_kernel(
    work, schedule, steps, x_ref, dx1_ref, gain_ref, vectors_ref, wq_ref, wk_ref, wv_ref, dq_ref, dk_ref, dv_ref,
    *refs,
):
    n, m = len(work.in_specs), len(work.out_specs)
    sources, (dx_ref, vector_sum_ref), sums = refs[:n], refs[n : n + 2], refs[n + 2 : n + 2 + m]
    stages = len(cube_dims())
    rest = refs[n + 2 + m :]
    doubling = Doubling(rest[0], rest[1 : stages + 1], *rest[stages + 1 : stages + 3])
    halving = work.bind(sources, sums, rest[stages + 3 :])
    step = pl.program_id(0)
    vectors = doubling.buffers[0]

    @pl.when(step == 0)
    def _():
        greet_partners()
        halving.step(-1)
        vectors[...] = vectors_ref[...]

    for stage, place in enumerate(schedule):

        @pl.when(step == place)
        def _(stage=stage):
            halving.step(stage)

    grad_normed = (
        nt(dq_ref[...], square(wq_ref)) + nt(dk_ref[...], square(wk_ref)) + nt(dv_ref[...], square(wv_ref))
    )
    standard, rate = standardize(x_ref[...].astype(jnp.float32))
    dx_ref[...] = dx1_ref[...] + norm_back(standard, rate, gain_ref[...], grad_normed)
    vectors[0:1, :] += column_sum(grad_normed * standard)
    vectors[1:2, :] += column_sum(grad_normed)

    @pl.when(step == steps - 1)
    def _():
        doubling.step(-1)
        for stage in range(max(stages, halving.stages)):
            if stage < stages:
                doubling.step(stage)
            if len(schedule) + stage < halving.stages:
                halving.step(len(schedule) + stage)
        vector_sum_ref[...] = doubling.buffers[-1][...]
        doubling.settle()
        halving.settle()


def first_back(tokens, dx1, gain, vectors, weights, grads, work, schedule, collective_id):
    rows, width = tokens.shape
    steps = rows // TILE
    tile = pl.BlockSpec((TILE, width), lambda i: (i, 0))
    arrays, specs = zip(*weights)
    f32 = jnp.float32
    results = pl.pallas_call(
        functools.partial(first_back_kernel, work, schedule, steps),
        grid=(steps,),
        in_specs=[tile] * 2
        + [whole_block(gain.shape), whole_block(vectors.shape)]
        + list(specs)
        + [tile] * 3
        + work.in_specs,
        out_specs=[tile, whole_block(vectors.shape)] + work.out_specs,
        out_shape=[
            jax.ShapeDtypeStruct(tokens.shape, f32),
            jax.ShapeDtypeStruct(vectors.shape, f32),
        ]
        + work.out_shape,
        scratch_shapes=doubling_scratch(vectors.shape) + work.scratch,
        compiler_params=params(collective_id=collective_id, has_side_effects=True),
        name="self_norm_back",
    )(tokens, dx1, gain, vectors, *arrays, *grads, *work.arrays)
    return results[:2], work.results(results[2:])


def cube_dims(axes=AXES):
    return [(axis, k) for axis in axes for k in reversed(range(axis_bits(axis)))]


def bits_of(dims):
    return [(lax.axis_index(axis) >> bit) & 1 for axis, bit in dims]


def partner(axis, bit):
    return {axis: lax.axis_index(axis) ^ (1 << bit)}


def halving_orders():
    x, y, near, far = ("narrow", 0), ("narrow", 1), ("wide", 1), ("wide", 2)
    core = ("wide", 0)
    six = (
        (far, x, y, near),
        (near, y, x, far),
        (y, far, x, near),
        (x, near, y, far),
        (x, y, far, near),
        (y, x, near, far),
    )
    rest = [d for d in cube_dims() if d not in (core, x, y, near, far)]
    return [[core, *order, *rest] for order in six]


def greet_partners():
    dims = cube_dims()
    barrier = pltpu.get_barrier_semaphore()
    for axis, bit in dims:
        pl.semaphore_signal(
            barrier, inc=1, device_id=partner(axis, bit), device_id_type=pl.DeviceIdType.MESH
        )
    pl.semaphore_wait(barrier, len(dims))


def row_pieces(rows, count, step=16):
    if rows % step:
        return [(0, rows)]
    cuts = [rows * k // count // step * step for k in range(count)] + [rows]
    return [(a, b - a) for a, b in zip(cuts[:-1], cuts[1:]) if b > a]


class Gathering:
    def __init__(self, pieces, dims, sources, outs, scratch):
        self.pieces, self.dims, self.sources, self.outs = pieces, dims, sources, outs
        self.send_sems, self.recv_sems, self.own_sems = scratch
        self.stages = max(len(order) for _, _, _, order in pieces)
        self.base = [sum(len(p[3]) for p in pieces[:k]) for k in range(len(pieces))]

    def own(self, which):
        there = self.outs[which].at[tuple(bits_of(self.dims[which]))]
        return pltpu.make_async_copy(self.sources[which], there, self.own_sems.at[which])

    def send(self, piece, stage):
        which, start, size, order = self.pieces[piece]
        rows = slice(start, start + size)
        held = order[:stage]
        dims = self.dims[which]
        at = tuple(slice(None) if d in held else b for d, b in zip(dims, bits_of(dims))) + (rows,)
        there = self.outs[which].at[at]
        sem = self.base[piece] + stage
        return pltpu.make_async_remote_copy(
            src_ref=there if stage else self.sources[which].at[rows],
            dst_ref=there,
            send_sem=self.send_sems.at[sem],
            recv_sem=self.recv_sems.at[sem],
            device_id=partner(*order[stage]),
            device_id_type=pl.DeviceIdType.MESH,
        )

    def step(self, stage):
        if stage < 0:
            for which in range(len(self.sources)):
                self.own(which).start()
        if stage == 0:
            for which in range(len(self.sources)):
                self.own(which).wait()
        for piece, (_, _, _, order) in enumerate(self.pieces):
            if 0 <= stage < len(order):
                self.send(piece, stage).wait_recv()
            if stage + 1 < len(order):
                self.send(piece, stage + 1).start()

    def settle(self):
        for piece, (_, _, _, order) in enumerate(self.pieces):
            for stage in range(len(order)):
                self.send(piece, stage).wait_send()


class Gather:
    def __init__(self, groups):
        self.arrays = [array for array, _, _ in groups]
        self.pieces, self.dims = [], []
        for which, (array, runs, orders) in enumerate(groups):
            self.dims.append([d for d in cube_dims() if d in orders[0]])
            for k, (start, size) in enumerate(runs):
                self.pieces.append((which, start, size, orders[k % len(orders)]))
        copies = sum(len(order) for _, _, _, order in self.pieces)
        self.in_specs = [pl.BlockSpec(memory_space=pl.ANY)] * len(groups)
        self.out_specs = self.in_specs
        self.out_shape = [
            jax.ShapeDtypeStruct((2,) * len(d) + a.shape, a.dtype)
            for a, d in zip(self.arrays, self.dims)
        ]
        self.scratch = [pltpu.SemaphoreType.DMA((copies,))] * 2
        self.scratch += [pltpu.SemaphoreType.DMA((len(groups),))]

    def bind(self, sources, outs, scratch):
        return Gathering(self.pieces, self.dims, sources, outs, scratch)

    def results(self, outs):
        return [out.reshape((-1,) + a.shape) for out, a in zip(outs, self.arrays)]


class Halving:
    def __init__(self, terms, sources, outs, scratch, near=False):
        count = len(terms)
        self.terms, self.sources, self.outs, self.near = terms, sources, outs, near
        self.kept, rest = ([], scratch) if near else (scratch[:count], scratch[count:])
        self.landed, self.base = [], []
        for _, _, _, order in terms:
            self.base.append(sum(len(t[3]) for t in terms[: len(self.base)]))
            self.landed.append(rest[: len(order)])
            rest = rest[len(order) :]
        self.send_sems, self.recv_sems = rest[:2]
        self.kept_sems = None if near else rest[2]
        self.stages = max(len(order) for _, _, _, order in terms)

    def half(self, term, stage, other):
        _, start, size, order = self.terms[term]
        left = [d for d in cube_dims() if d in order[stage:]]
        bit = bits_of([order[stage]])[0]
        at = [(1 - bit if other else bit) if d == order[stage] else slice(None) for d in left]
        if stage == 0:
            at.append(slice(start, start + size))
        return tuple(at)

    def before(self, term, stage):
        return self.sources[self.terms[term][0]] if stage == 0 else self.landed[term][stage - 1]

    def send(self, term, stage):
        order = self.terms[term][3]
        sem = self.base[term] + stage
        return pltpu.make_async_remote_copy(
            src_ref=self.before(term, stage).at[self.half(term, stage, True)],
            dst_ref=self.landed[term][stage],
            send_sem=self.send_sems.at[sem],
            recv_sem=self.recv_sems.at[sem],
            device_id=partner(*order[stage]),
            device_id_type=pl.DeviceIdType.MESH,
        )

    def keep(self, term):
        source = self.before(term, 0).at[self.half(term, 0, False)]
        return pltpu.make_async_copy(source, self.kept[term], self.kept_sems.at[term])

    def start(self, term, stage):
        self.send(term, stage).start()
        if stage == 0 and not self.near:
            self.keep(term).start()

    def finish(self, term, stage):
        self.send(term, stage).wait_recv()
        if stage == 0 and not self.near:
            self.keep(term).wait()
        landed = self.landed[term][stage]
        depth = len(self.terms[term][3]) - 1 - stage
        if stage == 0 and not self.near:
            other, chosen = self.kept[term], (slice(None),) * depth
        else:
            other, chosen = self.before(term, stage), self.half(term, stage, False)
        if depth == 0:
            total = landed[...].astype(jnp.float32) + other[chosen].astype(jnp.float32)
            self.outs[term][...] = total
            return

        def add(block, carry):
            at = [(block >> k) & 1 for k in reversed(range(depth))]
            rest = iter(at)
            there = [next(rest, c) if isinstance(c, slice) else c for c in chosen]
            total = landed[tuple(at)].astype(jnp.float32) + other[tuple(there)].astype(jnp.float32)
            landed[tuple(at)] = total.astype(landed.dtype)
            return carry

        lax.fori_loop(0, 1 << depth, add, 0)

    def step(self, stage, terms=None):
        for term in range(len(self.terms)) if terms is None else terms:
            stages = len(self.terms[term][3])
            if 0 <= stage < stages:
                self.finish(term, stage)
            if stage + 1 < stages:
                self.start(term, stage + 1)

    def settle(self):
        for term, (_, _, _, order) in enumerate(self.terms):
            for stage in range(len(order)):
                self.send(term, stage).wait_send()


class Scatter:
    def __init__(self, groups, near=False):
        self.near = near
        self.terms, self.arrays = [], []
        shapes, dtypes = [], []
        for which, (array, runs, orders) in enumerate(groups):
            lead = 1 << len(orders[0])
            columns = array.shape[-1]
            block = (array.size // columns // lead, columns)
            self.arrays.append(array if near else array.reshape((2,) * len(orders[0]) + block))
            for start, size in runs:
                order = orders[len(self.terms) % len(orders)]
                self.terms.append((which, start, size, order))
                shapes.append((size, columns))
                dtypes.append(array.dtype)
        like = [(s, d, len(t[3])) for s, d, t in zip(shapes, dtypes, self.terms)]
        kept = [pltpu.VMEM((2,) * (n - 1) + s, d) for s, d, n in like]
        landed = [pltpu.VMEM((2,) * (n - 1 - k) + s, d) for s, d, n in like for k in range(n)]
        copies = sum(n for _, _, n in like)
        self.in_specs = [] if near else [pl.BlockSpec(memory_space=pl.ANY)] * len(groups)
        self.out_specs = [whole_block(s) for s in shapes]
        self.out_shape = [jax.ShapeDtypeStruct(s, jnp.float32) for s in shapes]
        self.scratch = ([] if near else kept) + landed + [pltpu.SemaphoreType.DMA((copies,))] * 2
        if not near:
            self.scratch += [pltpu.SemaphoreType.DMA((len(self.terms),))]

    def bind(self, sources, outs, scratch):
        return Halving(self.terms, sources, outs, scratch, self.near)

    def results(self, outs):
        found = {}
        for (which, _, _, _), out in zip(self.terms, outs):
            found.setdefault(which, []).append(out)
        return [jnp.concatenate(found[k], axis=0) for k in sorted(found)]


def beside(kernel, work, counts, schedule, steps):
    n_in, n_out, n_scratch = counts

    def run(*refs):
        cuts = [0, n_in, len(work.in_specs), n_out, len(work.out_specs), n_scratch]
        at = [sum(cuts[: k + 1]) for k in range(len(cuts))]
        ins, sources, outs, sums, own = (refs[a:b] for a, b in zip(at[:-1], at[1:]))
        moving = work.bind(sources, sums, refs[at[-1] :])
        step = pl.program_id(0)
        for place in sorted({0, *schedule}):

            @pl.when(step == place)
            def _(place=place):
                if place == 0:
                    greet_partners()
                    moving.step(-1)
                for stage, when in enumerate(schedule):
                    if when == place:
                        moving.step(stage)

        kernel(*ins, *outs, *own)

        @pl.when(step == steps - 1)
        def _():
            for stage in range(len(schedule), moving.stages):
                moving.step(stage)
            moving.settle()

    return run


def alone_kernel(work, *refs):
    n, m = len(work.in_specs), len(work.out_specs)
    moving = work.bind(refs[:n], refs[n : n + m], refs[n + m :])
    greet_partners()
    for stage in range(-1, moving.stages):
        moving.step(stage)
    moving.settle()


def alone(work, collective_id):
    outs = pl.pallas_call(
        functools.partial(alone_kernel, work),
        in_specs=work.in_specs,
        out_specs=work.out_specs,
        out_shape=work.out_shape,
        scratch_shapes=work.scratch,
        compiler_params=params(collective_id=collective_id, has_side_effects=True),
        name="gather_weights",
    )(*work.arrays)
    return work.results(outs)


class Doubling:
    def __init__(self, source, landed, send_sems, recv_sems):
        self.buffers = [source, *landed]
        self.send_sems, self.recv_sems = send_sems, recv_sems

    def swap(self, stage):
        return pltpu.make_async_remote_copy(
            src_ref=self.buffers[stage],
            dst_ref=self.buffers[stage + 1],
            send_sem=self.send_sems.at[stage],
            recv_sem=self.recv_sems.at[stage],
            device_id=partner(*cube_dims()[stage]),
            device_id_type=pl.DeviceIdType.MESH,
        )

    def step(self, stage):
        if stage >= 0:
            self.swap(stage).wait_recv()
            self.buffers[stage + 1][...] += self.buffers[stage][...]
        if stage + 2 < len(self.buffers):
            self.swap(stage + 1).start()

    def settle(self):
        for stage in range(len(self.buffers) - 1):
            self.swap(stage).wait_send()


def doubling_scratch(shape):
    stages = len(cube_dims())
    return [pltpu.VMEM(shape, jnp.float32)] * (stages + 1) + [pltpu.SemaphoreType.DMA((stages,))] * 2


def on_device(
    image_tokens, text_states, text_segments, image_segment, out_grad,
    norm1_gain, norm1_bias, self_query, self_key, self_value, self_output,
    norm2_gain, norm2_bias, cross_query, cross_key, cross_value, cross_output,
    norm3_gain, norm3_bias, mlp_in, mlp_in_bias, mlp_out, mlp_out_bias,
):
    tokens = image_tokens[0]
    rows, width = tokens.shape
    hidden = mlp_in.shape[1]
    chunk = hidden // MLP_STEPS
    vectors = (
        norm1_gain, norm1_bias, norm2_gain, norm2_bias,
        norm3_gain, norm3_bias, mlp_in_bias, mlp_out_bias,
    )
    sizes = [v.shape[0] for v in vectors]
    shard = self_query.shape[0]
    owners = width // shard
    parts = hidden // width
    matrices = (
        self_query, self_key, self_value,
        self_output, cross_query, cross_key, cross_value, cross_output,
    )
    orders = halving_orders()
    spread = [order[::-1] for order in orders]
    down_shard = mlp_out.shape[0]
    first_pack = jnp.concatenate([*matrices[:3], pack_vectors(vectors)], axis=0)
    cross_pack = jnp.concatenate([mlp_out, *matrices[3:]], axis=0)
    up_pack = jnp.concatenate(
        [mlp_in[:, width * k : width * (k + 1)] for k in range(parts)], axis=0
    )
    first, text_full = alone(
        Gather(
            [
                (first_pack, row_pieces(first_pack.shape[0], 6), spread),
                (text_states[0], [(0, text_states.shape[1])], [cube_dims(("narrow",))]),
            ]
        ),
        1,
    )
    text_full = text_full.reshape(-1, width)

    def matrix(source, index):
        if shard % 16 == 0:
            spec = pl.BlockSpec(
                (owners, shard, width), lambda *_: (0, index, 0), pipeline_mode=pl.Buffered(1)
            )
            return source, spec
        taken = source[:, shard * index : shard * (index + 1)].reshape(1, width, width)
        return taken, whole_block(taken.shape)

    def columns(source, index):
        if shard % 16 == 0:
            return source, pl.BlockSpec((owners, shard, 128), lambda p: (0, index, p))
        taken = source[:, shard * index : shard * (index + 1)].reshape(1, width, width)
        return taken, pl.BlockSpec((1, width, 128), lambda p: (0, 0, p))

    weights_one = [matrix(first, k) for k in range(3)]
    gain_one, bias_one, gain_two, bias_two, gain_three, bias_three, up_bias, down_bias = (
        take_vectors(first[:, 3 * shard :], sizes)
    )
    mask = (text_segments[0] == image_segment[0, 0]).astype(jnp.int32).reshape(-1, 1)

    (normed_one, queries, keys, values, mixed_self, sums_self), (second,) = attend(
        tokens, gain_one, bias_one, [columns(first, k) for k in range(3)],
        Gather([(cross_pack, row_pieces(cross_pack.shape[0], 6), spread)]),
        (1, 2, 3, 5), 2,
    )
    places = down_shard // shard
    weights_two = [matrix(second, places + k) for k in range(5)]
    (x1, h2, q2, a2, x2, h3, k2, v2), (third,) = middle(
        tokens, mixed_self, text_full, mask, (gain_two, bias_two, gain_three, bias_three), weights_two,
        Gather([(up_pack, row_pieces(up_pack.shape[0], 6), spread)]),
        (1, 2), 3,
    )
    if shard % 16 == 0:
        per = width // chunk
        up = (third, pl.BlockSpec((owners, shard, chunk), lambda c: (0, c // per, c % per)))
        down = (
            second,
            pl.BlockSpec((chunk // down_shard, down_shard, width), lambda c: (c, 0, 0)),
        )
    else:
        taken = [
            third[:, shard * k : shard * (k + 1)].reshape(1, width, width) for k in range(parts)
        ]
        up = (
            jnp.concatenate(taken, axis=2),
            pl.BlockSpec((1, width, chunk), lambda c: (0, 0, c)),
        )
        down = (
            second[:, :down_shard].reshape(1, hidden, width),
            pl.BlockSpec((1, chunk, width), lambda c: (0, c, 0)),
        )
    halves = row_pieces(shard, 2)
    near = 2 if shard % 16 == 0 else 0
    (
        block_out, dx2, grad_up_bias, grad_gain_three, grad_bias_three, grad_down_bias,
        grad_down, grad_up, near_sums,
    ) = mlp(
        x2, h3, out_grad[0], gain_three, up, up_bias, down, down_bias, near, halves, orders, 4
    )
    down_runs = row_pieces(down_shard, 8)
    cut = 6 if len(down_runs) == 8 else 1
    (
        dx1, grad_mixed, grad_self_out, grad_cross_query, grad_cross_key, grad_cross_value,
        grad_cross_out, text_term, grad_gain_two, grad_bias_two,
    ), (down_first,) = middle_back(
        dx2, x1, mixed_self, h2, q2, a2, k2, v2, text_full, mask, gain_two, weights_two,
        Scatter([(grad_down, down_runs[:cut], orders)]), (1,), 5,
    )
    groups = [(g, halves, orders) for g in grad_up]
    groups += [(grad_down, down_runs[cut:], orders)] if down_runs[cut:] else []
    groups += [
        (g, halves, orders)
        for g in (grad_self_out, grad_cross_query, grad_cross_key, grad_cross_value, grad_cross_out)
    ]
    groups.append((text_term, [(0, text_states.shape[1])], [cube_dims(("narrow",))]))
    (grad_queries, grad_keys, grad_values, *self_weights), sums = attend_back(
        queries, keys, values, grad_mixed, sums_self, normed_one, Scatter(groups), (1, 5), 6
    )
    grad_up = jnp.concatenate([*near_sums, *sums[: parts - near]], axis=1)
    grad_down = jnp.concatenate([down_first, *sums[parts - near : -6]], axis=0)
    (
        grad_self_out, grad_cross_query, grad_cross_key, grad_cross_value, grad_cross_out, text_grad,
    ) = sums[-6:]
    self_terms = (grad_queries, grad_keys, grad_values)
    others = jnp.concatenate(
        [
            jnp.zeros((2, width), jnp.float32),
            grad_gain_two, grad_bias_two, grad_gain_three, grad_bias_three, grad_down_bias,
            grad_up_bias.reshape(-1, width),
        ],
        axis=0,
    )
    others = jnp.pad(others, ((0, -others.shape[0] % 8), (0, 0)))
    (image_grad, vector_sums), (grad_self_query, grad_self_key, grad_self_value) = first_back(
        tokens, dx1, gain_one, others, weights_one, self_terms,
        Scatter([(g, halves, orders) for g in self_weights]), (1,), 7,
    )
    place = lax.axis_index(AXES)
    flat = vector_sums.reshape(-1)
    rows_of = (0, 1, 2, 3, 4, 5, 7, 6)
    vector_grads = [
        lax.dynamic_slice_in_dim(flat, row * width + place * size, size)
        for row, size in zip(rows_of, sizes)
    ]
    return (
        block_out[None], image_grad[None], text_grad[None],
        vector_grads[0], vector_grads[1],
        grad_self_query, grad_self_key, grad_self_value, grad_self_out,
        vector_grads[2], vector_grads[3],
        grad_cross_query, grad_cross_key, grad_cross_value, grad_cross_out,
        vector_grads[4], vector_grads[5],
        grad_up, vector_grads[6], grad_down, vector_grads[7],
    )


def solution(mesh):
    placed = (
        P(("wide", "narrow"), None, None),
        P("wide", "narrow", None),
        P("wide", None),
        P("wide", "narrow"),
        P(("wide", "narrow"), None, None),
        P(("wide", "narrow")),
        P(("wide", "narrow")),
        P(("wide", "narrow"), None),
        P(("wide", "narrow"), None),
        P(("wide", "narrow"), None),
        P(("wide", "narrow"), None),
        P(("wide", "narrow")),
        P(("wide", "narrow")),
        P(("wide", "narrow"), None),
        P(("wide", "narrow"), None),
        P(("wide", "narrow"), None),
        P(("wide", "narrow"), None),
        P(("wide", "narrow")),
        P(("wide", "narrow")),
        P(("wide", "narrow"), None),
        P(("wide", "narrow")),
        P(("wide", "narrow"), None),
        P(("wide", "narrow")),
    )
    return jax.shard_map(
        on_device,
        mesh=mesh,
        in_specs=placed,
        out_specs=(
            P(("wide", "narrow"), None, None),
            P(("wide", "narrow"), None, None),
            P("wide", "narrow", None),
            P(("wide", "narrow")),
            P(("wide", "narrow")),
            P(("wide", "narrow"), None),
            P(("wide", "narrow"), None),
            P(("wide", "narrow"), None),
            P(("wide", "narrow"), None),
            P(("wide", "narrow")),
            P(("wide", "narrow")),
            P(("wide", "narrow"), None),
            P(("wide", "narrow"), None),
            P(("wide", "narrow"), None),
            P(("wide", "narrow"), None),
            P(("wide", "narrow")),
            P(("wide", "narrow")),
            P(("wide", "narrow"), None),
            P(("wide", "narrow")),
            P(("wide", "narrow"), None),
            P(("wide", "narrow")),
        ),
        check_vma=False,
    )
```

time: 646 us -> 558 us (0.86)
  waiting for transfers between devices: 44.3 us -> 0 us
  Pallas kernels: 530 us -> 504 us
  between operations: 15.6 us -> 2.16 us
  starting transfers between devices: 8.14 us -> 0 us
    all_gather x1 -> x0, waiting for transfers between devices: 43.7 us -> none  [gather_rows(): whole = lax.all_gather(packed, AXES, axis=0, tiled=True)]
    pallas_call x12 -> x7, Pallas kernels: 530 us -> 504 us  [the longest x1 106 us: attend(): pl.pallas_call(beside(attend_kernel, work, (6, 6, 0), schedule, pairs), g...]
    ppermute x6 -> x0, starting transfers between devices: 8.1 us -> none  [swap_narrow(): lax.ppermute(block, 'narrow', [(i, i ^ offset) for i in range(count)])]
    unnamed x75 -> x67, local copies, waits for them, and re-layouts: 15 us -> 13.9 us
  transfers between devices with their start and end apart: 7 -> 0, of which waited for: 2 -> 0; matrix products, arithmetic and copies ran while one was open for 2% -> 0% of each run, Pallas kernels for 20% -> 0%
where the time goes in v3:
time: 558 us; the launch traced here: 548 us
  Pallas kernels  504 us (90%)
  local copies, waits for them, and re-layouts  29.6 us (5%)
  other arithmetic  12.3 us (2%)
    pallas_call x1, Pallas kernels, attend(): pl.pallas_call(beside(attend_kernel, work, (6, 6, 0), schedule, pairs), g...  106 us
    pallas_call x1, Pallas kernels, mlp(): pl.pallas_call(functools.partial(mlp_kernel, near, far, work), grid=(MLP_...  87.2 us
    pallas_call x1, Pallas kernels, attend_back(): pl.pallas_call(beside(attend_back_kernel, work, (6, 6, 3), schedule, step...  86.5 us
    pallas_call x1, Pallas kernels, middle_back(): pl.pallas_call(beside(middle_back_kernel, work, (16, 10, 6), schedule, ro...  67.9 us
    pallas_call x1, Pallas kernels, middle(): pl.pallas_call(beside(middle_kernel, work, (13, 8, 0), schedule, rows //...  63 us
    pallas_call x1, Pallas kernels, alone(): pl.pallas_call(functools.partial(alone_kernel, work), in_specs=work.in_sp...  47.1 us
    pallas_call x1, Pallas kernels, first_back(): pl.pallas_call(functools.partial(first_back_kernel, work, schedule, steps...  45.9 us
    unnamed x67, local copies, waits for them, and re-layouts  13.9 us

profile of v3, /device:TPU:0, one launch (start us, length us, event | category | flops | bytes accessed | tf_op | source)
XLA Modules:
  0.0 547.8 jit_solution(9909677514034127431)
XLA Ops:
  0.7 5.4 concatenate.57
  6.1 1.6 pad_maximum_fusion.1.refs_0_
  7.7 47.1 %gather_weights.1 = (bf16[2,2,2,2,2,112,1024]{6,5,4,3,2,1,0:T(8,128)(2,1)}, bf16[2,2,32,1024]{3,2,1,0:T(8,128)(2,1)}) custom-call(bf16[112,1024]{1,0:T(8,128)(2,1)} %pad_maximum_fusion.1.refs_0_, bf16[32,1024]{1,0:T(8,128)(2,1)} %bitcast.79), custom_call_target="tpu_custom_call" | custom-call | tf_op jit(solution)/shard_map/gather_weights/pallas_call | solution.py:890
  54.9 0.0 copy-start.3
  54.9 0.0 copy-start.10
  54.9 0.0 copy-start.11
  54.9 0.0 copy-start.12
  54.9 1.4 slice.52
  56.3 0.0 copy-start.13
  56.3 0.0 copy-start.14
  56.3 0.6 copy.46
  56.9 0.1 slice_convert_fusion
  57.0 0.7 reshape.257.refs_1_.gain_ref
  57.6 0.7 reshape.258.refs_2_
  58.3 0.0 copy-done.3
  58.3 0.0 copy-done.10
  58.4 0.0 copy-done.11
  58.4 0.0 copy-done.12
  58.4 0.0 copy-done.13
  58.4 0.0 copy-done.14
  58.5 0.0 copy-start.2
  58.5 0.8 copy-done.2
  59.3 106.1 %self_attend.1 = (bf16[1024,1024]{1,0:T(8,128)(2,1)}, bf16[1024,1024]{1,0:T(8,128)(2,1)}, bf16[1024,1024]{1,0:T(8,128)(2,1)}, bf16[1024,1024]{1,0:T(8,128)(2,1)}...) custom-call(bf16[1024,1024]{1,0:T(8,128)(2,1)} %bitcast.51, ...), custom_call_target="tpu_custom_call" | custom-call | tf_op jit(solution)/shard_map/self_attend/pallas_call | solution.py:138
  165.5 0.7 pad_maximum_fusion.refs_13_
  166.2 0.7 reshape.260.refs_4_.refs_10_
  166.9 0.7 reshape.262.refs_6_.gain_ref
  167.5 0.7 reshape.261.refs_5_
  168.2 0.7 reshape.263.refs_7_
  169.5 0.7 copy.44.refs_3_.refs_9_
  170.3 63.0 %output_and_cross.1 = (f32[1024,1024]{1,0:T(8,128)}, bf16[1024,1024]{1,0:T(8,128)(2,1)}, bf16[1024,1024]{1,0:T(8,128)(2,1)}, bf16[1024,1024]{1,0:T(8,128)(2,1)},...) custom-call(bf16[1024,1024]{1,0:T(8,128)(2,1)} %bitcast.52, ...), custom_call_target="tpu_custom_call" | custom-call | tf_op jit(solution)/shard_map/output_and_cross/pallas_call | solution.py:425
  233.2 0.7 reshape.265.db_ref
  233.9 0.7 slice_convert_fusion.1
  234.6 87.2 %mlp_both_ways.1 = (bf16[1024,1024]{1,0:T(8,128)(2,1)}, f32[1024,1024]{1,0:T(8,128)}, f32[1,4096]{1,0:T(1,128)}, f32[1,1024]{1,0:T(1,128)}, f32[1,1024]{1,0:T(1,...) custom-call(f32[1024,1024]{1,0:T(8,128)} %get-tuple-element.103.x_re, ...), custom_call_target="tpu_custom_call" | custom-call | tf_op jit(solution)/shard_map/mlp_both_ways/pallas_call | solution.py:340
  321.8 67.9 %cross_back.1 = (f32[1024,1024]{1,0:T(8,128)}, bf16[1024,1024]{1,0:T(8,128)(2,1)}, bf16[1024,1024]{1,0:T(8,128)(2,1)}, bf16[1024,1024]{1,0:T(8,128)(2,1)}, bf16[...) custom-call(f32[1024,1024]{1,0:T(8,128)} %get-tuple-element.107.refs, ...), custom_call_target="tpu_custom_call" | custom-call | tf_op jit(solution)/shard_map/cross_back/pallas_call | solution.py:511
  389.8 0.8 constant_dynamic-update-slice_fusion.13
  390.6 0.8 constant_dynamic-update-slice_fusion.12
  391.5 0.8 constant_dynamic-update-slice_fusion.11
  392.3 0.8 constant_dynamic-update-slice_fusion.10
  393.1 0.8 constant_dynamic-update-slice_fusion.9
  394.0 0.8 constant_dynamic-update-slice_fusion.8
  394.9 86.5 %self_attend_back.1 = (bf16[1024,1024]{1,0:T(8,128)(2,1)}, bf16[1024,1024]{1,0:T(8,128)(2,1)}, bf16[1024,1024]{1,0:T(8,128)(2,1)}, bf16[1024,1024]{1,0:T(8,128)(...) custom-call(bf16[1024,1024]{1,0:T(8,128)(2,1)} %get-tuple-element.12, ...), custom_call_target="tpu_custom_call" | custom-call | tf_op jit(solution)/shard_map/self_attend_back/pallas_call | solution.py:212
  481.4 0.8 constant_dynamic-update-slice_fusion.7
  482.3 0.8 constant_dynamic-update-slice_fusion.6
  483.1 0.0 copy-done.6
  483.2 1.9 maximum_maximum_fusion
  485.1 1.7 pad_maximum_fusion.7
  486.7 1.7 pad_maximum_fusion.5
  488.4 0.5 broadcast.16
  488.9 0.7 reduce.3
  489.7 0.2 concatenate.61
  489.8 0.6 pad.9.vectors_ref
  490.5 45.9 %self_norm_back.1 = (f32[1024,1024]{1,0:T(8,128)}, f32[16,1024]{1,0:T(8,128)}, f32[16,1024]{1,0:T(8,128)}, f32[16,1024]{1,0:T(8,128)}, f32[16,1024]{1,0:T(8,128)...) custom-call(bf16[1024,1024]{1,0:T(8,128)(2,1)} %bitcast.53, ...), custom_call_target="tpu_custom_call" | custom-call | tf_op jit(solution)/shard_map/self_norm_back/pallas_call | solution.py:590
  536.4 0.0 copy-done.18
  536.4 0.0 copy-done.15
  536.4 0.0 copy-done.16
  536.4 1.6 pad_maximum_fusion.4
  538.0 1.7 pad_maximum_fusion.2
  539.7 0.9 copy.47
  540.5 0.6 fusion.2
  541.2 0.6 dynamic_slice.30
  541.8 1.3 copy.64
  543.1 1.6 copy-done
  544.7 2.0 copy.65
  546.7 0.7 copy.66
  (43 shorter events, 0.2 us)
Async XLA Ops:
  54.9 3.5 copy-start.3
  54.9 3.5 copy-start.10
  54.9 3.5 copy-start.11
  54.9 3.5 copy-start.12
  56.3 2.1 copy-start.13
  56.3 2.2 copy-start.14
  58.5 0.8 copy-start.2
  59.3 106.1 %copy-start.4 = (bf16[32,4096]{1,0:T(8,128)(2,1)S(1)}, bf16[32,4096]{1,0:T(8,128)(2,1)}, u32[]{:S(2)}) copy-start(bf16[32,4096]{1,0:T(8,128)(2,1)} %param.42) | copy-start | bytes 786436
  59.3 110.2 %copy-start.24 = (s32[1,128]{1,0:T(1,128)S(1)}, s32[1,128]{1,0:T(1,128)}, u32[]{:S(2)}) copy-start(s32[1,128]{1,0:T(1,128)} %param.25) | copy-start | bytes 1540
  394.8 88.3 %copy-start.6 = (f32[16,1024]{1,0:T(8,128)S(1)}, f32[16,1024]{1,0:T(8,128)}, u32[]{:S(2)}) copy-start(f32[16,1024]{1,0:T(8,128)} %get-tuple-element.161) | copy-start | bytes 196612
  394.8 88.3 %copy-start.7 = (f32[16,1024]{1,0:T(8,128)S(1)}, f32[16,1024]{1,0:T(8,128)}, u32[]{:S(2)}) copy-start(f32[16,1024]{1,0:T(8,128)} %get-tuple-element.162) | copy-start | bytes 196612
  394.8 88.3 %copy-start.8 = (f32[16,1024]{1,0:T(8,128)S(1)}, f32[16,1024]{1,0:T(8,128)}, u32[]{:S(2)}) copy-start(f32[16,1024]{1,0:T(8,128)} %get-tuple-element.163) | copy-start | bytes 196612
  394.8 88.3 %copy-start.9 = (f32[16,1024]{1,0:T(8,128)S(1)}, f32[16,1024]{1,0:T(8,128)}, u32[]{:S(2)}) copy-start(f32[16,1024]{1,0:T(8,128)} %get-tuple-element.164) | copy-start | bytes 196612
  481.4 7.5 %copy-start.17 = (f32[1,4096]{1,0:T(1,128)S(1)}, f32[1,4096]{1,0:T(1,128)}, u32[]{:S(2)}) copy-start(f32[1,4096]{1,0:T(1,128)} %get-tuple-element.121) | copy-start | bytes 49156
  481.4 8.2 %copy-start.19 = (f32[1,1024]{1,0:T(1,128)S(1)}, f32[1,1024]{1,0:T(1,128)}, u32[]{:S(2)}) copy-start(f32[1,1024]{1,0:T(1,128)} %get-tuple-element.118) | copy-start | bytes 12292
  481.4 8.2 %copy-start.20 = (f32[1,1024]{1,0:T(1,128)S(1)}, f32[1,1024]{1,0:T(1,128)}, u32[]{:S(2)}) copy-start(f32[1,1024]{1,0:T(1,128)} %get-tuple-element.119) | copy-start | bytes 12292
  481.4 8.2 %copy-start.21 = (f32[1,1024]{1,0:T(1,128)S(1)}, f32[1,1024]{1,0:T(1,128)}, u32[]{:S(2)}) copy-start(f32[1,1024]{1,0:T(1,128)} %get-tuple-element.120) | copy-start | bytes 12292
  481.4 8.2 %copy-start.22 = (f32[1,1024]{1,0:T(1,128)S(1)}, f32[1,1024]{1,0:T(1,128)}, u32[]{:S(2)}) copy-start(f32[1,1024]{1,0:T(1,128)} %get-tuple-element.116) | copy-start | bytes 12292
  481.4 8.2 %copy-start.23 = (f32[1,1024]{1,0:T(1,128)S(1)}, f32[1,1024]{1,0:T(1,128)}, u32[]{:S(2)}) copy-start(f32[1,1024]{1,0:T(1,128)} %get-tuple-element.117) | copy-start | bytes 12292
  483.1 53.3 %copy-start.18 = (f32[128,1024]{1,0:T(8,128)}, f32[128,1024]{1,0:T(8,128)S(1)}, u32[]{:S(2)}) copy-start(f32[128,1024]{1,0:T(8,128)S(1)} %constant_dynamic-update-slice_fusion.6) | copy-start | bytes 1572868
  490.5 45.9 %copy-start.15 = (f32[16,1024]{1,0:T(8,128)S(1)}, f32[16,1024]{1,0:T(8,128)}, u32[]{:S(2)}) copy-start(f32[16,1024]{1,0:T(8,128)} %get-tuple-element.159) | copy-start | bytes 196612
  490.5 45.9 %copy-start.16 = (f32[16,1024]{1,0:T(8,128)S(1)}, f32[16,1024]{1,0:T(8,128)}, u32[]{:S(2)}) copy-start(f32[16,1024]{1,0:T(8,128)} %get-tuple-element.160) | copy-start | bytes 196612
  490.5 51.3 %copy-start.1 = (bf16[1024,1024]{1,0:T(8,128)(2,1)S(1)}, bf16[1024,1024]{1,0:T(8,128)(2,1)}, u32[]{:S(2)}) copy-start(bf16[1024,1024]{1,0:T(8,128)(2,1)} %get-tuple-element.106) | copy-start | bytes 6291460
  541.8 2.9 copy-start
  544.7 2.0 copy-start.5

commit v4 on v3

v4 whole, which is shorter than its diff:
```python
import functools
import math

import jax
import jax.numpy as jnp
from jax import lax
from jax.experimental import pallas as pl
from jax.experimental.pallas import tpu as pltpu
from jax.sharding import PartitionSpec as P

HEAD_DIM = 64
TILE = 256
BF16 = jnp.bfloat16
VMEM_LIMIT = 60 * 1024 * 1024
MLP_STEPS = 8

EPSILON = 1e-05
NEGATIVE = -1e30

AXES = ("wide", "narrow")


def axis_bits(axis):
    return lax.axis_size(axis).bit_length() - 1


def pack_vectors(vectors):
    room = 1024
    placed = [
        jnp.pad(v.astype(jnp.float32), (128 * k, room - 128 * k - v.shape[0]))
        for k, v in enumerate(vectors)
    ]
    return sum(placed).reshape(-1, 128)


def nn(a, b):
    return lax.dot_general(a, b, (((1,), (0,)), ((), ())), preferred_element_type=jnp.float32)


def nt(a, b):
    return lax.dot_general(a, b, (((1,), (1,)), ((), ())), preferred_element_type=jnp.float32)


def tn(a, b):
    return lax.dot_general(a, b, (((0,), (0,)), ((), ())), preferred_element_type=jnp.float32)


def standardize(values):
    center = jnp.mean(values, axis=-1, keepdims=True)
    offset = values - center
    rate = lax.rsqrt(jnp.mean(offset * offset, axis=-1, keepdims=True) + EPSILON)
    return offset * rate, rate


def norm_back(standard, rate, gain, grad):
    scaled = grad * gain
    return rate * (
        scaled
        - jnp.mean(scaled, axis=-1, keepdims=True)
        - standard * jnp.mean(scaled * standard, axis=-1, keepdims=True)
    )


def column_sum(values):
    return jnp.sum(values, axis=0, keepdims=True)


def head_lanes(block, head):
    lane = lax.broadcasted_iota(jnp.int32, block.shape, 1)
    inside = (lane >= HEAD_DIM) if head else (lane < HEAD_DIM)
    return jnp.where(inside, block, jnp.zeros_like(block))


def whole_block(shape):
    zeros = (0,) * len(shape)
    return pl.BlockSpec(shape, lambda *_: zeros, pipeline_mode=pl.Buffered(1))


def params(**extra):
    return pltpu.CompilerParams(vmem_limit_bytes=VMEM_LIMIT, **extra)


def attend_kernel(
    x_ref, vectors_ref, wq_ref, wk_ref, wv_ref, h_ref, q_ref, k_ref, v_ref, o_ref, sums_ref,
    hook,
):
    rows = x_ref.shape[0]

    @pl.when(pl.program_id(0) == 0)
    def _():
        for start in range(0, rows, TILE):
            at = slice(start, start + TILE)
            standard, _ = standardize(x_ref[at, :].astype(jnp.float32))
            h_ref[at, :] = (standard * vectors_ref[0:1, :] + vectors_ref[1:2, :]).astype(BF16)

    weights = jnp.concatenate([w[...] for w in (wq_ref, wk_ref, wv_ref)], axis=1)
    mapped = nn(h_ref[...], weights).astype(BF16)
    q_ref[...] = mapped[:, :128]
    k_ref[...] = mapped[:, 128:256]
    v_ref[...] = mapped[:, 256:]
    flipped = v_ref[...].T
    for start in range(0, rows, TILE):
        span = start + TILE
        queries = q_ref[start:span, :] * (HEAD_DIM**-0.5)
        keys = k_ref[:span, :]
        mixed, sums = [], []
        for head in range(2):
            scores = nt(keys, head_lanes(queries, head))
            key_at = lax.broadcasted_iota(jnp.int32, (TILE, TILE), 0)
            query_at = lax.broadcasted_iota(jnp.int32, (TILE, TILE), 1)
            corner = jnp.where(key_at <= query_at, scores[start:], NEGATIVE)
            scores = jnp.concatenate([scores[:start], corner], axis=0) if start else corner
            top = jnp.max(scores, axis=0, keepdims=True)
            powers = jnp.exp(scores - top)
            total = jnp.sum(powers, axis=0, keepdims=True)
            part = nn(flipped[HEAD_DIM * head : HEAD_DIM * (head + 1), :span], powers.astype(BF16))
            mixed.append(part * (1.0 / total))
            sums.append(top + jnp.log(total))
        o_ref[start:span, :] = jnp.concatenate(mixed, axis=0).T.astype(BF16)
        sums_ref[0, :, start:span] = jnp.concatenate(sums, axis=0)


def attend(tokens, vectors, weights, work, schedule, collective_id):
    rows, width = tokens.shape
    pairs = width // 128
    block = pl.BlockSpec((rows, 128), lambda p: (0, p))
    like = jax.ShapeDtypeStruct(tokens.shape, BF16)
    results = pl.pallas_call(
        beside(attend_kernel, work, (5, 6, 0), schedule, pairs),
        grid=(pairs,),
        in_specs=[whole_block(tokens.shape), whole_block(vectors.shape)]
        + [pl.BlockSpec((width, 128), lambda p: (0, p))] * 3
        + work.in_specs,
        out_specs=[whole_block(tokens.shape)]
        + [block] * 4
        + [pl.BlockSpec((1, 2, rows), lambda p: (p, 0, 0))]
        + work.out_specs,
        out_shape=[like] * 5
        + [jax.ShapeDtypeStruct((pairs, 2, rows), jnp.float32)]
        + work.out_shape,
        scratch_shapes=work.scratch,
        compiler_params=params(collective_id=collective_id, has_side_effects=True),
        name="self_attend",
    )(tokens, vectors, *weights, *work.arrays)
    return results[:6], work.results(results[6:])


def attend_back_kernel(
    q_ref, k_ref, v_ref, da_ref, sums_ref, h_ref, dk2_ref, dv2_ref, text_ref, ck_ref, cv_ref,
    dq_ref, dk_ref, dv_ref, dwq_ref, dwk_ref, dwv_ref, dck_ref, dcv_ref, dtext_ref,
    dk_sum, dv_sum, h_flip, hook,
):
    rows, width = q_ref.shape

    @pl.when(pl.program_id(0) == 0)
    def _():
        h_flip[...] = h_ref[...].T
        dck_ref[...] = tn(text_ref[...], dk2_ref[...]).astype(BF16)
        dcv_ref[...] = tn(text_ref[...], dv2_ref[...]).astype(BF16)
        dtext_ref[...] = nt(dk2_ref[...], ck_ref[...]) + nt(dv2_ref[...], cv_ref[...])

    flipped = k_ref[...].T
    for start in reversed(range(0, rows, TILE)):
        if start == TILE:
            hook(1)
        span = start + TILE
        queries = q_ref[start:span, :] * (HEAD_DIM**-0.5)
        grads = da_ref[start:span, :]
        keys = k_ref[:span, :]
        values = v_ref[:span, :]
        parts = []
        for head in range(2):
            own_queries = head_lanes(queries, head)
            own_grads = head_lanes(grads, head)
            scores = nt(keys, own_queries)
            key_at = lax.broadcasted_iota(jnp.int32, (TILE, TILE), 0)
            query_at = lax.broadcasted_iota(jnp.int32, (TILE, TILE), 1)
            corner = jnp.where(key_at <= query_at, scores[start:], NEGATIVE)
            scores = jnp.concatenate([scores[:start], corner], axis=0) if start else corner
            probs = jnp.exp(scores - sums_ref[0, head : head + 1, start:span])
            grad_probs = nt(values, own_grads)
            inner = jnp.sum(probs * grad_probs, axis=0, keepdims=True)
            grad_scores = (probs * (grad_probs - inner)).astype(BF16)
            value_term = nn(probs.astype(BF16), own_grads)
            key_term = nn(grad_scores, own_queries)
            if span == rows and head == 0:
                dv_sum[...] = value_term
                dk_sum[...] = key_term
            else:
                dv_sum[:span, :] += value_term
                dk_sum[:span, :] += key_term
            parts.append(nn(flipped[HEAD_DIM * head : HEAD_DIM * (head + 1), :span], grad_scores))
        dq = jnp.concatenate(parts, axis=0).T * (HEAD_DIM**-0.5)
        dq_ref[start:span, :] = dq.astype(BF16)
    dk_ref[...] = dk_sum[...].astype(BF16)
    dv_ref[...] = dv_sum[...].astype(BF16)
    grads = jnp.concatenate([dq_ref[...], dk_ref[...], dv_ref[...]], axis=1)
    weights = nn(h_flip[...], grads).astype(BF16)
    dwq_ref[...] = weights[:, :128]
    dwk_ref[...] = weights[:, 128:256]
    dwv_ref[...] = weights[:, 256:]


def attend_back(queries, keys, values, grads, sums, normed, cross, work, schedule, collective_id):
    rows, width = queries.shape
    steps = width // 128
    block = pl.BlockSpec((rows, 128), lambda p: (0, p))
    results = pl.pallas_call(
        beside(attend_back_kernel, work, (11, 9, 3), schedule, steps),
        grid=(steps,),
        in_specs=[block] * 4
        + [pl.BlockSpec((1, 2, rows), lambda p: (p, 0, 0)), whole_block(normed.shape)]
        + [whole_block(c.shape) for c in cross]
        + work.in_specs,
        out_specs=[block] * 6
        + [whole_block((width, width))] * 2
        + [whole_block(cross[2].shape)]
        + work.out_specs,
        out_shape=[jax.ShapeDtypeStruct(queries.shape, BF16)] * 3
        + [jax.ShapeDtypeStruct((width, width), BF16)] * 5
        + [jax.ShapeDtypeStruct(cross[2].shape, jnp.float32)]
        + work.out_shape,
        scratch_shapes=[pltpu.VMEM((rows, 128), jnp.float32)] * 2
        + [pltpu.VMEM((width, rows), BF16)]
        + work.scratch,
        compiler_params=params(collective_id=collective_id, has_side_effects=True),
        name="self_attend_back",
    )(queries, keys, values, grads, sums, normed, *cross, *work.arrays)
    return results[:9], work.results(results[9:])


def gelu_both(values):
    phi = 0.5 + 0.5 * lax.erf(values * (0.5**0.5))
    density = jnp.exp(-0.5 * values * values) * ((2.0 * math.pi) ** -0.5)
    return values * phi, phi + values * density


def mlp_kernel(
    near, far, pace, work, x_ref, h_ref, g_ref, vectors_ref, up_ref, ub_ref, down_ref,
    out_ref, dx_ref, dub_ref, dgain_ref, dbias_ref, gsum_ref, ddown_ref, *refs,
):
    far_refs, refs = refs[:far], refs[far:]
    sums, refs = refs[:near], refs[near:]
    out_sum, dh_sum, h_flip, act, grad_act = refs[:5]
    near_refs, refs = refs[5 : 5 + near], refs[5 + near :]
    step, steps = pl.program_id(0), pl.num_programs(0)
    rows = h_ref.shape[0]
    parts = near + far
    per = MLP_STEPS // parts
    moving = work.bind(near_refs, sums, refs) if near else None

    @pl.when(step == 0)
    def _():
        if near:
            greet_partners()
        h_flip[...] = h_ref[...].T
        out_sum[...] = x_ref[...] + vectors_ref[7:8, :]
        dh_sum[...] = jnp.zeros_like(dh_sum)

    left, due = [], {}
    for part in range(near):
        pieces = [k for k, p in enumerate(work.pieces) if p[0][0] == part]
        for at in range(-1, work.ticks):
            place = 2 * per * (part + 1) + pace[at + 1]
            if place < 2 * MLP_STEPS:
                due.setdefault(place, []).append((at, pieces))
            else:
                left.append((at, pieces))

    def move(half):
        for place in due:
            if place % 2 == half:

                @pl.when(step == place // 2)
                def _(place=place):
                    for at, pieces in due[place]:
                        tick(moving, at, pieces)

    move(0)
    up = up_ref[...]
    down = down_ref[...]
    bias_sum = jnp.zeros_like(dub_ref)
    for start in range(0, rows, TILE):
        at = slice(start, start + TILE)
        hidden, slope = gelu_both(nn(h_ref[at, :], up) + ub_ref[...])
        act[at, :] = hidden.astype(BF16)
        grad_pre = (nt(g_ref[at, :], down) * slope).astype(BF16)
        grad_act[at, :] = grad_pre
        bias_sum += column_sum(grad_pre.astype(jnp.float32))
        out_sum[at, :] += nn(act[at, :], down)
        dh_sum[at, :] += nt(grad_pre, up)
    dub_ref[...] = bias_sum
    move(1)
    grad_up = nn(h_flip[...], grad_act[...]).astype(BF16)
    chunk = grad_up.shape[1]
    for part, ref in enumerate(far_refs):

        @pl.when(step // per == near + part)
        def _(ref=ref):
            ref[...] = grad_up

    for place in range(near * per):

        @pl.when(step == place)
        def _(place=place):
            ref = near_refs[place // per]
            first = chunk * (place % per)
            ref[..., first : first + chunk] = grad_up.reshape(ref.shape[:-1] + (chunk,))

    ddown_ref[...] = tn(act[...], g_ref[...]).astype(BF16)

    @pl.when(step == steps - 1)
    def _():
        gain_sum = jnp.zeros_like(dgain_ref)
        grad_sum = jnp.zeros_like(dbias_ref)
        tail_sum = jnp.zeros_like(gsum_ref)
        for start in range(0, rows, TILE):
            at = slice(start, start + TILE)
            out_ref[at, :] = out_sum[at, :].astype(BF16)
            standard, rate = standardize(x_ref[at, :])
            grad = dh_sum[at, :]
            tail = g_ref[at, :].astype(jnp.float32)
            dx_ref[at, :] = tail + norm_back(standard, rate, vectors_ref[4:5, :], grad)
            gain_sum += column_sum(grad * standard)
            grad_sum += column_sum(grad)
            tail_sum += column_sum(tail)
        dgain_ref[...] = gain_sum
        dbias_ref[...] = grad_sum
        gsum_ref[...] = tail_sum
        for at, pieces in left:
            tick(moving, at, pieces)
        if near:
            settle(moving)


def mlp(x, h, g, vectors, up, up_bias, down, near, pace, orders, collective_id):
    rows, width = x.shape
    hidden = up_bias.shape[1]
    chunk = hidden // MLP_STEPS
    f32 = jnp.float32
    row = (1, width)
    parts = hidden // width
    per = width // chunk
    lead = (2,) * len(cube_dims())
    block = lead + (width >> len(lead), width)
    source = jax.ShapeDtypeStruct(block, BF16)
    work = Scatter([(source, orders, 1)] * near, near=True) if near else None
    far = parts - near
    pace = [*pace, *range(pace[-1] + 1, pace[-1] + 1 + len(cube_dims()))]
    results = pl.pallas_call(
        functools.partial(mlp_kernel, near, far, pace, work),
        grid=(MLP_STEPS,),
        in_specs=[
            whole_block(x.shape), whole_block(h.shape), whole_block(g.shape), whole_block(vectors.shape),
            pl.BlockSpec((width, chunk), lambda c: (0, c)),
            pl.BlockSpec((1, chunk), lambda c: (0, c)),
            pl.BlockSpec((chunk, width), lambda c: (c, 0)),
        ],
        out_specs=[
            whole_block(x.shape), whole_block(x.shape),
            pl.BlockSpec((1, chunk), lambda c: (0, c)),
            whole_block(row), whole_block(row), whole_block(row),
            pl.BlockSpec((chunk, width), lambda c: (c, 0)),
        ]
        + [
            pl.BlockSpec((width, chunk), lambda c, k=k: (0, jnp.clip(c - per * k, 0, per - 1)))
            for k in range(near, parts)
        ]
        + (work.out_specs if near else []),
        out_shape=[
            jax.ShapeDtypeStruct(x.shape, BF16), jax.ShapeDtypeStruct(x.shape, f32),
            jax.ShapeDtypeStruct((1, hidden), f32),
            jax.ShapeDtypeStruct(row, f32), jax.ShapeDtypeStruct(row, f32), jax.ShapeDtypeStruct(row, f32),
            jax.ShapeDtypeStruct((hidden, width), BF16),
        ]
        + [jax.ShapeDtypeStruct((width, width), BF16)] * far
        + (work.out_shape if near else []),
        scratch_shapes=[
            pltpu.VMEM(x.shape, f32), pltpu.VMEM(x.shape, f32), pltpu.VMEM((width, rows), BF16),
            pltpu.VMEM((rows, chunk), BF16), pltpu.VMEM((rows, chunk), BF16),
        ]
        + [pltpu.VMEM(block, BF16)] * near
        + (work.scratch if near else []),
        compiler_params=params(collective_id=collective_id, has_side_effects=True) if near else params(),
        name="mlp_both_ways",
    )(x, h, g, vectors, up, up_bias, down)
    sums = work.results(results[7 + far :]) if near else []
    return *results[:7], results[7 : 7 + far], sums


def stack_heads(pair):
    return jnp.concatenate([head_lanes(pair, 0), head_lanes(pair, 1)], axis=0)


def by_head(stacked):
    return stacked.reshape(2, stacked.shape[0] // 2, stacked.shape[1])


def caption_probs(keys, queries, mask):
    scores = by_head(jnp.where(mask != 0, nt(keys, queries), NEGATIVE))
    powers = jnp.exp(scores - jnp.max(scores, axis=1, keepdims=True))
    return powers * (1.0 / jnp.sum(powers, axis=1, keepdims=True))


def middle_kernel(
    x_ref, a_ref, text_ref, mask_ref, vectors_ref,
    wo_ref, cq_ref, ck_ref, cv_ref, co_ref,
    x1_ref, h2_ref, q2_ref, a2_ref, x2_ref, h3_ref, k2_ref, v2_ref, keys, values_flip,
    hook,
):
    @pl.when(pl.program_id(0) == 0)
    def _():
        k2_ref[...] = nn(text_ref[...], ck_ref[...]).astype(BF16)
        v2_ref[...] = nn(text_ref[...], cv_ref[...]).astype(BF16)
        for pair in range(keys.shape[0]):
            at = slice(128 * pair, 128 * (pair + 1))
            keys[pair] = stack_heads(k2_ref[:, at])
            values_flip[pair] = stack_heads(v2_ref[:, at]).T

    after_self = x_ref[...].astype(jnp.float32) + nn(a_ref[...], wo_ref[...])
    x1_ref[...] = after_self
    standard, _ = standardize(after_self)
    normed = (standard * vectors_ref[2:3, :] + vectors_ref[3:4, :]).astype(BF16)
    h2_ref[...] = normed
    q2_ref[...] = nn(normed, cq_ref[...]).astype(BF16)
    mask = mask_ref[...]
    for pair in range(q2_ref.shape[1] // 128):
        at = slice(128 * pair, 128 * (pair + 1))
        queries = q2_ref[:, at] * (HEAD_DIM**-0.5)
        probs = caption_probs(keys[pair], queries, mask).astype(BF16)
        mixed = nn(values_flip[pair], probs.reshape(-1, probs.shape[2]))
        a2_ref[:, at] = mixed.T.astype(BF16)
    hook(1)
    after_cross = after_self + nn(a2_ref[...], co_ref[...])
    x2_ref[...] = after_cross
    standard, _ = standardize(after_cross)
    h3_ref[...] = (standard * vectors_ref[4:5, :] + vectors_ref[5:6, :]).astype(BF16)


def middle(tokens, mixed, text, mask, vectors, weights, work, schedule, collective_id):
    rows, width = tokens.shape
    slots = text.shape[0]
    tile = pl.BlockSpec((TILE, width), lambda i: (i, 0))
    f32 = jnp.float32
    like = lambda dtype: jax.ShapeDtypeStruct(tokens.shape, dtype)
    results = pl.pallas_call(
        beside(middle_kernel, work, (10, 8, 2), schedule, rows // TILE),
        grid=(rows // TILE,),
        in_specs=[
            tile, tile, whole_block(text.shape), whole_block(mask.shape),
            whole_block(vectors.shape), *[whole_block(w.shape) for w in weights], *work.in_specs,
        ],
        out_specs=[tile] * 6 + [whole_block(text.shape)] * 2 + work.out_specs,
        out_shape=[like(f32), like(BF16), like(BF16), like(BF16), like(f32), like(BF16)]
        + [jax.ShapeDtypeStruct(text.shape, BF16)] * 2
        + work.out_shape,
        scratch_shapes=[
            pltpu.VMEM((width // 128, 2 * slots, 128), BF16),
            pltpu.VMEM((width // 128, 128, 2 * slots), BF16),
        ]
        + work.scratch,
        compiler_params=params(collective_id=collective_id, has_side_effects=True),
        name="output_and_cross",
    )(tokens, mixed, text, mask, vectors, *weights, *work.arrays)
    return results[:8], work.results(results[8:])


def middle_back_kernel(
    dx2_ref, x1_ref, a1_ref, h2_ref, q2_ref, a2_ref, k2_ref, v2_ref, mask_ref, vectors_ref,
    wo_ref, cq_ref, co_ref,
    dx1_ref, da1_ref, dwo_ref, dcq_ref, dco_ref, dk2_ref, dv2_ref, dgain_ref, dbias_ref,
    wo_sum, cq_sum, co_sum, dk_sum, dv_sum, dq2, keys, keys_flip, values,
    hook,
):
    step, steps = pl.program_id(0), pl.num_programs(0)
    pairs = keys.shape[0]
    slots = k2_ref.shape[0]

    @pl.when(step == 0)
    def _():
        for ref in (wo_sum, cq_sum, co_sum, dk_sum, dv_sum, dgain_ref, dbias_ref):
            ref[...] = jnp.zeros_like(ref)
        for pair in range(pairs):
            at = slice(128 * pair, 128 * (pair + 1))
            keys[pair] = stack_heads(k2_ref[:, at])
            keys_flip[pair] = keys[pair].T
            values[pair] = stack_heads(v2_ref[:, at])

    grad_out = dx2_ref[...].astype(BF16)
    co_sum[...] += tn(a2_ref[...], grad_out)
    grad_mixed = nt(grad_out, co_ref[...]).astype(BF16)
    mask = mask_ref[...]
    for pair in range(pairs):
        at = slice(128 * pair, 128 * (pair + 1))
        queries = q2_ref[:, at] * (HEAD_DIM**-0.5)
        grads = grad_mixed[:, at]
        probs = caption_probs(keys[pair], queries, mask)
        grad_probs = by_head(nt(values[pair], grads))
        inner = jnp.sum(probs * grad_probs, axis=1, keepdims=True)
        grad_scores = (probs * (grad_probs - inner)).astype(BF16).reshape(2 * slots, -1)
        dv_sum[pair] += nn(probs.astype(BF16).reshape(2 * slots, -1), grads)
        dk_sum[pair] += nn(grad_scores, queries)
        dq2[:, at] = (nn(keys_flip[pair], grad_scores).T * (HEAD_DIM**-0.5)).astype(BF16)
    hook(1)
    cq_sum[...] += tn(h2_ref[...], dq2[...])
    grad_normed = nt(dq2[...], cq_ref[...])
    standard, rate = standardize(x1_ref[...])
    grad_after = dx2_ref[...] + norm_back(standard, rate, vectors_ref[2:3, :], grad_normed)
    dgain_ref[...] += column_sum(grad_normed * standard)
    dbias_ref[...] += column_sum(grad_normed)
    dx1_ref[...] = grad_after
    grad_self = grad_after.astype(BF16)
    wo_sum[...] += tn(a1_ref[...], grad_self)
    da1_ref[...] = nt(grad_self, wo_ref[...]).astype(BF16)

    @pl.when(step == steps - 1)
    def _():
        dwo_ref[...] = wo_sum[...].astype(BF16)
        dcq_ref[...] = cq_sum[...].astype(BF16)
        dco_ref[...] = co_sum[...].astype(BF16)
        for pair in range(pairs):
            at = slice(128 * pair, 128 * (pair + 1))
            for total, ref in ((dk_sum, dk2_ref), (dv_sum, dv2_ref)):
                upper, lower = total[pair, :slots], total[pair, slots:]
                ref[:, at] = (head_lanes(upper, 0) + head_lanes(lower, 1)).astype(BF16)


def middle_back(
    dx2, x1, a1, h2, q2, a2, k2, v2, mask, vectors, weights, work, schedule, collective_id
):
    rows, width = x1.shape
    slots = k2.shape[0]
    pairs = width // 128
    tile = pl.BlockSpec((TILE, width), lambda i: (i, 0))
    f32 = jnp.float32
    matrix = (width, width)
    results = pl.pallas_call(
        beside(middle_back_kernel, work, (13, 9, 9), schedule, rows // TILE),
        grid=(rows // TILE,),
        in_specs=[tile] * 6
        + [whole_block(v.shape) for v in (k2, v2, mask, vectors, *weights)]
        + work.in_specs,
        out_specs=[tile] * 2
        + [whole_block(matrix)] * 3
        + [whole_block(k2.shape)] * 2
        + [whole_block((1, width))] * 2
        + work.out_specs,
        out_shape=[jax.ShapeDtypeStruct(x1.shape, f32), jax.ShapeDtypeStruct(x1.shape, BF16)]
        + [jax.ShapeDtypeStruct(matrix, BF16)] * 3
        + [jax.ShapeDtypeStruct(k2.shape, BF16)] * 2
        + [jax.ShapeDtypeStruct((1, width), f32)] * 2
        + work.out_shape,
        scratch_shapes=[pltpu.VMEM(matrix, f32)] * 3
        + [pltpu.VMEM((pairs, 2 * slots, 128), f32)] * 2
        + [
            pltpu.VMEM((TILE, width), BF16),
            pltpu.VMEM((pairs, 2 * slots, 128), BF16),
            pltpu.VMEM((pairs, 128, 2 * slots), BF16),
            pltpu.VMEM((pairs, 2 * slots, 128), BF16),
        ]
        + work.scratch,
        compiler_params=params(collective_id=collective_id, has_side_effects=True),
        name="cross_back",
    )(dx2, x1, a1, h2, q2, a2, k2, v2, mask, vectors, *weights, *work.arrays)
    return results[:9], work.results(results[9:])


def first_back_kernel(
    work, schedule, steps, x_ref, dx1_ref, given_ref, vectors_ref, wq_ref, wk_ref, wv_ref, dq_ref, dk_ref, dv_ref,
    *refs,
):
    n, m = len(work.in_specs), len(work.out_specs)
    sources, (dx_ref, vector_sum_ref), sums = refs[:n], refs[n : n + 2], refs[n + 2 : n + 2 + m]
    stages = len(cube_dims())
    rest = refs[n + 2 + m :]
    doubling = Doubling(rest[0], rest[1 : stages + 1], *rest[stages + 1 : stages + 3])
    halving = work.bind(sources, sums, rest[stages + 3 :])
    step = pl.program_id(0)
    vectors = doubling.buffers[0]

    @pl.when(step == 0)
    def _():
        greet_partners()
        tick(halving, -1)
        vectors[...] = vectors_ref[...]

    for at, place in enumerate(schedule):

        @pl.when(step == place)
        def _(at=at):
            tick(halving, at)

    grad_normed = (
        nt(dq_ref[...], wq_ref[...]) + nt(dk_ref[...], wk_ref[...]) + nt(dv_ref[...], wv_ref[...])
    )
    standard, rate = standardize(x_ref[...].astype(jnp.float32))
    dx_ref[...] = dx1_ref[...] + norm_back(standard, rate, given_ref[0:1, :], grad_normed)
    vectors[0:1, :] += column_sum(grad_normed * standard)
    vectors[1:2, :] += column_sum(grad_normed)

    @pl.when(step == steps - 1)
    def _():
        doubling.step(-1)
        for at in range(max(stages, work.ticks)):
            if at < stages:
                doubling.step(at)
            if len(schedule) + at < work.ticks:
                tick(halving, len(schedule) + at)
        vector_sum_ref[...] = doubling.buffers[-1][...]
        doubling.settle()
        settle(halving)


def first_back(tokens, dx1, given, vectors, weights, grads, work, schedule, collective_id):
    rows, width = tokens.shape
    steps = rows // TILE
    tile = pl.BlockSpec((TILE, width), lambda i: (i, 0))
    f32 = jnp.float32
    results = pl.pallas_call(
        functools.partial(first_back_kernel, work, schedule, steps),
        grid=(steps,),
        in_specs=[tile] * 2
        + [whole_block(given.shape), whole_block(vectors.shape)]
        + [whole_block(w.shape) for w in weights]
        + [tile] * 3
        + work.in_specs,
        out_specs=[tile, whole_block(vectors.shape)] + work.out_specs,
        out_shape=[
            jax.ShapeDtypeStruct(tokens.shape, f32),
            jax.ShapeDtypeStruct(vectors.shape, f32),
        ]
        + work.out_shape,
        scratch_shapes=doubling_scratch(vectors.shape) + work.scratch,
        compiler_params=params(collective_id=collective_id, has_side_effects=True),
        name="self_norm_back",
    )(tokens, dx1, given, vectors, *weights, *grads, *work.arrays)
    return results[:2], work.results(results[2:])


def hand_over_kernel(groups, *refs):
    ins, outs = refs[: sum(groups)], refs[sum(groups) :]
    at = 0
    for count, out in zip(groups, outs):
        width = out.shape[1] // count
        for part in range(count):
            out[:, width * part : width * (part + 1)] = ins[at + part][...]
        at += count


def hand_over(groups):
    arrays = [a for group in groups for a in group]
    return pl.pallas_call(
        functools.partial(hand_over_kernel, [len(group) for group in groups]),
        in_specs=[pl.BlockSpec(memory_space=pltpu.VMEM)] * len(arrays),
        out_specs=[pl.BlockSpec(memory_space=pltpu.VMEM)] * len(groups),
        out_shape=[
            jax.ShapeDtypeStruct((g[0].shape[0], sum(a.shape[1] for a in g)), g[0].dtype) for g in groups
        ],
        compiler_params=params(),
        name="hand_over",
    )(*arrays)


def cube_dims(axes=AXES):
    return [(axis, k) for axis in axes for k in reversed(range(axis_bits(axis)))]


def bits_of(dims):
    return [(lax.axis_index(axis) >> bit) & 1 for axis, bit in dims]


def partner(axis, bit):
    return {axis: lax.axis_index(axis) ^ (1 << bit)}


def halving_orders():
    x, y, near, far = ("narrow", 0), ("narrow", 1), ("wide", 1), ("wide", 2)
    core = ("wide", 0)
    six = (
        (far, x, y, near),
        (near, y, x, far),
        (y, far, x, near),
        (x, near, y, far),
        (x, y, far, near),
        (y, x, near, far),
    )
    rest = [d for d in cube_dims() if d not in (core, x, y, near, far)]
    return [[core, *order, *rest] for order in six]


def greet_partners():
    dims = cube_dims()
    barrier = pltpu.get_barrier_semaphore()
    for axis, bit in dims:
        pl.semaphore_signal(
            barrier, inc=1, device_id=partner(axis, bit), device_id_type=pl.DeviceIdType.MESH
        )
    pl.semaphore_wait(barrier, len(dims))


def runs_of(rows, step=16):
    step = step if rows % step == 0 else rows
    return [(start, step) for start in range(0, rows, step)]


def columns_of(columns, parts=6):
    if columns <= 1024:
        return [(0, columns)]
    cuts = [columns * k // parts // 128 * 128 for k in range(parts)] + [columns]
    return [(a, b - a) for a, b in zip(cuts[:-1], cuts[1:])]


def cut_up(groups):
    pieces = []
    for which, ((rows, columns), orders, rounds) in enumerate(groups):
        for start, size in runs_of(rows):
            for first, width in columns_of(columns):
                k = len(pieces)
                box = (which, slice(start, start + size), slice(first, first + width))
                pieces.append((box, orders[k % len(orders)], k // 6 % rounds))
    return pieces


def tick(mover, at, pieces=None):
    for piece in range(len(mover.pieces)) if pieces is None else pieces:
        _, order, late = mover.pieces[piece]
        stage = at - late
        if 0 <= stage < len(order):
            mover.finish(piece, stage)
        if -1 <= stage < len(order) - 1:
            mover.start(piece, stage + 1)


def settle(mover):
    for piece, (_, order, _) in enumerate(mover.pieces):
        for stage in range(len(order)):
            mover.send(piece, stage).wait_send()


def ticks_of(pieces):
    return max(len(order) + late for _, order, late in pieces)


def places_of(pieces):
    ends = [sum(len(p[1]) for p in pieces[:k]) for k in range(len(pieces) + 1)]
    return ends[:-1], ends[-1]


class Gathering:
    def __init__(self, pieces, dims, sources, outs, scratch):
        self.pieces, self.dims, self.sources, self.outs = pieces, dims, sources, outs
        self.send_sems, self.recv_sems, self.own_sems = scratch
        self.base, _ = places_of(pieces)
        self.ready = set()

    def own(self, piece):
        (which, *box), _, _ = self.pieces[piece]
        there = self.outs[which].at[(*bits_of(self.dims[which]), *box)]
        return pltpu.make_async_copy(self.sources[which].at[tuple(box)], there, self.own_sems.at[piece])

    def send(self, piece, stage):
        (which, *box), order, _ = self.pieces[piece]
        held = order[:stage]
        dims = self.dims[which]
        at = [slice(None) if d in held else b for d, b in zip(dims, bits_of(dims))]
        there = self.outs[which].at[(*at, *box)]
        sem = self.base[piece] + stage
        return pltpu.make_async_remote_copy(
            src_ref=there if stage else self.sources[which].at[tuple(box)],
            dst_ref=there,
            send_sem=self.send_sems.at[sem],
            recv_sem=self.recv_sems.at[sem],
            device_id=partner(*order[stage]),
            device_id_type=pl.DeviceIdType.MESH,
        )

    def start(self, piece, stage):
        if stage == 0:
            self.own(piece).start()
        if stage == 1:
            self.own(piece).wait()
        self.send(piece, stage).start()

    def finish(self, piece, stage):
        self.send(piece, stage).wait_recv()


class Gather:
    def __init__(self, groups):
        self.arrays = [array for array, _, _ in groups]
        self.pieces = cut_up([(array.shape, orders, rounds) for array, orders, rounds in groups])
        self.dims = [[d for d in cube_dims() if d in orders[0]] for _, orders, _ in groups]
        self.ticks = ticks_of(self.pieces)
        _, copies = places_of(self.pieces)
        self.in_specs = [pl.BlockSpec(memory_space=pl.ANY)] * len(groups)
        self.out_specs = self.in_specs
        self.out_shape = [
            jax.ShapeDtypeStruct((2,) * len(d) + a.shape, a.dtype)
            for a, d in zip(self.arrays, self.dims)
        ]
        self.scratch = [pltpu.SemaphoreType.DMA((copies,))] * 2
        self.scratch += [pltpu.SemaphoreType.DMA((len(self.pieces),))]

    def bind(self, sources, outs, scratch):
        return Gathering(self.pieces, self.dims, sources, outs, scratch)

    def results(self, outs):
        return [out.reshape(-1, a.shape[-1]) for out, a in zip(outs, self.arrays)]


class Halving:
    def __init__(self, pieces, firsts, sources, outs, scratch, near=False):
        count = len(pieces)
        self.firsts = firsts
        self.pieces, self.sources, self.outs, self.near = pieces, sources, outs, near
        self.kept, rest = ([], scratch) if near else (scratch[:count], scratch[count:])
        self.base, _ = places_of(pieces)
        self.landed = []
        for _, order, _ in pieces:
            self.landed.append(rest[: len(order)])
            rest = rest[len(order) :]
        self.send_sems, self.recv_sems = rest[:2]
        self.kept_sems = None if near else rest[2]

    def half(self, piece, stage, other):
        (which, rows, columns), order, _ = self.pieces[piece]
        left = [d for d in cube_dims() if d in order[stage:]]
        bit = bits_of([order[stage]])[0]
        at = [(1 - bit if other else bit) if d == order[stage] else slice(None) for d in left]
        if stage == 0:
            first = self.firsts[which]
            at += [slice(first + rows.start, first + rows.stop), columns]
        return tuple(at)

    def before(self, piece, stage):
        return self.sources[self.pieces[piece][0][0]] if stage == 0 else self.landed[piece][stage - 1]

    def send(self, piece, stage):
        sem = self.base[piece] + stage
        return pltpu.make_async_remote_copy(
            src_ref=self.before(piece, stage).at[self.half(piece, stage, True)],
            dst_ref=self.landed[piece][stage],
            send_sem=self.send_sems.at[sem],
            recv_sem=self.recv_sems.at[sem],
            device_id=partner(*self.pieces[piece][1][stage]),
            device_id_type=pl.DeviceIdType.MESH,
        )

    def keep(self, piece):
        source = self.before(piece, 0).at[self.half(piece, 0, False)]
        return pltpu.make_async_copy(source, self.kept[piece], self.kept_sems.at[piece])

    def start(self, piece, stage):
        self.send(piece, stage).start()
        if stage == 0 and not self.near:
            self.keep(piece).start()

    def finish(self, piece, stage):
        (which, rows, columns), order, _ = self.pieces[piece]
        self.send(piece, stage).wait_recv()
        if stage == 0 and not self.near:
            self.keep(piece).wait()
        landed = self.landed[piece][stage]
        depth = len(order) - 1 - stage
        if stage == 0 and not self.near:
            other, chosen = self.kept[piece], (slice(None),) * depth
        else:
            other, chosen = self.before(piece, stage), self.half(piece, stage, False)
        if depth == 0:
            total = landed[...].astype(jnp.float32) + other[chosen].astype(jnp.float32)
            self.outs[which][rows, columns] = total
            return

        def add(block, carry):
            at = [(block >> k) & 1 for k in reversed(range(depth))]
            rest = iter(at)
            there = [next(rest, c) if isinstance(c, slice) else c for c in chosen]
            landed[tuple(at)] = landed[tuple(at)] + other[tuple(there)]
            return carry

        lax.fori_loop(0, 1 << depth, add, 0, unroll=min(4, 1 << depth))


class Scatter:
    def __init__(self, groups, near=False):
        self.near = near
        self.arrays, self.firsts, shapes, cuts = [], [], [], []
        for array, orders, rounds, *span in groups:
            columns = array.shape[-1]
            block = (array.size // columns >> len(orders[0]), columns)
            self.arrays.append(array if near else array.reshape((2,) * len(orders[0]) + block))
            first, last = span or (0, block[0])
            self.firsts.append(first)
            shapes.append((last - first, columns))
            cuts.append(((last - first, columns), orders, rounds))
        self.pieces = cut_up(cuts)
        self.ticks = ticks_of(self.pieces)
        like = [
            ((rows.stop - rows.start, columns.stop - columns.start), self.arrays[which].dtype, len(order))
            for (which, rows, columns), order, _ in self.pieces
        ]
        kept = [pltpu.VMEM((2,) * (n - 1) + s, d) for s, d, n in like]
        landed = [pltpu.VMEM((2,) * (n - 1 - k) + s, d) for s, d, n in like for k in range(n)]
        _, copies = places_of(self.pieces)
        self.in_specs = [] if near else [pl.BlockSpec(memory_space=pl.ANY)] * len(groups)
        self.out_specs = [whole_block(s) for s in shapes]
        self.out_shape = [jax.ShapeDtypeStruct(s, jnp.float32) for s in shapes]
        self.scratch = ([] if near else kept) + landed + [pltpu.SemaphoreType.DMA((copies,))] * 2
        if not near:
            self.scratch += [pltpu.SemaphoreType.DMA((len(self.pieces),))]

    def bind(self, sources, outs, scratch):
        return Halving(self.pieces, self.firsts, sources, outs, scratch, self.near)

    def results(self, outs):
        return list(outs)


def beside(kernel, work, counts, schedule, steps):
    n_in, n_out, n_scratch = counts

    def run(*refs):
        cuts = [0, n_in, len(work.in_specs), n_out, len(work.out_specs), n_scratch]
        at = [sum(cuts[: k + 1]) for k in range(len(cuts))]
        ins, sources, outs, sums, own = (refs[a:b] for a, b in zip(at[:-1], at[1:]))
        moving = work.bind(sources, sums, refs[at[-1] :])
        step = pl.program_id(0)

        def hook(place):
            for when in sorted({when for when, where in schedule if where == place}):

                @pl.when(step == when)
                def _(when=when):
                    for at, slot in enumerate(schedule):
                        if slot == (when, place):
                            tick(moving, at)

        @pl.when(step == 0)
        def _():
            greet_partners()
            tick(moving, -1)

        hook(0)
        kernel(*ins, *outs, *own, hook=hook)

        @pl.when(step == steps - 1)
        def _():
            for at in range(len(schedule), work.ticks):
                tick(moving, at)
            settle(moving)

    return run


def alone_kernel(work, *refs):
    n, m = len(work.in_specs), len(work.out_specs)
    moving = work.bind(refs[:n], refs[n : n + m], refs[n + m :])
    greet_partners()
    for at in range(-1, work.ticks):
        tick(moving, at)
    settle(moving)


def alone(work, collective_id):
    outs = pl.pallas_call(
        functools.partial(alone_kernel, work),
        in_specs=work.in_specs,
        out_specs=work.out_specs,
        out_shape=work.out_shape,
        scratch_shapes=work.scratch,
        compiler_params=params(collective_id=collective_id, has_side_effects=True),
        name="gather_weights",
    )(*work.arrays)
    return work.results(outs)


class Doubling:
    def __init__(self, source, landed, send_sems, recv_sems):
        self.buffers = [source, *landed]
        self.send_sems, self.recv_sems = send_sems, recv_sems

    def swap(self, stage):
        return pltpu.make_async_remote_copy(
            src_ref=self.buffers[stage],
            dst_ref=self.buffers[stage + 1],
            send_sem=self.send_sems.at[stage],
            recv_sem=self.recv_sems.at[stage],
            device_id=partner(*cube_dims()[stage]),
            device_id_type=pl.DeviceIdType.MESH,
        )

    def step(self, stage):
        if stage >= 0:
            self.swap(stage).wait_recv()
            self.buffers[stage + 1][...] += self.buffers[stage][...]
        if stage + 2 < len(self.buffers):
            self.swap(stage + 1).start()

    def settle(self):
        for stage in range(len(self.buffers) - 1):
            self.swap(stage).wait_send()


def doubling_scratch(shape):
    stages = len(cube_dims())
    return [pltpu.VMEM(shape, jnp.float32)] * (stages + 1) + [pltpu.SemaphoreType.DMA((stages,))] * 2


def on_device(
    image_tokens, text_states, text_segments, image_segment, out_grad,
    norm1_gain, norm1_bias, self_query, self_key, self_value, self_output,
    norm2_gain, norm2_bias, cross_query, cross_key, cross_value, cross_output,
    norm3_gain, norm3_bias, mlp_in, mlp_in_bias, mlp_out, mlp_out_bias,
):
    tokens = image_tokens[0]
    rows, width = tokens.shape
    hidden = mlp_in.shape[1]
    vectors = (
        norm1_gain, norm1_bias, norm2_gain, norm2_bias,
        norm3_gain, norm3_bias, mlp_in_bias, mlp_out_bias,
    )
    sizes = [v.shape[0] for v in vectors]
    shard = self_query.shape[0]
    owners = width // shard
    parts = hidden // width
    orders = halving_orders()
    spread = [order[::-1] for order in orders]
    w_query, w_key, w_value, shared, text_full = alone(
        Gather(
            [(w, spread, 1) for w in (self_query, self_key, self_value, pack_vectors(vectors))]
            + [(text_states[0], [cube_dims(("narrow",))], 1)]
        ),
        1,
    )
    shared = shared.reshape(owners, -1, 128)
    given = shared[:, :, :shard].transpose(1, 0, 2).reshape(-1, width)
    up_bias = shared[:, 6, : sizes[6]].reshape(1, -1)
    mask = (text_segments[0] == image_segment[0, 0]).astype(jnp.int32)
    mask = jnp.concatenate([mask, mask]).reshape(-1, 1)

    (normed_one, queries, keys, values, mixed_self, sums_self), (down, *weights_two) = attend(
        tokens, given, (w_query, w_key, w_value),
        Gather(
            [
                (w, spread, 2)
                for w in (mlp_out, self_output, cross_query, cross_key, cross_value, cross_output)
            ]
        ),
        ((1, 0), (2, 0), (3, 0), (5, 0)), 2,
    )
    (x1, h2, q2, a2, x2, h3, k2, v2), ups = middle(
        tokens, mixed_self, text_full, mask, given, weights_two,
        Gather([(mlp_in, spread, 1)]), ((0, 1), (1, 1), (2, 1)), 3,
    )
    (
        block_out, dx2, grad_up_bias, grad_gain_three, grad_bias_three, grad_down_bias,
        grad_down, grad_up, near_sums,
    ) = mlp(x2, h3, out_grad[0], given, ups[0], up_bias, down, 2, (0, 1, 3, 5, 6, 7), orders[4:], 4)
    w_output, c_query, c_key, c_value, c_output = weights_two
    (
        dx1, grad_mixed, grad_self_out, grad_cross_query, grad_cross_out, grad_k2, grad_v2,
        grad_gain_two, grad_bias_two,
    ), (grad_down,) = middle_back(
        dx2, x1, mixed_self, h2, q2, a2, k2, v2, mask, given, (w_output, c_query, c_output),
        Scatter([(grad_down, orders, 1)]), ((0, 1), (2, 1), (3, 1)), 5,
    )
    (
        grad_queries, grad_keys, grad_values, *late, text_term,
    ), (*far_sums, grad_self_out, grad_cross_query, grad_cross_out) = attend_back(
        queries, keys, values, grad_mixed, sums_self, normed_one,
        (grad_k2, grad_v2, text_full, c_key, c_value),
        Scatter(
            [(g, orders, 1) for g in (*grad_up, grad_self_out, grad_cross_query, grad_cross_out)]
        ),
        ((1, 0), (4, 0), (6, 0), (7, 0)), 6,
    )
    self_terms = (grad_queries, grad_keys, grad_values)
    others = jnp.concatenate(
        [
            jnp.zeros((2, width), jnp.float32),
            grad_gain_two, grad_bias_two, grad_gain_three, grad_bias_three, grad_down_bias,
            grad_up_bias.reshape(-1, width),
        ],
        axis=0,
    )
    others = jnp.pad(others, ((0, -others.shape[0] % 8), (0, 0)))
    (image_grad, vector_sums), (
        grad_self_query, grad_self_key, grad_self_value, grad_cross_key, grad_cross_value, text_grad,
    ) = first_back(
        tokens, dx1, given, others, (w_query, w_key, w_value), self_terms,
        Scatter(
            [(g, orders, 1) for g in late] + [(text_term, [cube_dims(("narrow",))], 1)]
        ),
        (1,), 7,
    )
    (
        grad_self_query, grad_self_key, grad_self_value, grad_self_out,
        grad_cross_query, grad_cross_key, grad_cross_value, grad_cross_out,
        grad_up, grad_down, text_grad,
    ) = hand_over(
        [
            (g,)
            for g in (
                grad_self_query, grad_self_key, grad_self_value, grad_self_out,
                grad_cross_query, grad_cross_key, grad_cross_value, grad_cross_out,
            )
        ]
        + [(*near_sums, *far_sums), (grad_down,), (text_grad,)]
    )
    place = lax.axis_index(AXES)
    flat = vector_sums.reshape(-1)
    rows_of = (0, 1, 2, 3, 4, 5, 7, 6)
    vector_grads = [
        lax.dynamic_slice_in_dim(flat, row * width + place * size, size)
        for row, size in zip(rows_of, sizes)
    ]
    return (
        block_out[None], image_grad[None], text_grad[None],
        vector_grads[0], vector_grads[1],
        grad_self_query, grad_self_key, grad_self_value, grad_self_out,
        vector_grads[2], vector_grads[3],
        grad_cross_query, grad_cross_key, grad_cross_value, grad_cross_out,
        vector_grads[4], vector_grads[5],
        grad_up, vector_grads[6], grad_down, vector_grads[7],
    )


def solution(mesh):
    placed = (
        P(("wide", "narrow"), None, None),
        P("wide", "narrow", None),
        P("wide", None),
        P("wide", "narrow"),
        P(("wide", "narrow"), None, None),
        P(("wide", "narrow")),
        P(("wide", "narrow")),
        P(("wide", "narrow"), None),
        P(("wide", "narrow"), None),
        P(("wide", "narrow"), None),
        P(("wide", "narrow"), None),
        P(("wide", "narrow")),
        P(("wide", "narrow")),
        P(("wide", "narrow"), None),
        P(("wide", "narrow"), None),
        P(("wide", "narrow"), None),
        P(("wide", "narrow"), None),
        P(("wide", "narrow")),
        P(("wide", "narrow")),
        P(("wide", "narrow"), None),
        P(("wide", "narrow")),
        P(("wide", "narrow"), None),
        P(("wide", "narrow")),
    )
    return jax.shard_map(
        on_device,
        mesh=mesh,
        in_specs=placed,
        out_specs=(
            P(("wide", "narrow"), None, None),
            P(("wide", "narrow"), None, None),
            P("wide", "narrow", None),
            P(("wide", "narrow")),
            P(("wide", "narrow")),
            P(("wide", "narrow"), None),
            P(("wide", "narrow"), None),
            P(("wide", "narrow"), None),
            P(("wide", "narrow"), None),
            P(("wide", "narrow")),
            P(("wide", "narrow")),
            P(("wide", "narrow"), None),
            P(("wide", "narrow"), None),
            P(("wide", "narrow"), None),
            P(("wide", "narrow"), None),
            P(("wide", "narrow")),
            P(("wide", "narrow")),
            P(("wide", "narrow"), None),
            P(("wide", "narrow")),
            P(("wide", "narrow"), None),
            P(("wide", "narrow")),
        ),
        check_vma=False,
    )
```

time: 558 us -> 488 us (0.87)
  Pallas kernels: 504 us -> 466 us
  local copies, waits for them, and re-layouts: 29.6 us -> 11.5 us
  other arithmetic: 12.3 us -> 2.07 us
    pallas_call x5 -> x6, Pallas kernels: 411 us -> 362 us  [the longest x1 92.1 us: attend(): pl.pallas_call(beside(attend_kernel, work, (5, 6, 0), schedule, pairs), g...]
    pallas_call x1, Pallas kernels: 45.9 us -> 63.6 us  [first_back(): pl.pallas_call(functools.partial(first_back_kernel, work, schedule, steps...]
    concatenate x7 -> x0, other arithmetic: 10.8 us -> none  [the longest x4 6.55 us: results(): return [jnp.concatenate(found[k], axis=0) for k in sorted(found)]]
    unnamed x67 -> x24, local copies, waits for them, and re-layouts: 13.9 us -> 5.94 us
    pallas_call x1, Pallas kernels: 47.1 us -> 40.8 us  [alone(): pl.pallas_call(functools.partial(alone_kernel, work), in_specs=work.in_sp...]
    concatenate x3 -> x0, local copies, waits for them, and re-layouts: 6.28 us -> none  [the longest x1 5.43 us: pack_vectors(): flat = jnp.concatenate(vectors)]
where the time goes in v4:
time: 488 us; the launch traced here: 482 us
  Pallas kernels  466 us (95%)
  local copies, waits for them, and re-layouts  11.5 us (2%)
    pallas_call x1, Pallas kernels, attend(): pl.pallas_call(beside(attend_kernel, work, (5, 6, 0), schedule, pairs), g...  92.1 us
    pallas_call x1, Pallas kernels, mlp(): pl.pallas_call(functools.partial(mlp_kernel, near, far, pace, work), grid...  79.2 us
    pallas_call x1, Pallas kernels, attend_back(): pl.pallas_call(beside(attend_back_kernel, work, (11, 9, 3), schedule, ste...  70.5 us
    pallas_call x1, Pallas kernels, first_back(): pl.pallas_call(functools.partial(first_back_kernel, work, schedule, steps...  63.6 us
    pallas_call x1, Pallas kernels, middle_back(): pl.pallas_call(beside(middle_back_kernel, work, (13, 9, 9), schedule, row...  59.5 us
    pallas_call x1, Pallas kernels, middle(): pl.pallas_call(beside(middle_kernel, work, (10, 8, 2), schedule, rows //...  57.6 us
    pallas_call x1, Pallas kernels, alone(): pl.pallas_call(functools.partial(alone_kernel, work), in_specs=work.in_sp...  40.8 us

profile of v4, /device:TPU:0, one launch (start us, length us, event | category | flops | bytes accessed | tf_op | source)
XLA Modules:
  0.0 481.7 jit_solution(16994365986787070689)
XLA Ops:
  0.7 1.4 add_bitcast_fusion.refs_3_
  2.0 40.8 %gather_weights.1 = (bf16[2,2,2,2,2,32,1024]{6,5,4,3,2,1,0:T(8,128)(2,1)}, bf16[2,2,2,2,2,32,1024]{6,5,4,3,2,1,0:T(8,128)(2,1)}, bf16[2,2,2,2,2,32,1024]{6,5,4,3...) custom-call(bf16[32,1024]{1,0:T(8,128)(2,1)} %refs_0_.1, bf16[32,1024]{1,0:T(8,128)(2,1)} %refs_1_.1, ...), custom_call_target="tpu_custom_call" | custom-call | tf_op jit(solution)/shard_map/gather_weights/pallas_call | solution.py:965
  42.8 0.9 copy.54
  43.8 0.7 reshape.133.refs_1_.refs_4_.vectors_ref.refs_9_.given_ref
  44.5 0.0 copy-start.9
  44.5 92.1 %self_attend.1 = (bf16[1024,1024]{1,0:T(8,128)(2,1)}, bf16[1024,1024]{1,0:T(8,128)(2,1)}, bf16[1024,1024]{1,0:T(8,128)(2,1)}, bf16[1024,1024]{1,0:T(8,128)(2,1)}...) custom-call(bf16[1024,1024]{1,0:T(8,128)(2,1)} %bitcast.47, ...), custom_call_target="tpu_custom_call" | custom-call | tf_op jit(solution)/shard_map/self_attend/pallas_call | solution.py:128
  137.2 0.0 copy-done.9
  137.2 0.8 copy.47.refs_3_.refs_8_
  138.0 57.6 %output_and_cross.1 = (f32[1024,1024]{1,0:T(8,128)}, bf16[1024,1024]{1,0:T(8,128)(2,1)}, bf16[1024,1024]{1,0:T(8,128)(2,1)}, bf16[1024,1024]{1,0:T(8,128)(2,1)},...) custom-call(bf16[1024,1024]{1,0:T(8,128)(2,1)} %bitcast.48, ...), custom_call_target="tpu_custom_call" | custom-call | tf_op jit(solution)/shard_map/output_and_cross/pallas_call | solution.py:446
  195.7 1.5 slice_bitcast_fusion.ub_ref
  197.2 79.2 %mlp_both_ways.1 = (bf16[1024,1024]{1,0:T(8,128)(2,1)}, f32[1024,1024]{1,0:T(8,128)}, f32[1,4096]{1,0:T(1,128)}, f32[1,1024]{1,0:T(1,128)}, f32[1,1024]{1,0:T(1,...) custom-call(f32[1024,1024]{1,0:T(8,128)} %get-tuple-element.112.x_re, ...), custom_call_target="tpu_custom_call" | custom-call | tf_op jit(solution)/shard_map/mlp_both_ways/pallas_call | solution.py:350
  276.4 59.5 %cross_back.1 = (f32[1024,1024]{1,0:T(8,128)}, bf16[1024,1024]{1,0:T(8,128)(2,1)}, bf16[1024,1024]{1,0:T(8,128)(2,1)}, bf16[1024,1024]{1,0:T(8,128)(2,1)}, bf16[...) custom-call(f32[1024,1024]{1,0:T(8,128)} %get-tuple-element.117.refs, ...), custom_call_target="tpu_custom_call" | custom-call | tf_op jit(solution)/shard_map/cross_back/pallas_call | solution.py:537
  335.9 0.0 copy-start.3
  335.9 0.0 copy-start.4
  335.9 0.0 copy-start.5
  335.9 0.0 copy-start.6
  335.9 0.0 copy-start.7
  335.9 0.0 copy-start.8
  335.9 70.5 %self_attend_back.1 = (bf16[1024,1024]{1,0:T(8,128)(2,1)}, bf16[1024,1024]{1,0:T(8,128)(2,1)}, bf16[1024,1024]{1,0:T(8,128)(2,1)}, bf16[1024,1024]{1,0:T(8,128)(...) custom-call(bf16[1024,1024]{1,0:T(8,128)(2,1)} %get-tuple-element.13, ...), custom_call_target="tpu_custom_call" | custom-call | tf_op jit(solution)/shard_map/self_attend_back/pallas_call | solution.py:208
  406.4 0.5 broadcast.23
  407.0 0.0 copy-done.3
  407.0 0.7 reduce.3
  407.7 0.0 copy-done.4
  407.7 0.0 copy-done.5
  407.7 0.0 copy-done.6
  407.7 0.0 copy-done.7
  407.7 0.0 copy-done.8
  407.7 0.2 concatenate.8
  407.9 0.6 pad.76.vectors_ref
  408.5 63.6 %self_norm_back.1 = (f32[1024,1024]{1,0:T(8,128)}, f32[16,1024]{1,0:T(8,128)}, f32[32,1024]{1,0:T(8,128)}, f32[32,1024]{1,0:T(8,128)}, f32[32,1024]{1,0:T(8,128)...) custom-call(bf16[1024,1024]{1,0:T(8,128)(2,1)} %bitcast.49, ...), custom_call_target="tpu_custom_call" | custom-call | tf_op jit(solution)/shard_map/self_norm_back/pallas_call | solution.py:619
  472.1 0.0 copy-start.2
  472.1 0.0 copy-start.1
  472.1 3.1 hand_over.1
  475.3 0.0 copy-done.2
  475.3 0.6 fusion
  475.9 0.6 dynamic_slice.30
  476.5 0.0 copy-done.1
  476.5 0.0 copy-start
  476.5 1.3 copy.58
  477.8 1.6 copy-done
  479.5 2.0 copy.59
  (5 shorter events, 0.0 us)
Async XLA Ops:
  44.5 92.7 %copy-start.9 = (s32[1,128]{1,0:T(1,128)S(1)}, s32[1,128]{1,0:T(1,128)}, u32[]{:S(2)}) copy-start(s32[1,128]{1,0:T(1,128)} %param.25) | copy-start | bytes 1540
  335.9 71.1 %copy-start.3 = (f32[1,4096]{1,0:T(1,128)S(1)}, f32[1,4096]{1,0:T(1,128)}, u32[]{:S(2)}) copy-start(f32[1,4096]{1,0:T(1,128)} %get-tuple-element.131) | copy-start | bytes 49156
  335.9 71.8 %copy-start.4 = (f32[1,1024]{1,0:T(1,128)S(1)}, f32[1,1024]{1,0:T(1,128)}, u32[]{:S(2)}) copy-start(f32[1,1024]{1,0:T(1,128)} %get-tuple-element.128) | copy-start | bytes 12292
  335.9 71.8 %copy-start.5 = (f32[1,1024]{1,0:T(1,128)S(1)}, f32[1,1024]{1,0:T(1,128)}, u32[]{:S(2)}) copy-start(f32[1,1024]{1,0:T(1,128)} %get-tuple-element.129) | copy-start | bytes 12292
  335.9 71.8 %copy-start.6 = (f32[1,1024]{1,0:T(1,128)S(1)}, f32[1,1024]{1,0:T(1,128)}, u32[]{:S(2)}) copy-start(f32[1,1024]{1,0:T(1,128)} %get-tuple-element.130) | copy-start | bytes 12292
  335.9 71.8 %copy-start.7 = (f32[1,1024]{1,0:T(1,128)S(1)}, f32[1,1024]{1,0:T(1,128)}, u32[]{:S(2)}) copy-start(f32[1,1024]{1,0:T(1,128)} %get-tuple-element.126) | copy-start | bytes 12292
  335.9 71.8 %copy-start.8 = (f32[1,1024]{1,0:T(1,128)S(1)}, f32[1,1024]{1,0:T(1,128)}, u32[]{:S(2)}) copy-start(f32[1,1024]{1,0:T(1,128)} %get-tuple-element.127) | copy-start | bytes 12292
  472.1 3.2 copy-start.2
  472.1 4.4 copy-start.1
  476.5 2.9 copy-start

commit v5 on v4

--- a/solution.py
+++ b/solution.py
@@ -13,6 +13,8 @@
 BF16 = jnp.bfloat16
 VMEM_LIMIT = 60 * 1024 * 1024
 MLP_STEPS = 8
+MLP_TILE = 512
+VECTOR_ROWS = 16
 
 EPSILON = 1e-05
 NEGATIVE = -1e30
@@ -236,36 +238,43 @@
 
 
 def mlp_kernel(
-    near, far, pace, work, x_ref, h_ref, g_ref, vectors_ref, up_ref, ub_ref, down_ref,
-    out_ref, dx_ref, dub_ref, dgain_ref, dbias_ref, gsum_ref, ddown_ref, *refs,
+    near, far, paces, coming, work, x_ref, h_ref, g_ref, vectors_ref, ub_ref, down_ref, *refs
 ):
-    far_refs, refs = refs[:far], refs[far:]
+    parts = near + far
+    late = len(coming.arrays)
+    per = MLP_STEPS // parts
+    early_refs, refs = refs[: parts - late], refs[parts - late :]
+    shard_refs, refs = refs[:late], refs[late:]
+    dx_ref, dub_ref, dgain_ref, dbias_ref, gsum_ref, ddown_ref, act = refs[:7]
+    far_refs, refs = refs[7 : 7 + far], refs[7 + far :]
     sums, refs = refs[:near], refs[near:]
-    out_sum, dh_sum, h_flip, act, grad_act = refs[:5]
-    near_refs, refs = refs[5 : 5 + near], refs[5 + near :]
+    dh_sum, h_flip, up, grad_act = refs[:4]
+    near_refs, refs = refs[4 : 4 + near], refs[4 + near :]
+    late_refs, refs = refs[:late], refs[late:]
     step, steps = pl.program_id(0), pl.num_programs(0)
     rows = h_ref.shape[0]
-    parts = near + far
-    per = MLP_STEPS // parts
-    moving = work.bind(near_refs, sums, refs) if near else None
+    chunk = up.shape[1]
+    moving = work.bind(near_refs, sums, refs[: len(work.scratch)])
+    arriving = coming.bind(shard_refs, late_refs, refs[len(work.scratch) :])
 
     @pl.when(step == 0)
     def _():
-        if near:
-            greet_partners()
+        greet_partners()
+        tick(arriving, -1)
         h_flip[...] = h_ref[...].T
-        out_sum[...] = x_ref[...] + vectors_ref[7:8, :]
         dh_sum[...] = jnp.zeros_like(dh_sum)
 
     left, due = [], {}
+    for at in range(coming.ticks):
+        due.setdefault(paces[0][at], []).append((arriving, at, None))
     for part in range(near):
         pieces = [k for k, p in enumerate(work.pieces) if p[0][0] == part]
         for at in range(-1, work.ticks):
-            place = 2 * per * (part + 1) + pace[at + 1]
+            place = 2 * per * (part + 1) + paces[1][at + 1]
             if place < 2 * MLP_STEPS:
-                due.setdefault(place, []).append((at, pieces))
+                due.setdefault(place, []).append((moving, at, pieces))
             else:
-                left.append((at, pieces))
+                left.append((moving, at, pieces))
 
     def move(half):
         for place in due:
@@ -273,26 +282,34 @@
 
                 @pl.when(step == place // 2)
                 def _(place=place):
-                    for at, pieces in due[place]:
-                        tick(moving, at, pieces)
+                    for mover, at, pieces in due[place]:
+                        tick(mover, at, pieces)
 
     move(0)
-    up = up_ref[...]
+    for place in range(MLP_STEPS):
+
+        @pl.when(step == place)
+        def _(place=place):
+            part, first = place // per, chunk * (place % per)
+            if part < parts - late:
+                up[...] = early_refs[part][...]
+            else:
+                ref = late_refs[part - parts + late]
+                up[...] = ref[..., first : first + chunk].reshape(up.shape)
+
     down = down_ref[...]
     bias_sum = jnp.zeros_like(dub_ref)
-    for start in range(0, rows, TILE):
-        at = slice(start, start + TILE)
-        hidden, slope = gelu_both(nn(h_ref[at, :], up) + ub_ref[...])
+    for start in range(0, rows, MLP_TILE):
+        at = slice(start, start + MLP_TILE)
+        hidden, slope = gelu_both(nn(h_ref[at, :], up[...]) + ub_ref[...])
         act[at, :] = hidden.astype(BF16)
         grad_pre = (nt(g_ref[at, :], down) * slope).astype(BF16)
         grad_act[at, :] = grad_pre
         bias_sum += column_sum(grad_pre.astype(jnp.float32))
-        out_sum[at, :] += nn(act[at, :], down)
-        dh_sum[at, :] += nt(grad_pre, up)
+        dh_sum[at, :] += nt(grad_pre, up[...])
     dub_ref[...] = bias_sum
     move(1)
     grad_up = nn(h_flip[...], grad_act[...]).astype(BF16)
-    chunk = grad_up.shape[1]
     for part, ref in enumerate(far_refs):
 
         @pl.when(step // per == near + part)
@@ -316,7 +333,6 @@
         tail_sum = jnp.zeros_like(gsum_ref)
         for start in range(0, rows, TILE):
             at = slice(start, start + TILE)
-            out_ref[at, :] = out_sum[at, :].astype(BF16)
             standard, rate = standardize(x_ref[at, :])
             grad = dh_sum[at, :]
             tail = g_ref[at, :].astype(jnp.float32)
@@ -327,13 +343,13 @@
         dgain_ref[...] = gain_sum
         dbias_ref[...] = grad_sum
         gsum_ref[...] = tail_sum
-        for at, pieces in left:
-            tick(moving, at, pieces)
-        if near:
-            settle(moving)
-
-
-def mlp(x, h, g, vectors, up, up_bias, down, near, pace, orders, collective_id):
+        for mover, at, pieces in left:
+            tick(mover, at, pieces)
+        settle(moving)
+        settle(arriving)
+
+
+def mlp(x, h, g, vectors, early, coming, up_bias, down, near, paces, orders, collective_id):
     rows, width = x.shape
     hidden = up_bias.shape[1]
     chunk = hidden // MLP_STEPS
@@ -344,48 +360,69 @@
     lead = (2,) * len(cube_dims())
     block = lead + (width >> len(lead), width)
     source = jax.ShapeDtypeStruct(block, BF16)
-    work = Scatter([(source, orders, 1)] * near, near=True) if near else None
+    work = Scatter([(source, orders, (1, 16))] * near, near=True)
     far = parts - near
-    pace = [*pace, *range(pace[-1] + 1, pace[-1] + 1 + len(cube_dims()))]
+    more = range(1, 1 + len(cube_dims()))
+    paces = [[*pace, *(pace[-1] + k for k in more)] for pace in paces]
+
+    def part_of(k):
+        return pl.BlockSpec((width, chunk), lambda c: (0, jnp.clip(c - per * k, 0, per - 1)))
+
     results = pl.pallas_call(
-        functools.partial(mlp_kernel, near, far, pace, work),
+        functools.partial(mlp_kernel, near, far, paces, coming, work),
         grid=(MLP_STEPS,),
         in_specs=[
             whole_block(x.shape), whole_block(h.shape), whole_block(g.shape), whole_block(vectors.shape),
-            pl.BlockSpec((width, chunk), lambda c: (0, c)),
             pl.BlockSpec((1, chunk), lambda c: (0, c)),
             pl.BlockSpec((chunk, width), lambda c: (c, 0)),
-        ],
+        ]
+        + [part_of(k) for k in range(len(early))]
+        + coming.in_specs,
         out_specs=[
-            whole_block(x.shape), whole_block(x.shape),
+            whole_block(x.shape),
             pl.BlockSpec((1, chunk), lambda c: (0, c)),
             whole_block(row), whole_block(row), whole_block(row),
             pl.BlockSpec((chunk, width), lambda c: (c, 0)),
+            pl.BlockSpec((rows, chunk), lambda c: (0, c)),
         ]
-        + [
-            pl.BlockSpec((width, chunk), lambda c, k=k: (0, jnp.clip(c - per * k, 0, per - 1)))
-            for k in range(near, parts)
-        ]
-        + (work.out_specs if near else []),
+        + [part_of(k) for k in range(near, parts)]
+        + work.out_specs,
         out_shape=[
-            jax.ShapeDtypeStruct(x.shape, BF16), jax.ShapeDtypeStruct(x.shape, f32),
+            jax.ShapeDtypeStruct(x.shape, f32),
             jax.ShapeDtypeStruct((1, hidden), f32),
             jax.ShapeDtypeStruct(row, f32), jax.ShapeDtypeStruct(row, f32), jax.ShapeDtypeStruct(row, f32),
             jax.ShapeDtypeStruct((hidden, width), BF16),
+            jax.ShapeDtypeStruct((rows, hidden), BF16),
         ]
         + [jax.ShapeDtypeStruct((width, width), BF16)] * far
-        + (work.out_shape if near else []),
+        + work.out_shape,
         scratch_shapes=[
-            pltpu.VMEM(x.shape, f32), pltpu.VMEM(x.shape, f32), pltpu.VMEM((width, rows), BF16),
-            pltpu.VMEM((rows, chunk), BF16), pltpu.VMEM((rows, chunk), BF16),
+            pltpu.VMEM(x.shape, f32), pltpu.VMEM((width, rows), BF16),
+            pltpu.VMEM((width, chunk), BF16), pltpu.VMEM((rows, chunk), BF16),
         ]
         + [pltpu.VMEM(block, BF16)] * near
-        + (work.scratch if near else []),
-        compiler_params=params(collective_id=collective_id, has_side_effects=True) if near else params(),
+        + [pltpu.VMEM(b, BF16) for b in coming.blocks]
+        + work.scratch
+        + coming.scratch,
+        compiler_params=params(collective_id=collective_id, has_side_effects=True),
         name="mlp_both_ways",
-    )(x, h, g, vectors, up, up_bias, down)
-    sums = work.results(results[7 + far :]) if near else []
-    return *results[:7], results[7 : 7 + far], sums
+    )(x, h, g, vectors, up_bias, down, *early, *coming.arrays)
+    return *results[:7], results[7 : 7 + far], work.results(results[7 + far :])
+
+
+def load_all(sources, buffers, sems):
+    copies = [
+        pltpu.make_async_copy(source, buffer, sems.at[k])
+        for k, (source, buffer) in enumerate(zip(sources, buffers))
+    ]
+    for copy in copies:
+        copy.start()
+    for copy in copies:
+        copy.wait()
+
+
+def room_for(arrays):
+    return [pltpu.VMEM(a.shape, a.dtype) for a in arrays] + [pltpu.SemaphoreType.DMA((len(arrays),))]
 
 
 def stack_heads(pair):
@@ -404,12 +441,18 @@
 
 def middle_kernel(
     x_ref, a_ref, text_ref, mask_ref, vectors_ref,
-    wo_ref, cq_ref, ck_ref, cv_ref, co_ref,
+    wo_hbm, cq_hbm, ck_hbm, cv_hbm, co_hbm,
     x1_ref, h2_ref, q2_ref, a2_ref, x2_ref, h3_ref, k2_ref, v2_ref, keys, values_flip,
+    wo_ref, cq_ref, ck_ref, cv_ref, co_ref, weight_sems,
     hook,
 ):
     @pl.when(pl.program_id(0) == 0)
     def _():
+        load_all(
+            (wo_hbm, cq_hbm, ck_hbm, cv_hbm, co_hbm),
+            (wo_ref, cq_ref, ck_ref, cv_ref, co_ref),
+            weight_sems,
+        )
         k2_ref[...] = nn(text_ref[...], ck_ref[...]).astype(BF16)
         v2_ref[...] = nn(text_ref[...], cv_ref[...]).astype(BF16)
         for pair in range(keys.shape[0]):
@@ -444,11 +487,11 @@
     f32 = jnp.float32
     like = lambda dtype: jax.ShapeDtypeStruct(tokens.shape, dtype)
     results = pl.pallas_call(
-        beside(middle_kernel, work, (10, 8, 2), schedule, rows // TILE),
+        beside(middle_kernel, work, (10, 8, 8), schedule, rows // TILE),
         grid=(rows // TILE,),
         in_specs=[
             tile, tile, whole_block(text.shape), whole_block(mask.shape),
-            whole_block(vectors.shape), *[whole_block(w.shape) for w in weights], *work.in_specs,
+            whole_block(vectors.shape), *[pl.BlockSpec(memory_space=pl.ANY)] * 5, *work.in_specs,
         ],
         out_specs=[tile] * 6 + [whole_block(text.shape)] * 2 + work.out_specs,
         out_shape=[like(f32), like(BF16), like(BF16), like(BF16), like(f32), like(BF16)]
@@ -458,6 +501,7 @@
             pltpu.VMEM((width // 128, 2 * slots, 128), BF16),
             pltpu.VMEM((width // 128, 128, 2 * slots), BF16),
         ]
+        + room_for(weights)
         + work.scratch,
         compiler_params=params(collective_id=collective_id, has_side_effects=True),
         name="output_and_cross",
@@ -566,13 +610,14 @@
 
 
 def first_back_kernel(
-    work, schedule, steps, x_ref, dx1_ref, given_ref, vectors_ref, wq_ref, wk_ref, wv_ref, dq_ref, dk_ref, dv_ref,
-    *refs,
+    work, schedule, steps, x_ref, dx1_ref, given_ref, gain2_ref, bias2_ref, gain3_ref, bias3_ref, db_ref, ub_ref,
+    wq_ref, wk_ref, wv_ref, dq_ref, dk_ref, dv_ref,
+    x2_ref, act_ref, down_ref, *refs,
 ):
     n, m = len(work.in_specs), len(work.out_specs)
-    sources, (dx_ref, vector_sum_ref), sums = refs[:n], refs[n : n + 2], refs[n + 2 : n + 2 + m]
+    sources, (dx_ref, out_ref, vector_sum_ref) = refs[:n], refs[n : n + 3]
+    sums, rest = refs[n + 3 : n + 3 + m], refs[n + 3 + m :]
     stages = len(cube_dims())
-    rest = refs[n + 2 + m :]
     doubling = Doubling(rest[0], rest[1 : stages + 1], *rest[stages + 1 : stages + 3])
     halving = work.bind(sources, sums, rest[stages + 3 :])
     step = pl.program_id(0)
@@ -582,7 +627,12 @@
     def _():
         greet_partners()
         tick(halving, -1)
-        vectors[...] = vectors_ref[...]
+        vectors[...] = jnp.zeros_like(vectors)
+        for row, ref in enumerate((gain2_ref, bias2_ref, gain3_ref, bias3_ref, db_ref)):
+            vectors[row + 2 : row + 3, :] = ref[...]
+        width = vectors.shape[1]
+        for part in range(ub_ref.shape[1] // width):
+            vectors[part + 7 : part + 8, :] = ub_ref[:, width * part : width * (part + 1)]
 
     for at, place in enumerate(schedule):
 
@@ -595,6 +645,8 @@
     )
     standard, rate = standardize(x_ref[...].astype(jnp.float32))
     dx_ref[...] = dx1_ref[...] + norm_back(standard, rate, given_ref[0:1, :], grad_normed)
+    out = x2_ref[...] + nn(act_ref[...], down_ref[...]) + given_ref[7:8, :]
+    out_ref[...] = out.astype(BF16)
     vectors[0:1, :] += column_sum(grad_normed * standard)
     vectors[1:2, :] += column_sum(grad_normed)
 
@@ -611,7 +663,9 @@
         settle(halving)
 
 
-def first_back(tokens, dx1, given, vectors, weights, grads, work, schedule, collective_id):
+def first_back(
+    tokens, dx1, given, vectors, weights, grads, x2, act, down, work, schedule, collective_id
+):
     rows, width = tokens.shape
     steps = rows // TILE
     tile = pl.BlockSpec((TILE, width), lambda i: (i, 0))
@@ -620,21 +674,23 @@
         functools.partial(first_back_kernel, work, schedule, steps),
         grid=(steps,),
         in_specs=[tile] * 2
-        + [whole_block(given.shape), whole_block(vectors.shape)]
+        + [whole_block(v.shape) for v in (given, *vectors)]
         + [whole_block(w.shape) for w in weights]
-        + [tile] * 3
+        + [tile] * 4
+        + [pl.BlockSpec((TILE, act.shape[1]), lambda i: (i, 0)), whole_block(down.shape)]
         + work.in_specs,
-        out_specs=[tile, whole_block(vectors.shape)] + work.out_specs,
+        out_specs=[tile, tile, whole_block((VECTOR_ROWS, width))] + work.out_specs,
         out_shape=[
             jax.ShapeDtypeStruct(tokens.shape, f32),
-            jax.ShapeDtypeStruct(vectors.shape, f32),
+            jax.ShapeDtypeStruct(tokens.shape, BF16),
+            jax.ShapeDtypeStruct((VECTOR_ROWS, width), f32),
         ]
         + work.out_shape,
-        scratch_shapes=doubling_scratch(vectors.shape) + work.scratch,
+        scratch_shapes=doubling_scratch((VECTOR_ROWS, width)) + work.scratch,
         compiler_params=params(collective_id=collective_id, has_side_effects=True),
         name="self_norm_back",
-    )(tokens, dx1, given, vectors, *weights, *grads, *work.arrays)
-    return results[:2], work.results(results[2:])
+    )(tokens, dx1, given, *vectors, *weights, *grads, x2, act, down, *work.arrays)
+    return results[:3], work.results(results[3:])
 
 
 def hand_over_kernel(groups, *refs):
@@ -698,7 +754,7 @@
     pl.semaphore_wait(barrier, len(dims))
 
 
-def runs_of(rows, step=16):
+def runs_of(rows, step):
     step = step if rows % step == 0 else rows
     return [(start, step) for start in range(0, rows, step)]
 
@@ -712,8 +768,8 @@
 
 def cut_up(groups):
     pieces = []
-    for which, ((rows, columns), orders, rounds) in enumerate(groups):
-        for start, size in runs_of(rows):
+    for which, ((rows, columns), orders, (rounds, step)) in enumerate(groups):
+        for start, size in runs_of(rows, step):
             for first, width in columns_of(columns):
                 k = len(pieces)
                 box = (which, slice(start, start + size), slice(first, first + width))
@@ -747,16 +803,22 @@
 
 
 class Gathering:
-    def __init__(self, pieces, dims, sources, outs, scratch):
-        self.pieces, self.dims, self.sources, self.outs = pieces, dims, sources, outs
+    def __init__(self, pieces, dims, firsts, sources, outs, scratch):
+        self.pieces, self.dims, self.firsts = pieces, dims, firsts
+        self.sources, self.outs = sources, outs
         self.send_sems, self.recv_sems, self.own_sems = scratch
         self.base, _ = places_of(pieces)
         self.ready = set()
 
+    def source(self, piece):
+        (which, rows, columns), _, _ = self.pieces[piece]
+        first = self.firsts[which]
+        return self.sources[which].at[rows, slice(first + columns.start, first + columns.stop)]
+
     def own(self, piece):
         (which, *box), _, _ = self.pieces[piece]
         there = self.outs[which].at[(*bits_of(self.dims[which]), *box)]
-        return pltpu.make_async_copy(self.sources[which].at[tuple(box)], there, self.own_sems.at[piece])
+        return pltpu.make_async_copy(self.source(piece), there, self.own_sems.at[piece])
 
     def send(self, piece, stage):
         (which, *box), order, _ = self.pieces[piece]
@@ -766,7 +828,7 @@
         there = self.outs[which].at[(*at, *box)]
         sem = self.base[piece] + stage
         return pltpu.make_async_remote_copy(
-            src_ref=there if stage else self.sources[which].at[tuple(box)],
+            src_ref=there if stage else self.source(piece),
             dst_ref=there,
             send_sem=self.send_sems.at[sem],
             recv_sem=self.recv_sems.at[sem],
@@ -787,25 +849,31 @@
 
 class Gather:
     def __init__(self, groups):
-        self.arrays = [array for array, _, _ in groups]
-        self.pieces = cut_up([(array.shape, orders, rounds) for array, orders, rounds in groups])
-        self.dims = [[d for d in cube_dims() if d in orders[0]] for _, orders, _ in groups]
+        self.arrays, self.firsts, self.shapes, cuts = [], [], [], []
+        for array, orders, rounds, *span in groups:
+            first, last = span or (0, array.shape[1])
+            self.arrays.append(array)
+            self.firsts.append(first)
+            self.shapes.append((array.shape[0], last - first))
+            cuts.append((self.shapes[-1], orders, rounds))
+        self.pieces = cut_up(cuts)
+        self.dims = [[d for d in cube_dims() if d in group[1][0]] for group in groups]
         self.ticks = ticks_of(self.pieces)
         _, copies = places_of(self.pieces)
         self.in_specs = [pl.BlockSpec(memory_space=pl.ANY)] * len(groups)
         self.out_specs = self.in_specs
+        self.blocks = [(2,) * len(d) + s for d, s in zip(self.dims, self.shapes)]
         self.out_shape = [
-            jax.ShapeDtypeStruct((2,) * len(d) + a.shape, a.dtype)
-            for a, d in zip(self.arrays, self.dims)
+            jax.ShapeDtypeStruct(b, a.dtype) for b, a in zip(self.blocks, self.arrays)
         ]
         self.scratch = [pltpu.SemaphoreType.DMA((copies,))] * 2
         self.scratch += [pltpu.SemaphoreType.DMA((len(self.pieces),))]
 
     def bind(self, sources, outs, scratch):
-        return Gathering(self.pieces, self.dims, sources, outs, scratch)
+        return Gathering(self.pieces, self.dims, self.firsts, sources, outs, scratch)
 
     def results(self, outs):
-        return [out.reshape(-1, a.shape[-1]) for out, a in zip(outs, self.arrays)]
+        return [out.reshape(-1, s[1]) for out, s in zip(outs, self.shapes)]
 
 
 class Halving:
@@ -1027,8 +1095,8 @@
     spread = [order[::-1] for order in orders]
     w_query, w_key, w_value, shared, text_full = alone(
         Gather(
-            [(w, spread, 1) for w in (self_query, self_key, self_value, pack_vectors(vectors))]
-            + [(text_states[0], [cube_dims(("narrow",))], 1)]
+            [(w, spread, (1, 16)) for w in (self_query, self_key, self_value, pack_vectors(vectors))]
+            + [(text_states[0], [cube_dims(("narrow",))], (1, 32))]
         ),
         1,
     )
@@ -1038,31 +1106,42 @@
     mask = (text_segments[0] == image_segment[0, 0]).astype(jnp.int32)
     mask = jnp.concatenate([mask, mask]).reshape(-1, 1)
 
-    (normed_one, queries, keys, values, mixed_self, sums_self), (down, *weights_two) = attend(
+    late = parts // 2
+
+    def part(k):
+        return (mlp_in, spread, (2, 16), width * k, width * (k + 1))
+
+    (normed_one, queries, keys, values, mixed_self, sums_self), (*weights_two, up_first) = attend(
         tokens, given, (w_query, w_key, w_value),
         Gather(
             [
-                (w, spread, 2)
-                for w in (mlp_out, self_output, cross_query, cross_key, cross_value, cross_output)
+                (w, spread, (2, 16))
+                for w in (self_output, cross_query, cross_key, cross_value, cross_output)
             ]
+            + [(mlp_in, spread, (2, 16), 0, width)]
         ),
         ((1, 0), (2, 0), (3, 0), (5, 0)), 2,
     )
-    (x1, h2, q2, a2, x2, h3, k2, v2), ups = middle(
+    (x1, h2, q2, a2, x2, h3, k2, v2), (down, *up_more) = middle(
         tokens, mixed_self, text_full, mask, given, weights_two,
-        Gather([(mlp_in, spread, 1)]), ((0, 1), (1, 1), (2, 1)), 3,
+        Gather([(mlp_out, spread, (2, 16))] + [part(k) for k in range(1, parts - late)]),
+        ((0, 1), (1, 1), (2, 0), (3, 0)), 3,
     )
     (
-        block_out, dx2, grad_up_bias, grad_gain_three, grad_bias_three, grad_down_bias,
-        grad_down, grad_up, near_sums,
-    ) = mlp(x2, h3, out_grad[0], given, ups[0], up_bias, down, 2, (0, 1, 3, 5, 6, 7), orders[4:], 4)
+        dx2, grad_up_bias, grad_gain_three, grad_bias_three, grad_down_bias,
+        grad_down, hidden_act, grad_up, near_sums,
+    ) = mlp(
+        x2, h3, out_grad[0], given, [up_first, *up_more],
+        Gather([(mlp_in, spread, (1, 16), width * k, width * (k + 1)) for k in range(parts - late, parts)]),
+        up_bias, down, 2, ((2, 3, 5, 7, 8), (0, 1, 3, 5, 6, 7)), orders[4:], 4,
+    )
     w_output, c_query, c_key, c_value, c_output = weights_two
     (
         dx1, grad_mixed, grad_self_out, grad_cross_query, grad_cross_out, grad_k2, grad_v2,
         grad_gain_two, grad_bias_two,
     ), (grad_down,) = middle_back(
         dx2, x1, mixed_self, h2, q2, a2, k2, v2, mask, given, (w_output, c_query, c_output),
-        Scatter([(grad_down, orders, 1)]), ((0, 1), (2, 1), (3, 1)), 5,
+        Scatter([(grad_down, orders, (1, 16))]), ((0, 1), (2, 1), (3, 1)), 5,
     )
     (
         grad_queries, grad_keys, grad_values, *late, text_term,
@@ -1070,26 +1149,20 @@
         queries, keys, values, grad_mixed, sums_self, normed_one,
         (grad_k2, grad_v2, text_full, c_key, c_value),
         Scatter(
-            [(g, orders, 1) for g in (*grad_up, grad_self_out, grad_cross_query, grad_cross_out)]
+            [(g, orders, (1, 32)) for g in (*grad_up, grad_self_out, grad_cross_query, grad_cross_out)]
         ),
         ((1, 0), (4, 0), (6, 0), (7, 0)), 6,
     )
     self_terms = (grad_queries, grad_keys, grad_values)
-    others = jnp.concatenate(
-        [
-            jnp.zeros((2, width), jnp.float32),
-            grad_gain_two, grad_bias_two, grad_gain_three, grad_bias_three, grad_down_bias,
-            grad_up_bias.reshape(-1, width),
-        ],
-        axis=0,
-    )
-    others = jnp.pad(others, ((0, -others.shape[0] % 8), (0, 0)))
-    (image_grad, vector_sums), (
+    others = (
+        grad_gain_two, grad_bias_two, grad_gain_three, grad_bias_three, grad_down_bias, grad_up_bias,
+    )
+    (image_grad, block_out, vector_sums), (
         grad_self_query, grad_self_key, grad_self_value, grad_cross_key, grad_cross_value, text_grad,
     ) = first_back(
-        tokens, dx1, given, others, (w_query, w_key, w_value), self_terms,
+        tokens, dx1, given, others, (w_query, w_key, w_value), self_terms, x2, hidden_act, down,
         Scatter(
-            [(g, orders, 1) for g in late] + [(text_term, [cube_dims(("narrow",))], 1)]
+            [(g, orders, (1, 16)) for g in late] + [(text_term, [cube_dims(("narrow",))], (1, 32))]
         ),
         (1,), 7,
     )

time: 488 us -> 484 us (level)
  Pallas kernels: 466 us -> 461 us
    pallas_call x1, Pallas kernels: 92.1 us -> 72.2 us  [attend(): pl.pallas_call(beside(attend_kernel, work, (5, 6, 0), schedule, pairs), g...]
    pallas_call x2, Pallas kernels: 137 us -> 147 us  [the longest x1 82.3 us: mlp(): pl.pallas_call(functools.partial(mlp_kernel, near, far, paces, coming, wo...]
where the time goes in v5:
time: 484 us; the launch traced here: 474 us
  Pallas kernels  461 us (95%)
  local copies, waits for them, and re-layouts  10.2 us (2%)
    pallas_call x1, Pallas kernels, mlp(): pl.pallas_call(functools.partial(mlp_kernel, near, far, paces, coming, wo...  82.3 us
    pallas_call x1, Pallas kernels, attend(): pl.pallas_call(beside(attend_kernel, work, (5, 6, 0), schedule, pairs), g...  72.2 us
    pallas_call x1, Pallas kernels, attend_back(): pl.pallas_call(beside(attend_back_kernel, work, (11, 9, 3), schedule, ste...  70.9 us
    pallas_call x1, Pallas kernels, first_back(): pl.pallas_call(functools.partial(first_back_kernel, work, schedule, steps...  67.9 us
    pallas_call x1, Pallas kernels, middle(): pl.pallas_call(beside(middle_kernel, work, (10, 8, 8), schedule, rows //...  64.7 us
    pallas_call x1, Pallas kernels, middle_back(): pl.pallas_call(beside(middle_back_kernel, work, (13, 9, 9), schedule, row...  58.7 us
    pallas_call x1, Pallas kernels, alone(): pl.pallas_call(functools.partial(alone_kernel, work), in_specs=work.in_sp...  41.1 us

profile of v5, /device:TPU:0, one launch (start us, length us, event | category | flops | bytes accessed | tf_op | source)
XLA Modules:
  0.0 474.1 jit_solution(16090062888389667700)
XLA Ops:
  0.7 1.4 add_bitcast_fusion.refs_3_
  2.0 41.1 %gather_weights.1 = (bf16[2,2,2,2,2,32,1024]{6,5,4,3,2,1,0:T(8,128)(2,1)}, bf16[2,2,2,2,2,32,1024]{6,5,4,3,2,1,0:T(8,128)(2,1)}, bf16[2,2,2,2,2,32,1024]{6,5,4,3...) custom-call(bf16[32,1024]{1,0:T(8,128)(2,1)} %refs_0_.1, bf16[32,1024]{1,0:T(8,128)(2,1)} %refs_1_.1, ...), custom_call_target="tpu_custom_call" | custom-call | tf_op jit(solution)/shard_map/gather_weights/pallas_call | solution.py:1033
  43.2 0.9 copy.54
  44.1 0.7 reshape.133.refs_1_.refs_4_.vectors_ref.refs_9_.given_ref
  44.8 0.0 copy-start.3
  44.8 72.2 %self_attend.1 = (bf16[1024,1024]{1,0:T(8,128)(2,1)}, bf16[1024,1024]{1,0:T(8,128)(2,1)}, bf16[1024,1024]{1,0:T(8,128)(2,1)}, bf16[1024,1024]{1,0:T(8,128)(2,1)}...) custom-call(bf16[1024,1024]{1,0:T(8,128)(2,1)} %bitcast.50, ...), custom_call_target="tpu_custom_call" | custom-call | tf_op jit(solution)/shard_map/self_attend/pallas_call | solution.py:130
  117.6 0.0 copy-done.3
  117.7 0.8 copy.47.refs_3_.refs_8_
  118.5 64.7 %output_and_cross.1 = (f32[1024,1024]{1,0:T(8,128)}, bf16[1024,1024]{1,0:T(8,128)(2,1)}, bf16[1024,1024]{1,0:T(8,128)(2,1)}, bf16[1024,1024]{1,0:T(8,128)(2,1)},...) custom-call(bf16[1024,1024]{1,0:T(8,128)(2,1)} %bitcast.51, ...), custom_call_target="tpu_custom_call" | custom-call | tf_op jit(solution)/shard_map/output_and_cross/pallas_call | solution.py:489
  183.2 1.5 slice_bitcast_fusion.ub_ref
  184.7 82.3 %mlp_both_ways.1 = (f32[1024,1024]{1,0:T(8,128)}, f32[1,4096]{1,0:T(1,128)}, f32[1,1024]{1,0:T(1,128)}, f32[1,1024]{1,0:T(1,128)}, f32[1,1024]{1,0:T(1,128)}, /*...) custom-call(f32[1024,1024]{1,0:T(8,128)} %get-tuple-element.114.x_re, ...), custom_call_target="tpu_custom_call" | custom-call | tf_op jit(solution)/shard_map/mlp_both_ways/pallas_call | solution.py:371
  267.0 58.7 %cross_back.1 = (f32[1024,1024]{1,0:T(8,128)}, bf16[1024,1024]{1,0:T(8,128)(2,1)}, bf16[1024,1024]{1,0:T(8,128)(2,1)}, bf16[1024,1024]{1,0:T(8,128)(2,1)}, bf16[...) custom-call(f32[1024,1024]{1,0:T(8,128)} %get-tuple-element.119.refs, ...), custom_call_target="tpu_custom_call" | custom-call | tf_op jit(solution)/shard_map/cross_back/pallas_call | solution.py:581
  325.7 70.9 %self_attend_back.1 = (bf16[1024,1024]{1,0:T(8,128)(2,1)}, bf16[1024,1024]{1,0:T(8,128)(2,1)}, bf16[1024,1024]{1,0:T(8,128)(2,1)}, bf16[1024,1024]{1,0:T(8,128)(...) custom-call(bf16[1024,1024]{1,0:T(8,128)(2,1)} %get-tuple-element.13, ...), custom_call_target="tpu_custom_call" | custom-call | tf_op jit(solution)/shard_map/self_attend_back/pallas_call | solution.py:210
  396.6 67.9 %self_norm_back.1 = (f32[1024,1024]{1,0:T(8,128)}, bf16[1024,1024]{1,0:T(8,128)(2,1)}, f32[16,1024]{1,0:T(8,128)}, f32[32,1024]{1,0:T(8,128)}, f32[32,1024]{1,0:...) custom-call(bf16[1024,1024]{1,0:T(8,128)(2,1)} %bitcast.52, ...), custom_call_target="tpu_custom_call" | custom-call | tf_op jit(solution)/shard_map/self_norm_back/pallas_call | solution.py:673
  464.5 0.0 copy-start.2
  464.5 0.0 copy-start.1
  464.5 3.1 hand_over.1
  467.7 0.0 copy-done.2
  467.7 0.6 fusion
  468.3 0.6 dynamic_slice.30
  468.9 0.0 copy-done.1
  468.9 0.0 copy-start
  468.9 1.3 copy.58
  470.2 1.6 copy-done
  471.9 2.0 copy.59
  (3 shorter events, 0.0 us)
Async XLA Ops:
  44.8 72.8 %copy-start.3 = (s32[1,128]{1,0:T(1,128)S(1)}, s32[1,128]{1,0:T(1,128)}, u32[]{:S(2)}) copy-start(s32[1,128]{1,0:T(1,128)} %param.25) | copy-start | bytes 1540
  464.5 3.2 copy-start.2
  464.5 4.4 copy-start.1
  468.9 2.9 copy-start

commit v6 on v5

--- a/solution.py
+++ b/solution.py
@@ -13,7 +13,7 @@
 BF16 = jnp.bfloat16
 VMEM_LIMIT = 60 * 1024 * 1024
 MLP_STEPS = 8
-MLP_TILE = 512
+MLP_TILE = 1024
 VECTOR_ROWS = 16
 
 EPSILON = 1e-05

time: 484 us -> 481 us (level)
  no operation moved by 1% of the time
where the time goes in v6:
time: 481 us; the launch traced here: 472 us
  Pallas kernels  459 us (95%)
  local copies, waits for them, and re-layouts  10.2 us (2%)
    pallas_call x1, Pallas kernels, mlp(): pl.pallas_call(functools.partial(mlp_kernel, near, far, paces, coming, wo...  80.4 us
    pallas_call x1, Pallas kernels, attend(): pl.pallas_call(beside(attend_kernel, work, (5, 6, 0), schedule, pairs), g...  72.2 us
    pallas_call x1, Pallas kernels, attend_back(): pl.pallas_call(beside(attend_back_kernel, work, (11, 9, 3), schedule, ste...  70.3 us
    pallas_call x1, Pallas kernels, first_back(): pl.pallas_call(functools.partial(first_back_kernel, work, schedule, steps...  68.3 us
    pallas_call x1, Pallas kernels, middle(): pl.pallas_call(beside(middle_kernel, work, (10, 8, 8), schedule, rows //...  64.7 us
    pallas_call x1, Pallas kernels, middle_back(): pl.pallas_call(beside(middle_back_kernel, work, (13, 9, 9), schedule, row...  58.7 us
    pallas_call x1, Pallas kernels, alone(): pl.pallas_call(functools.partial(alone_kernel, work), in_specs=work.in_sp...  41.1 us

profile of v6, /device:TPU:0, one launch (start us, length us, event | category | flops | bytes accessed | tf_op | source)
XLA Modules:
  0.0 472.2 jit_solution(12728518961445569477)
XLA Ops:
  0.7 1.4 add_bitcast_fusion.refs_3_
  2.0 41.1 %gather_weights.1 = (bf16[2,2,2,2,2,32,1024]{6,5,4,3,2,1,0:T(8,128)(2,1)}, bf16[2,2,2,2,2,32,1024]{6,5,4,3,2,1,0:T(8,128)(2,1)}, bf16[2,2,2,2,2,32,1024]{6,5,4,3...) custom-call(bf16[32,1024]{1,0:T(8,128)(2,1)} %refs_0_.1, bf16[32,1024]{1,0:T(8,128)(2,1)} %refs_1_.1, ...), custom_call_target="tpu_custom_call" | custom-call | tf_op jit(solution)/shard_map/gather_weights/pallas_call | solution.py:1033
  43.2 0.9 copy.54
  44.1 0.7 reshape.133.refs_1_.refs_4_.vectors_ref.refs_9_.given_ref
  44.8 0.0 copy-start.3
  44.8 72.2 %self_attend.1 = (bf16[1024,1024]{1,0:T(8,128)(2,1)}, bf16[1024,1024]{1,0:T(8,128)(2,1)}, bf16[1024,1024]{1,0:T(8,128)(2,1)}, bf16[1024,1024]{1,0:T(8,128)(2,1)}...) custom-call(bf16[1024,1024]{1,0:T(8,128)(2,1)} %bitcast.50, ...), custom_call_target="tpu_custom_call" | custom-call | tf_op jit(solution)/shard_map/self_attend/pallas_call | solution.py:130
  117.6 0.0 copy-done.3
  117.7 0.8 copy.47.refs_3_.refs_8_
  118.5 64.7 %output_and_cross.1 = (f32[1024,1024]{1,0:T(8,128)}, bf16[1024,1024]{1,0:T(8,128)(2,1)}, bf16[1024,1024]{1,0:T(8,128)(2,1)}, bf16[1024,1024]{1,0:T(8,128)(2,1)},...) custom-call(bf16[1024,1024]{1,0:T(8,128)(2,1)} %bitcast.51, ...), custom_call_target="tpu_custom_call" | custom-call | tf_op jit(solution)/shard_map/output_and_cross/pallas_call | solution.py:489
  183.2 1.5 slice_bitcast_fusion.ub_ref
  184.7 80.4 %mlp_both_ways.1 = (f32[1024,1024]{1,0:T(8,128)}, f32[1,4096]{1,0:T(1,128)}, f32[1,1024]{1,0:T(1,128)}, f32[1,1024]{1,0:T(1,128)}, f32[1,1024]{1,0:T(1,128)}, /*...) custom-call(f32[1024,1024]{1,0:T(8,128)} %get-tuple-element.114.x_re, ...), custom_call_target="tpu_custom_call" | custom-call | tf_op jit(solution)/shard_map/mlp_both_ways/pallas_call | solution.py:371
  265.1 58.7 %cross_back.1 = (f32[1024,1024]{1,0:T(8,128)}, bf16[1024,1024]{1,0:T(8,128)(2,1)}, bf16[1024,1024]{1,0:T(8,128)(2,1)}, bf16[1024,1024]{1,0:T(8,128)(2,1)}, bf16[...) custom-call(f32[1024,1024]{1,0:T(8,128)} %get-tuple-element.119.refs, ...), custom_call_target="tpu_custom_call" | custom-call | tf_op jit(solution)/shard_map/cross_back/pallas_call | solution.py:581
  323.9 70.3 %self_attend_back.1 = (bf16[1024,1024]{1,0:T(8,128)(2,1)}, bf16[1024,1024]{1,0:T(8,128)(2,1)}, bf16[1024,1024]{1,0:T(8,128)(2,1)}, bf16[1024,1024]{1,0:T(8,128)(...) custom-call(bf16[1024,1024]{1,0:T(8,128)(2,1)} %get-tuple-element.13, ...), custom_call_target="tpu_custom_call" | custom-call | tf_op jit(solution)/shard_map/self_attend_back/pallas_call | solution.py:210
  394.2 68.3 %self_norm_back.1 = (f32[1024,1024]{1,0:T(8,128)}, bf16[1024,1024]{1,0:T(8,128)(2,1)}, f32[16,1024]{1,0:T(8,128)}, f32[32,1024]{1,0:T(8,128)}, f32[32,1024]{1,0:...) custom-call(bf16[1024,1024]{1,0:T(8,128)(2,1)} %bitcast.52, ...), custom_call_target="tpu_custom_call" | custom-call | tf_op jit(solution)/shard_map/self_norm_back/pallas_call | solution.py:673
  462.6 0.0 copy-start.2
  462.6 0.0 copy-start.1
  462.6 3.1 hand_over.1
  465.7 0.0 copy-done.2
  465.8 0.6 fusion
  466.4 0.6 dynamic_slice.30
  467.0 0.0 copy-done.1
  467.0 0.0 copy-start
  467.0 1.3 copy.58
  468.3 1.6 copy-done
  469.9 2.0 copy.59
  (3 shorter events, 0.0 us)
Async XLA Ops:
  44.8 72.8 %copy-start.3 = (s32[1,128]{1,0:T(1,128)S(1)}, s32[1,128]{1,0:T(1,128)}, u32[]{:S(2)}) copy-start(s32[1,128]{1,0:T(1,128)} %param.25) | copy-start | bytes 1540
  462.6 3.2 copy-start.2
  462.6 4.4 copy-start.1
  467.0 2.9 copy-start
